TPU v7x, 32 devices: a whole 2x2x4 slice. The times are simulated.
32 devices in a mesh: rep: 4 (over x, core), dp: 8 (over z, y).
Axes of the slice: x: 2, y: 2, z: 4, core: 2. Of those that a mesh axis runs over, the one named last changes fastest.
Arguments:
- features: float32 [288, 15, 15, 512], P(('rep', 'dp')), may hold values from -6 to 6
- map_size: int32 [288], P(('rep', 'dp')), may hold values from 13 to 15, as said below
- item_count: int32 [32], P(('rep', 'dp')), may hold values from 2 to 9, as said below
- conv4_weight: float32 [2359296], P(('rep', 'dp')), may hold values from -0.09375 to 0.09375
- conv4_bias: float32 [512], replicated, may hold values from -3 to 3
- conv5_weight: float32 [2359296], P(('rep', 'dp')), may hold values from -0.09375 to 0.09375
- conv5_bias: float32 [512], replicated, may hold values from -3 to 3
- cotangent: float32 [288, 15, 15, 512], P(('rep', 'dp')), may hold values from -6 to 6
Outputs:
- conv5_out: float32 [288, 15, 15, 512], P(('rep', 'dp'))
- input_grad: float32 [288, 15, 15, 512], P(('rep', 'dp'))
- conv4_weight_grad: float32 [2359296], P(('rep', 'dp'))
- conv4_bias_grad: float32 [512], replicated
- conv5_weight_grad: float32 [2359296], P(('rep', 'dp'))
- conv5_bias_grad: float32 [512], replicated
Inputs may be any that keep to these rules, and one draw needn't show every extreme that they name: `map_size`: each item's map is 13 or 15 cells on a side, in the upper left corner of its slot; both sizes occur in every draw. `item_count`: the number of live items in each device's 9 slots, which come first; slots at or past it are empty; some device is full and some holds the fewest.
All inputs are finite; a program needn't handle non-finite values.
Results may differ from a plain program's by a relative error of at most 0.0003.
Values sent between devices are 32-bit elements; how exact they have to be, the bound alone decides.
No kernel may reach another device: no remote copies, remote signals or barrier semaphores. Data moves between devices by JAX's collectives and lax.ppermute only.
A program may use at most 384 MiB of HBM per device.

v0:
```python
import jax
import jax.numpy as jnp
from jax import lax
from jax.sharding import PartitionSpec as P


def smooth_act(values):
    return jax.nn.gelu(values, approximate=True)


def act_grad(pre_values, upstream):
    return jax.vjp(smooth_act, pre_values)[1](upstream)[0]


def pad_cells(source):
    return jnp.pad(source, ((0, 0), (1, 1), (1, 1), (0, 0)))


def tap_columns(source, flipped):
    map_side = source.shape[1]
    channels = source.shape[3]
    padded = pad_cells(source)
    windows = []
    for row_tap in range(3):
        for col_tap in range(3):
            if flipped:
                row_start, col_start = (2 - row_tap, 2 - col_tap)
            else:
                row_start, col_start = (row_tap, col_tap)
            windows.append(
                padded[:, row_start : row_start + map_side, col_start : col_start + map_side, :]
            )
    return jnp.concatenate(windows, axis=3).reshape(-1, 9 * channels)


def convolve(source, kernel, offset):
    channels = source.shape[3]
    columns = tap_columns(source, False)
    summed = jnp.dot(
        columns,
        kernel.reshape(9 * channels, channels),
        precision=lax.Precision.HIGHEST,
        preferred_element_type=jnp.float32,
    )
    return (summed + offset).reshape(source.shape)


def convolve_back(upstream, kernel):
    channels = upstream.shape[3]
    columns = tap_columns(upstream, True)
    flipped_kernel = jnp.transpose(kernel, (0, 2, 1)).reshape(9 * channels, channels)
    summed = jnp.dot(
        columns, flipped_kernel, precision=lax.Precision.HIGHEST, preferred_element_type=jnp.float32
    )
    return summed.reshape(upstream.shape)


def kernel_grad(source, upstream):
    channels = source.shape[3]
    columns = tap_columns(source, False)
    product = lax.dot_general(
        columns,
        upstream.reshape(-1, channels),
        (((0,), (0,)), ((), ())),
        precision=lax.Precision.HIGHEST,
        preferred_element_type=jnp.float32,
    )
    return product.reshape(-1)


def reduce_grad(flat_grad):
    return lax.psum_scatter(flat_grad, ("rep", "dp"), scatter_dimension=0, tiled=True)


def body(
    features, map_size, item_count, conv4_weight, conv4_bias, conv5_weight, conv5_bias, cotangent
):
    slot_count = features.shape[0]
    map_side = features.shape[1]
    channels = features.shape[3]
    slot_ids = jnp.arange(slot_count, dtype=jnp.int32)
    live = slot_ids < item_count[0]
    cells = jnp.arange(map_side, dtype=jnp.int32)
    inside = cells[None, :] < map_size[:, None]
    valid = live[:, None, None] & inside[:, :, None] & inside[:, None, :]
    valid_mask = valid.astype(jnp.float32)[..., None]

    def fetch_kernel(flat_shard):
        return lax.all_gather(flat_shard, ("rep", "dp"), axis=0, tiled=True).reshape(
            9, channels, channels
        )

    kernel4 = fetch_kernel(conv4_weight)
    masked = features * valid_mask
    pre4 = convolve(masked, kernel4, conv4_bias)
    hidden = smooth_act(pre4) * valid_mask
    kernel5 = fetch_kernel(conv5_weight)
    pre5 = convolve(hidden, kernel5, conv5_bias)
    conv5_out = smooth_act(pre5) * valid_mask
    total_cells = slot_count * lax.axis_size(("rep", "dp")) * map_side * map_side
    grad_scale = float(total_cells) ** (-0.5)
    back5 = act_grad(pre5, cotangent * valid_mask)
    share5 = reduce_grad(kernel_grad(hidden, back5))
    bias5_local = jnp.sum(back5, axis=(0, 1, 2))
    back_hidden = convolve_back(back5, kernel5)
    back4 = act_grad(pre4, back_hidden * valid_mask)
    share4 = reduce_grad(kernel_grad(masked, back4))
    bias4_local = jnp.sum(back4, axis=(0, 1, 2))
    input_grad = convolve_back(back4, kernel4) * valid_mask
    bias4_sum, bias5_sum = lax.psum((bias4_local, bias5_local), ("rep", "dp"))
    return (
        conv5_out,
        input_grad,
        share4 * grad_scale,
        bias4_sum * grad_scale,
        share5 * grad_scale,
        bias5_sum * grad_scale,
    )


def solution(mesh):
    placed = (
        P(("rep", "dp"), None, None, None),
        P(("rep", "dp")),
        P(("rep", "dp")),
        P(("rep", "dp")),
        P(),
        P(("rep", "dp")),
        P(),
        P(("rep", "dp"), None, None, None),
    )
    return jax.shard_map(
        body,
        mesh=mesh,
        in_specs=placed,
        out_specs=(
            P(("rep", "dp"), None, None, None),
            P(("rep", "dp"), None, None, None),
            P(("rep", "dp")),
            P(),
            P(("rep", "dp")),
            P(),
        ),
        check_vma=False,
    )
```

profile of v0, /device:TPU:0, one launch (start us, length us, event | category | flops | bytes accessed | tf_op | source)
XLA Modules:
  0.0 937.7 jit_solution(11556730032076615355)
XLA Ops:
  38.5 33.0 %reshape.116 = f32[2025,4608]{1,0:T(8,128)} reshape(f32[9,15,15,4608]{3,2,1,0:T(8,128)} %fusion.19) | data formatting | bytes 74649600 | tf_op jit(solution)/shard_map/reshape | solution.py:33
  71.5 24.2 %all-gather.3.cloned.1.call-done = f32[2359296]{0:T(1024)} async-done(((f32[73728]{0:T(1024)}), f32[2359296]{0:T(1024)}) %all-gather.3.cloned.1.call-update) | async-done | bytes 9437200 | tf_op jit(solution)/shard_map/all_gather | solution.py:89
  95.7 11.2 %reshape_reshape.6 = f32[4608,512]{1,0:T(8,128)} reshape(f32[2359296]{0:T(1024)} %all-gather.3.cloned.1.call-done) | data formatting | bytes 18874368 | tf_op jit(solution)/shard_map/reshape;reshape | solution.py:41
  106.9 64.5 %convolution_add_fusion.1 = f32[2025,512]{1,0:T(8,128)} fusion(f32[2025,4608]{1,0:T(8,128)} %reshape.116, f32[4608,512]{1,0:T(8,128)} %reshape_reshape.6, f32[512]{0:T(512)S(1)} %copy-done.6), kind=kOutput, calls=%fused_computation.85 | convolution fusion | flops 57331929088 | bytes 50911232 | tf_op jit(solution)/shard_map/dot_general | solution.py:39
  206.1 32.3 %reshape.118 = f32[2025,4608]{1,0:T(8,128)} reshape(f32[9,15,15,4608]{3,2,1,0:T(8,128)} %fusion.27) | data formatting | bytes 74649600 | tf_op jit(solution)/shard_map/reshape | solution.py:33
  238.3 11.2 %reshape_reshape.7 = f32[4608,512]{1,0:T(8,128)} reshape(f32[2359296]{0:T(1024)} %all-gather.5.cloned.1.call-done) | data formatting | bytes 18874368 | tf_op jit(solution)/shard_map/reshape;reshape | solution.py:41
  249.5 64.5 %convolution_add_fusion = f32[2025,512]{1,0:T(8,128)} fusion(f32[2025,4608]{1,0:T(8,128)} %reshape.118, f32[4608,512]{1,0:T(8,128)} %reshape_reshape.7, f32[512]{0:T(512)S(1)} %copy-done.7), kind=kOutput, calls=%fused_computation.84 | convolution fusion | flops 57331929088 | bytes 50911232 | tf_op jit(solution)/shard_map/dot_general | solution.py:39
  319.1 7.9 fusion.44
  327.0 74.0 %convolution_bitcast_fusion = f32[576,4,8,128]{3,2,1,0:T(8,128)} fusion(f32[9,15,15,4608]{3,2,1,0:T(8,128)} %fusion.27, f32[9,15,15,512]{3,2,1,0:T(8,128)S(1)} %get-tuple-element.11), kind=kOutput, calls=%fused_computation.82 | convolution fusion | flops 57330892800 | bytes 50909184 | tf_op jit(solution)/shard_map/dot_general | solution.py:61
  403.9 11.2 %reshape.120 = f32[9,512,512]{2,1,0:T(8,128)} reshape(f32[2359296]{0:T(1024)} %all-gather.5.cloned.1.call-done) | data formatting | bytes 18874368 | tf_op jit(solution)/shard_map/reshape | solution.py:89
  415.1 9.7 %copy.16 = f32[9,512,512]{2,1,0:T(8,128)} copy(f32[9,512,512]{1,2,0:T(8,128)} %bitcast.48) | data formatting | bytes 18874368 | tf_op jit(solution)/shard_map/transpose | solution.py:51
  424.8 9.7 %copy.23 = f32[576,4,8,128]{3,1,2,0:T(4,128)} copy(f32[576,4,8,128]{3,2,1,0:T(8,128)} %convolution_bitcast_fusion) | data formatting | bytes 18874368
  439.7 5.3 fusion.30
  462.4 77.8 %fusion.5 = f32[9,15,15,512]{3,2,1,0:T(8,128)S(1)} fusion(f32[9,15,15,512]{3,2,1,0:T(8,128)S(1)} %bitcast.45, f32[9,15,15,4608]{3,2,1,0:T(8,128)} %fusion.35, f32[4608,512,1,1]{1,0,3,2:T(8,128)} %bitcast.55, f32[9,15,15]{2,1,0:T(8,128)S(1)} %copy-done.3), kind=kOutput, calls=%fused_computation.41 | convolution fusion | flops 57351618560 | bytes 55064484 | tf_op jit(solution)/shard_map/dot_general | solution.py:52
  542.4 72.8 %convolution_bitcast_fusion.1 = f32[576,4,8,128]{3,2,1,0:T(8,128)} fusion(f32[9,15,15,4608]{3,2,1,0:T(8,128)} %fusion.19, f32[9,15,15,512]{3,2,1,0:T(8,128)S(1)} %fusion.5), kind=kOutput, calls=%fused_computation.83 | convolution fusion | flops 57330892800 | bytes 50909184 | tf_op jit(solution)/shard_map/dot_general | solution.py:61
  615.1 9.8 %copy.22 = f32[576,4,8,128]{3,1,2,0:T(4,128)} copy(f32[576,4,8,128]{3,2,1,0:T(8,128)} %convolution_bitcast_fusion.1) | data formatting | bytes 18874368
  624.9 11.3 %reshape.122 = f32[9,512,512]{2,1,0:T(8,128)} reshape(f32[2359296]{0:T(1024)} %all-gather.3.cloned.1.call-done) | data formatting | bytes 18874368 | tf_op jit(solution)/shard_map/reshape | solution.py:89
  636.2 9.7 %copy.17 = f32[9,512,512]{2,1,0:T(8,128)} copy(f32[9,512,512]{1,2,0:T(8,128)} %bitcast.49) | data formatting | bytes 18874368 | tf_op jit(solution)/shard_map/transpose | solution.py:51
  651.2 6.7 fusion.46
  657.9 40.4 %all-reduce.6 = (f32[512]{0:T(512)S(1)}, f32[512]{0:T(512)S(1)}) all-reduce(f32[512]{0:T(512)S(1)} %get-tuple-element.13, f32[512]{0:T(512)S(1)} %copy-done.5), channel_id=1, replica_groups=mesh['rep'=4,'dp'=8] {'rep','dp'}, use_global_device_ids=true, to_apply=%region_2.3 | all-reduce | flops 1024 | bytes 8192 | tf_op jit(solution)/shard_map/psum | solution.py:110
  698.3 5.4 fusion.38
  703.7 5.3 fusion.39
  724.9 69.1 %convolution_multiply_fusion = f32[9,15,15,512]{3,2,1,0:T(8,128)} fusion(f32[9,15,15,4608]{3,2,1,0:T(8,128)} %fusion.43, f32[4608,512,1,1]{1,0,3,2:T(8,128)S(1)} %bitcast.54, f32[9,15,15]{2,1,0:T(8,128)S(1)} %copy-done.4), kind=kOutput, calls=%fused_computation.86 | convolution fusion | flops 57331929088 | bytes 50917284 | tf_op jit(solution)/shard_map/dot_general | solution.py:52
  794.0 135.1 %all-reduce.10.cloned.1.call-done = (f32[2359296]{0:T(1024)}, f32[2359296]{0:T(1024)}) async-done(((f32[2359296]{0:T(1024)}, f32[2359296]{0:T(1024)}), (f32[2359296]{0:T(1024)}, f32[2359296]{0:T(1024)})) %all-reduce.10.cloned.1.call-update) | async-done | bytes 18874384
  (96 shorter events, 121.1 us)
Async XLA Ops:
  7.2 88.5 %all-gather.3.cloned.1.call-start = ((), (), s32[]{:S(2)}) async-start(), calls=%async_computation | async-start | bytes 9732096 | tf_op jit(solution)/shard_map/all_gather | solution.py:89
  7.9 230.4 %all-gather.5.cloned.1.call-start = ((), (), s32[]{:S(2)}) async-start(), calls=%async_computation.1 | async-start | bytes 9732096 | tf_op jit(solution)/shard_map/all_gather | solution.py:89
  8.6 920.4 %all-reduce.10.cloned.1.call-start = ((), (), s32[]{:S(2)}) async-start(), calls=%async_computation.2 | async-start | bytes 37748736
  10.2 308.9 %copy-start.2 = (f32[9,15,15]{2,1,0:T(8,128)}, f32[9,15,15]{2,1,0:T(8,128)S(1)}, u32[]{:S(2)}) copy-start(f32[9,15,15]{2,1,0:T(8,128)S(1)} %and_convert_fusion) | copy-start | bytes 24304
  18.5 5.9 slice-start.8
  21.4 2.9 slice-start.9
  71.5 35.4 %copy-start.6 = (f32[512]{0:T(512)S(1)}, f32[512]{0:T(512)}, u32[]{:S(2)}) copy-start(f32[512]{0:T(512)} %param.12) | copy-start | bytes 6148
  185.5 5.9 slice-start.4
  188.4 3.0 slice-start.5
  238.3 11.2 %copy-start.7 = (f32[512]{0:T(512)S(1)}, f32[512]{0:T(512)}, u32[]{:S(2)}) copy-start(f32[512]{0:T(512)} %param.14) | copy-start | bytes 6148
  327.0 74.0 %copy-start = (f32[9,15,15,512]{3,2,1,0:T(8,128)}, f32[9,15,15,512]{3,2,1,0:T(8,128)S(1)}, u32[]{:S(2)}) copy-start(f32[9,15,15,512]{3,2,1,0:T(8,128)S(1)} %get-tuple-element.11) | copy-start | bytes 12441604
  434.5 10.5 %slice-start = ((s8[4423680]{0:T(1024)(128)(4,1)}), s8[4194304]{0:T(1024)(128)(4,1)S(1)}, s32[]{:S(2)}) async-start(s8[4423680]{0:T(1024)(128)(4,1)} %bitcast.38), calls=%async_computation.3 | async-start | bytes 8388608
  439.7 5.3 slice-start.1
  456.7 5.7 slice-start.6
  459.5 3.0 slice-start.7
  459.5 3.0 copy-start.3
  540.3 2.1 copy-start.1
  651.2 6.7 copy-start.5
  698.3 10.7 %slice-start.2 = ((s8[4423680]{0:T(1024)(128)(4,1)}), s8[4194304]{0:T(1024)(128)(4,1)S(1)}, s32[]{:S(2)}) async-start(s8[4423680]{0:T(1024)(128)(4,1)} %bitcast.40), calls=%async_computation.5 | async-start | bytes 8388608
  703.7 5.3 slice-start.3
  717.8 6.5 slice-start.10
  717.8 6.5 slice-start.11
  720.6 4.4 slice-start.12
  720.6 4.4 copy-start.4
Sparse Core Ops, SparseCore 0:
  10.9 84.7 all-gather.2
  98.6 80.6 all-gather.4
  625.1 303.9 all-reduce.9
where the time goes:
time: 945 us; the launch traced here: 938 us
  matrix products  423 us (45%)
  local copies, waits for them, and re-layouts  270 us (29%)
  waiting for transfers between devices  161 us (17%)
  blocking collectives  40.4 us (4%)
  other arithmetic  29.5 us (3%)
  between operations  14.7 us (2%)
    dot_general x2, matrix products, convolve_back(): jnp.dot(columns, flipped_kernel, precision=lax.Precision.HIGHEST, preferr...  147 us
    dot_general x2, matrix products, kernel_grad(): lax.dot_general(columns, upstream.reshape(-1, channels), (((0,), (0,)), (...  147 us
    unnamed x4, waiting for transfers between devices  136 us
    dot_general x2, matrix products, convolve(): jnp.dot(columns, kernel.reshape(9 * channels, channels), precision=lax.Pr...  129 us
    unnamed x73, local copies, waits for them, and re-layouts  118 us
    reshape x2, local copies, waits for them, and re-layouts, tap_columns(): return jnp.concatenate(windows, axis=3).reshape(-1, 9 * channels)  65.3 us
    psum x1, blocking collectives, body(): bias4_sum, bias5_sum = lax.psum((bias4_local, bias5_local), ('rep', 'dp'))  40.4 us
    all_gather x2, waiting for transfers between devices, fetch_kernel(): lax.all_gather(flat_shard, ('rep', 'dp'), axis=0, tiled=True)  24.2 us
  transfers between devices with their start and end apart: 3, of which 2 were waited for; matrix products, arithmetic and copies ran while one was open for 35% of the time, Pallas kernels for 0%

commit v1 on v0

v1 whole, which is shorter than its diff:
```python
import functools

import jax
import jax.numpy as jnp
from jax import lax
from jax.experimental import pallas as pl
from jax.experimental.pallas import tpu as pltpu
from jax.sharding import PartitionSpec as P

AXES = ("rep", "dp")
F32 = jnp.float32
BF16 = jnp.bfloat16
LANES = 128
VMEM_LIMIT = 62 * 2**20
NN = (((1,), (0,)), ((), ()))
NT = (((1,), (1,)), ((), ()))
TN = (((0,), (0,)), ((), ()))
GELU_K = 0.7978845608028654
GELU_C = 0.044715


def patch_to_points(p0, p1, p2, p3, p4):
    d31 = p3 - p1
    return (
        2.0 * (p0 - p2) + d31,
        (p3 - p2) - 2.0 * p1,
        2.0 * p1 - 3.0 * p2 + p3,
        d31,
        (p4 - p2) - 2.0 * d31,
    )


def points_to_patch(n0, n1, n2, n3, n4):
    s = n1 + n2
    return (
        2.0 * (n2 - n1 + n4) - (n0 + n3),
        -(2.0 * (n0 + n2) + (s + n4)),
        (n0 + s) + (n3 - 2.0 * n4),
    )


def taps_to_points(k0, k1, k2):
    s = k0 + k2
    return (k0, s + k1, s - k1, k0 + 2.0 * (k1 + 2.0 * k2), k2)


def taps_to_point(index, k0, k1, k2):
    if index == 0:
        return k0
    if index == 1:
        return (k0 + k2) + k1
    if index == 2:
        return (k0 + k2) - k1
    if index == 3:
        return k0 + 2.0 * (k1 + 2.0 * k2)
    return k2


POINT_TAPS = (((0, 1.0),), ((0, 1.0), (1, 1.0), (2, 1.0)), ((0, 1.0), (1, -1.0), (2, 1.0)), ((0, 1.0), (1, 2.0), (2, 4.0)), ((2, 1.0),))


def points_to_taps(d0, d1, d2, d3, d4):
    s = d1 + d2
    return (d0 + s + d3, (d1 - d2) + 2.0 * d3, s + 4.0 * d3 + d4)


def points_to_cells(m0, m1, m2, m3, m4):
    half = 0.5 * m1
    f = (1.0 / 6.0) * m2
    g = (1.0 / 6.0) * m3
    return (0.5 * m0 - half - f + g, f - half + 2.0 * g, (4.0 * g - half) + (m4 - f))


def cells_to_points(y0, y1, y2):
    s = y0 + y2
    return (
        0.5 * y0,
        -0.5 * (s + y1),
        (1.0 / 6.0) * (y1 - s),
        (1.0 / 6.0) * (y0 + 2.0 * (y1 + 2.0 * y2)),
        y2,
    )


def split(value):
    high = value.astype(BF16)
    return high, (value - high.astype(F32)).astype(BF16)


def dot3(left_high, left_low, right_high, right_low, dims):
    def dot(left, right):
        return lax.dot_general(left, right, dims, preferred_element_type=F32)

    return dot(left_high, right_high) + dot(left_low, right_high) + dot(left_high, right_low)


def gelu_parts(v):
    square = v * v
    t = jnp.tanh(GELU_K * (v + GELU_C * (square * v)))
    half = 0.5 * (1.0 + t)
    slope = half + (0.5 * v) * (1.0 - t * t) * (GELU_K + (3.0 * GELU_K * GELU_C) * square)
    return v * half, slope


def segments(tap, start, rows, tap_rows, block_rows):
    cuts = []
    at = tap * tap_rows + start
    end = at + rows
    first = at
    while at < end:
        block = at // block_rows
        stop = min(end, (block + 1) * block_rows)
        cuts.append((block, at - block * block_rows, at - first, stop - at))
        at = stop
    return cuts


class Plan:
    def __init__(self, channels, rows, tiles, block_rows, n_pieces, n_outs):
        self.C = channels
        self.R = rows
        self.T = tiles
        self.block_rows = block_rows
        self.n_pieces = n_pieces
        self.n_outs = n_outs
        self.N = min(256, channels)


def for_each_cut(plan, tab, row, count, cut_block, act):
    if count == 1:
        act(0, 0)
        return
    which = tab[row, cut_block]
    index = tab[row + 1, cut_block]
    for ref in range(count):
        pl.when(which == ref)(functools.partial(act, ref, index))


def start_kernel_fetch(plan, tab, pieces, buf, sem, row_start, rows, col_start, cols):
    for tap in range(9):
        for block, at, to, length in segments(tap, row_start, rows, plan.C, plan.block_rows):

            def act(ref, index, tap=tap, at=at, to=to, length=length):
                pltpu.make_async_copy(
                    pieces[ref].at[index, pl.ds(at, length), pl.ds(col_start, cols)],
                    buf.at[tap, pl.ds(to, length)],
                    sem,
                ).start()

            for_each_cut(plan, tab, 0, plan.n_pieces, block, act)


def start_grad_store(plan, tab, buf, outs, sem, col_start, cols):
    for tap in range(9):
        for block, at, to, length in segments(tap, 0, plan.C, plan.C, plan.block_rows):

            def act(ref, index, tap=tap, at=at, to=to, length=length):
                pltpu.make_async_copy(
                    buf.at[tap, pl.ds(to, length)],
                    outs[ref].at[index, pl.ds(at, length), pl.ds(col_start, cols)],
                    sem,
                ).start()

            for_each_cut(plan, tab, 2, plan.n_outs, block, act)


def wait_for(buf, sem):
    pltpu.make_async_copy(buf, buf, sem).wait()


def edge_masks(plan):
    place = lax.broadcasted_iota(jnp.int32, (plan.R, LANES), 0) % plan.T
    return (place != 0).astype(F32), (place != plan.T - 1).astype(F32)


def make_patch_points(plan, x_hbm, xp, vh, vl, sem):
    T, R = plan.T, plan.R
    cols = 3 * T
    not_first, not_last = edge_masks(plan)
    chunks = plan.C // LANES

    def copy(chunk):
        slot = chunk % 2
        return pltpu.make_async_copy(
            x_hbm.at[:, :, :, pl.ds(chunk * LANES, LANES)],
            xp.at[slot, pl.ds(1, 3), pl.ds(1, cols)],
            sem.at[slot],
        )

    for slot in range(2):
        for plane in range(5):
            for col in (0, cols + 1):
                xp[slot, plane, col] = jnp.zeros((R, LANES), F32)
    copy(0).start()
    for chunk in range(chunks):
        slot = chunk % 2
        copy(chunk).wait()
        if chunk + 1 < chunks:
            copy(chunk + 1).start()

        def shift(col, _, slot=slot):
            xp[slot, 0, col + 1] = pltpu.roll(xp[slot, 3, col + 1], 1, 0) * not_first
            xp[slot, 4, col + 1] = pltpu.roll(xp[slot, 1, col + 1], R - 1, 0) * not_last
            return 0

        lax.fori_loop(0, cols, shift, 0)

        def body(j, _, slot=slot, chunk=chunk):
            for rb in range(0, R, 16):
                points = []
                for v in range(5):
                    patch = [xp[slot, u, 3 * j + v, pl.ds(rb, 16)] for u in range(5)]
                    points.append(patch_to_points(*patch))
                for u in range(5):
                    row = patch_to_points(*[points[v][u] for v in range(5)])
                    for v in range(5):
                        high, low = split(row[v])
                        vh[u, v, j, pl.ds(rb, 16), pl.ds(chunk * LANES, LANES)] = high
                        vl[u, v, j, pl.ds(rb, 16), pl.ds(chunk * LANES, LANES)] = low
            return 0

        lax.fori_loop(0, T, body, 0)


def make_cell_points(plan, y_hbm, yb, wh, wl, sem, first_chunk, chunks):
    T, R = plan.T, plan.R

    def copy(chunk):
        slot = chunk % 2
        return pltpu.make_async_copy(
            y_hbm.at[:, :, :, pl.ds((first_chunk + chunk) * LANES, LANES)], yb.at[slot], sem.at[slot]
        )

    copy(0).start()
    for chunk in range(chunks):
        slot = chunk % 2
        copy(chunk).wait()
        if chunk + 1 < chunks:
            copy(chunk + 1).start()

        def body(j, _, slot=slot, chunk=chunk):
            for rb in range(0, R, 16):
                points = []
                for b in range(3):
                    cells = [yb[slot, a, 3 * j + b, pl.ds(rb, 16)] for a in range(3)]
                    points.append(cells_to_points(*cells))
                for u in range(5):
                    row = cells_to_points(*[points[b][u] for b in range(3)])
                    for v in range(5):
                        high, low = split(row[v])
                        wh[u, v, j, pl.ds(rb, 16), pl.ds(chunk * LANES, LANES)] = high
                        wl[u, v, j, pl.ds(rb, 16), pl.ds(chunk * LANES, LANES)] = low
            return 0

        lax.fori_loop(0, T, body, 0)


def make_tap_points(kbuf, uh, ul, point):
    rows = kbuf.shape[1]
    step = 16

    def body(i, _):
        at = pl.ds(pl.multiple_of(i * step, step), step)
        parts = [taps_to_point(point, kbuf[q, at], kbuf[3 + q, at], kbuf[6 + q, at]) for q in range(3)]
        for v, value in enumerate(taps_to_points(*parts)):
            high, low = split(value)
            uh[v, at] = high
            ul[v, at] = low
        return 0

    lax.fori_loop(0, rows // step, body, 0)


def forward_kernel(plan, last, tab, mask, bias, *refs):
    refs = list(refs)
    C, N, R, T = plan.C, plan.N, plan.R, plan.T
    cols = 3 * T
    x_hbm = refs.pop(0)
    cot_hbm = refs.pop(0) if last else None
    pieces = [refs.pop(0) for _ in range(plan.n_pieces)]
    act_hbm, slope_hbm = refs.pop(0), refs.pop(0)
    bias_sum = refs.pop(0) if last else None
    xp, vh, vl, kbuf, uh, ul, mbuf, ebuf, stage, x_sem, k_sem, out_sem = refs[:12]
    cbuf, c_sem = refs[12:] if last else (None, None)
    chunks = C // N
    for n in range(chunks):
        start_kernel_fetch(plan, tab, pieces, kbuf.at[n], k_sem.at[n], 0, C, n * N, N)
    if last:
        for n in range(chunks):
            pltpu.make_async_copy(cot_hbm.at[:, :, :, pl.ds(n * N, N)], cbuf.at[n], c_sem.at[n]).start()
    make_patch_points(plan, x_hbm, xp, vh, vl, x_sem)
    for n in range(chunks):
        wait_for(kbuf.at[n], k_sem.at[n])
        for u in range(5):
            make_tap_points(kbuf.at[n], uh, ul, u)
            for v in range(5):
                left = (vh[u, v].reshape(T * R, C), vl[u, v].reshape(T * R, C))
                mbuf[v] = dot3(*left, uh[v], ul[v], NN).reshape(T, R, N)

            def columns(j, _, u=u):
                for rb in range(0, R, 16):
                    cells = points_to_cells(*[mbuf[v, j, pl.ds(rb, 16)] for v in range(5)])
                    for b in range(3):
                        ebuf[u, 3 * j + b, pl.ds(rb, 16)] = cells[b]
                return 0

            lax.fori_loop(0, T, columns, 0)
        if last:
            pltpu.make_async_copy(cot_hbm.at[:, :, :, pl.ds(n * N, N)], cbuf.at[n], c_sem.at[n]).wait()
            stage[n, 2, 0, 0] = jnp.zeros((R, N), F32)

        def finish(col, _, n=n):
            for lane in range(0, N, LANES):
                at = pl.ds(lane, LANES)
                offset = bias[0:1, pl.ds(n * N + lane, LANES)]
                for rb in range(0, R, 16):
                    rows = pl.ds(rb, 16)
                    cells = points_to_cells(*[ebuf[u, col, rows, at] for u in range(5)])
                    for a in range(3):
                        value, slope = gelu_parts(cells[a] + offset)
                        keep = mask[a, col, rows]
                        stage[n, 0, a, col, rows, at] = value * keep
                        if last:
                            back = slope * keep * cbuf[n, a, col, rows, at]
                            stage[n, 1, a, col, rows, at] = back
                            stage[n, 2, 0, 0, rows, at] += back
                        else:
                            stage[n, 1, a, col, rows, at] = slope * keep
            return 0

        lax.fori_loop(0, cols, finish, 0)
        if last:
            bias_sum[0:1, pl.ds(n * N, N)] = jnp.sum(stage[n, 2, 0, 0], axis=0, keepdims=True)
        for which, out in ((0, act_hbm), (1, slope_hbm)):
            pltpu.make_async_copy(stage.at[n, which], out.at[:, :, :, pl.ds(n * N, N)], out_sem.at[which, n]).start()
    for n in range(chunks):
        for which, out in ((0, act_hbm), (1, slope_hbm)):
            pltpu.make_async_copy(stage.at[n, which], out.at[:, :, :, pl.ds(n * N, N)], out_sem.at[which, n]).wait()


def back_kernel(plan, last, tab, mask, y_hbm, *refs):
    refs = list(refs)
    C, N, R, T = plan.C, plan.N, plan.R, plan.T
    cols = 3 * T
    slope_hbm = None if last else refs.pop(0)
    pieces = [refs.pop(0) for _ in range(plan.n_pieces)]
    out_hbm = refs.pop(0)
    bias_sum = None if last else refs.pop(0)
    yb, wh, wl, kbuf, uh, ul, mbuf, ebuf, stage, y_sem, k_sem, out_sem = refs[:12]
    sbuf, total, s_sem = (None, None, None) if last else refs[12:]
    chunks = C // N
    for n in range(chunks):
        start_kernel_fetch(plan, tab, pieces, kbuf.at[n], k_sem.at[n], n * N, N, 0, C)
    if not last:
        for n in range(chunks):
            pltpu.make_async_copy(slope_hbm.at[:, :, :, pl.ds(n * N, N)], sbuf.at[n], s_sem.at[n]).start()
    make_cell_points(plan, y_hbm, yb, wh, wl, y_sem, 0, C // LANES)
    not_first, not_last = edge_masks(plan)
    for v in range(5):
        mbuf[v, 0] = jnp.zeros((R, N), F32)
        mbuf[v, T + 1] = jnp.zeros((R, N), F32)
    for n in range(chunks):
        wait_for(kbuf.at[n], k_sem.at[n])
        for u in range(5):
            make_tap_points(kbuf.at[n], uh, ul, u)
            for v in range(5):
                left = (wh[u, v].reshape(T * R, C), wl[u, v].reshape(T * R, C))
                mbuf[v, pl.ds(1, T)] = dot3(*left, uh[v], ul[v], NT).reshape(T, R, N)

            def columns(j, _, u=u):
                for rb in range(0, R, 16):
                    rows = pl.ds(rb, 16)
                    here = points_to_patch(*[mbuf[v, j + 1, rows] for v in range(5)])
                    ebuf[u, 3 * j, rows] = here[0] + mbuf[4, j, rows]
                    ebuf[u, 3 * j + 1, rows] = here[1]
                    ebuf[u, 3 * j + 2, rows] = here[2] + 2.0 * mbuf[0, j + 2, rows]
                return 0

            lax.fori_loop(0, T, columns, 0)
        if not last:
            pltpu.make_async_copy(slope_hbm.at[:, :, :, pl.ds(n * N, N)], sbuf.at[n], s_sem.at[n]).wait()
            total[...] = jnp.zeros((R, N), F32)

        def finish(col, _, n=n):
            for lane in range(0, N, LANES):
                at = pl.ds(lane, LANES)
                points = [ebuf[u, col, :, at] for u in range(5)]
                here = points_to_patch(*points)
                cells = (
                    here[0] + pltpu.roll(points[4], 1, 0) * not_first,
                    here[1],
                    here[2] + 2.0 * (pltpu.roll(points[0], R - 1, 0) * not_last),
                )
                for a in range(3):
                    if last:
                        stage[n, a, col, :, at] = cells[a] * mask[a, col]
                    else:
                        back = cells[a] * sbuf[n, a, col, :, at]
                        stage[n, a, col, :, at] = back
                        total[:, at] += back
            return 0

        lax.fori_loop(0, cols, finish, 0)
        if not last:
            bias_sum[0:1, pl.ds(n * N, N)] = jnp.sum(total[...], axis=0, keepdims=True)
        pltpu.make_async_copy(stage.at[n], out_hbm.at[:, :, :, pl.ds(n * N, N)], out_sem.at[n]).start()
    for n in range(chunks):
        pltpu.make_async_copy(stage.at[n], out_hbm.at[:, :, :, pl.ds(n * N, N)], out_sem.at[n]).wait()


def grad_kernel(plan, tab, x_hbm, y_hbm, *refs):
    refs = list(refs)
    C, N, R, T = plan.C, plan.N, plan.R, plan.T
    outs = [refs.pop(0) for _ in range(plan.n_outs)]
    xp, vh, vl, yb, wh, wl, dbuf, kgrad, x_sem, y_sem, out_sem = refs
    chunks = C // N
    step = 16
    make_patch_points(plan, x_hbm, xp, vh, vl, x_sem)
    for n in range(chunks):
        make_cell_points(plan, y_hbm, yb, wh, wl, y_sem, n * N // LANES, N // LANES)
        for u in range(5):
            for v in range(5):
                left = (vh[u, v].reshape(T * R, C), vl[u, v].reshape(T * R, C))
                right = (wh[u, v].reshape(T * R, N), wl[u, v].reshape(T * R, N))
                dbuf[v] = dot3(*left, *right, TN)

            def add(i, _, n=n, u=u):
                at = pl.ds(pl.multiple_of(i * step, step), step)
                taps = points_to_taps(*[dbuf[v, at] for v in range(5)])
                for p, weight in POINT_TAPS[u]:
                    for q in range(3):
                        term = taps[q] if weight == 1.0 else weight * taps[q]
                        if u == 0 or (u == 1 and p > 0):
                            kgrad[n, 3 * p + q, at] = term
                        else:
                            kgrad[n, 3 * p + q, at] += term
                return 0

            lax.fori_loop(0, C // step, add, 0)
        start_grad_store(plan, tab, kgrad.at[n], outs, out_sem.at[n], n * N, N)
    for n in range(chunks):
        wait_for(kgrad.at[n], out_sem.at[n])


SMEM_SPEC = pl.BlockSpec(memory_space=pltpu.SMEM)
VMEM_SPEC = pl.BlockSpec(memory_space=pltpu.VMEM)
ANY_SPEC = pl.BlockSpec(memory_space=pl.ANY)


def plane_shape(plan):
    return jax.ShapeDtypeStruct((3, 3 * plan.T, plan.R, plan.C), F32)


def point_scratch(plan, width):
    shape = (5, 5, plan.T, plan.R, width)
    return [pltpu.VMEM(shape, BF16), pltpu.VMEM(shape, BF16)]


def call(kernel, outs, in_specs, out_specs, scratch, flops, args, name):
    moved = sum(a.size * a.dtype.itemsize for a in args) + sum(o.size * 4 for o in outs)
    return pl.pallas_call(
        kernel,
        out_shape=outs,
        in_specs=in_specs,
        out_specs=out_specs,
        scratch_shapes=scratch,
        compiler_params=pltpu.CompilerParams(vmem_limit_bytes=VMEM_LIMIT),
        cost_estimate=pl.CostEstimate(flops=flops, bytes_accessed=moved, transcendentals=0),
        name=name,
    )(*args)


def pass_flops(plan):
    return 2 * 3 * 25 * plan.T * plan.R * plan.C * plan.C


def run_forward(plan, tab, mask, bias, x, cot, pieces, name):
    last = cot is not None
    C, N, R, T = plan.C, plan.N, plan.R, plan.T
    cols = 3 * T
    chunks = C // N
    outs = [plane_shape(plan), plane_shape(plan)]
    out_specs = [ANY_SPEC, ANY_SPEC]
    scratch = [
        pltpu.VMEM((2, 5, cols + 2, R, LANES), F32),
        *point_scratch(plan, C),
        pltpu.VMEM((chunks, 9, C, N), F32),
        pltpu.VMEM((5, C, N), BF16),
        pltpu.VMEM((5, C, N), BF16),
        pltpu.VMEM((5, T, R, N), F32),
        pltpu.VMEM((5, cols, R, N), F32),
        pltpu.VMEM((chunks, 2 + last, 3, cols, R, N), F32) if not last else pltpu.VMEM((chunks, 3, 3, cols, R, N), F32),
        pltpu.SemaphoreType.DMA((2,)),
        pltpu.SemaphoreType.DMA((chunks,)),
        pltpu.SemaphoreType.DMA((2, chunks)),
    ]
    args = [tab, mask, bias, x]
    if last:
        outs.append(jax.ShapeDtypeStruct((1, C), F32))
        out_specs.append(VMEM_SPEC)
        scratch += [pltpu.VMEM((chunks, 3, cols, R, N), F32), pltpu.SemaphoreType.DMA((chunks,))]
        args.append(cot)
    args += pieces
    in_specs = [SMEM_SPEC, VMEM_SPEC, VMEM_SPEC] + [ANY_SPEC] * (len(args) - 3)
    kernel = functools.partial(forward_kernel, plan, last)
    return call(kernel, outs, in_specs, out_specs, scratch, pass_flops(plan), args, name)


def run_back(plan, tab, mask, y, slope, pieces, name):
    last = slope is None
    C, N, R, T = plan.C, plan.N, plan.R, plan.T
    cols = 3 * T
    chunks = C // N
    outs = [plane_shape(plan)]
    out_specs = [ANY_SPEC]
    scratch = [
        pltpu.VMEM((2, 3, cols, R, LANES), F32),
        *point_scratch(plan, C),
        pltpu.VMEM((chunks, 9, N, C), F32),
        pltpu.VMEM((5, N, C), BF16),
        pltpu.VMEM((5, N, C), BF16),
        pltpu.VMEM((5, T + 2, R, N), F32),
        pltpu.VMEM((5, cols, R, N), F32),
        pltpu.VMEM((chunks, 3, cols, R, N), F32),
        pltpu.SemaphoreType.DMA((2,)),
        pltpu.SemaphoreType.DMA((chunks,)),
        pltpu.SemaphoreType.DMA((chunks,)),
    ]
    args = [tab, mask, y]
    if not last:
        outs.append(jax.ShapeDtypeStruct((1, C), F32))
        out_specs.append(VMEM_SPEC)
        scratch += [
            pltpu.VMEM((chunks, 3, cols, R, N), F32),
            pltpu.VMEM((R, N), F32),
            pltpu.SemaphoreType.DMA((chunks,)),
        ]
        args.append(slope)
    args += pieces
    in_specs = [SMEM_SPEC, VMEM_SPEC] + [ANY_SPEC] * (len(args) - 2)
    kernel = functools.partial(back_kernel, plan, last)
    return call(kernel, outs, in_specs, out_specs, scratch, pass_flops(plan), args, name)


def run_grad(plan, tab, x, y, name):
    C, N, R, T = plan.C, plan.N, plan.R, plan.T
    cols = 3 * T
    chunks = C // N
    blocks = 9 * C // plan.block_rows // plan.n_outs
    outs = [jax.ShapeDtypeStruct((blocks, plan.block_rows, C), F32) for _ in range(plan.n_outs)]
    scratch = [
        pltpu.VMEM((2, 5, cols + 2, R, LANES), F32),
        *point_scratch(plan, C),
        pltpu.VMEM((2, 3, cols, R, LANES), F32),
        *point_scratch(plan, N),
        pltpu.VMEM((5, C, N), F32),
        pltpu.VMEM((chunks, 9, C, N), F32),
        pltpu.SemaphoreType.DMA((2,)),
        pltpu.SemaphoreType.DMA((2,)),
        pltpu.SemaphoreType.DMA((chunks,)),
    ]
    in_specs = [SMEM_SPEC, ANY_SPEC, ANY_SPEC]
    kernel = functools.partial(grad_kernel, plan)
    return call(kernel, outs, in_specs, [ANY_SPEC] * plan.n_outs, scratch, pass_flops(plan), [tab, x, y], name)


def to_planes(plan, cells):
    slots, side, _, channels = cells.shape
    tiled = cells.reshape(slots, plan.T, 3, side, channels).transpose(2, 3, 0, 1, 4)
    flat = tiled.reshape(3, side, slots * plan.T, channels)
    return jnp.pad(flat, ((0, 0), (0, 0), (0, plan.R - slots * plan.T), (0, 0)))


def from_planes(plan, planes, slots):
    side = 3 * plan.T
    kept = planes[:, :, : slots * plan.T].reshape(3, side, slots, plan.T, planes.shape[3])
    return kept.transpose(2, 3, 0, 1, 4).reshape(slots, side, side, planes.shape[3])


class Net:
    def __init__(self):
        self.rep = lax.axis_size("rep")
        self.dp = lax.axis_size("dp")
        self.routed = self.rep == 4 and self.dp == 8
        self.n_pieces = 4 if self.routed else 1
        self.n_outs = 2 if self.routed else 1

    def perm(self, move):
        pairs = []
        for x in range(2):
            for c in range(2):
                for z in range(4):
                    for y in range(2):
                        to = move(x, c, z, y)
                        pairs.append((((x * 2 + c) * 4 + z) * 2 + y, ((to[0] * 2 + to[1]) * 4 + to[2]) * 2 + to[3]))
        return pairs

    def send(self, value, move):
        return lax.ppermute(value, AXES, self.perm(move))

    def over_core(self, value):
        return self.send(value, lambda x, c, z, y: (x, 1 - c, z, y))

    def over_first(self, value):
        return self.send(value, lambda x, c, z, y: (x, c, z, 1 - y) if c == 0 else (1 - x, c, z, y))

    def over_second(self, value):
        return self.send(value, lambda x, c, z, y: (1 - x, c, z, y) if c == 0 else (x, c, z, 1 - y))

    def over_z(self, value, step):
        return self.send(value, lambda x, c, z, y: (x, c, (z + step) % 4, y))

    def tables(self):
        if not self.routed:
            return jnp.zeros((4, 8), jnp.int32)
        rep = lax.axis_index("rep")
        dp = lax.axis_index("dp")
        x, c, z, y = rep // 2, rep % 2, dp // 2, dp % 2
        block = jnp.arange(32, dtype=jnp.int32)
        bx, bc, bz, by = block // 16, block // 8 % 2, block // 2 % 4, block % 2
        dx, dy = bx ^ x, by ^ y
        second = jnp.where(bc == 0, dx, dy)
        first = jnp.where(bc == 0, dy, dx)
        other = (bc != c).astype(jnp.int32)
        return jnp.stack(
            [2 * other + second, 4 * first + (z - bz) % 4, other, 8 * second + 4 * first + (bz - z) % 4]
        ).astype(jnp.int32)

    def gather(self, shard):
        if not self.routed:
            return [lax.all_gather(shard, AXES, axis=0, tiled=True)[None]]
        four = jnp.stack([shard] + [self.over_z(shard, step) for step in (1, 2, 3)])
        eight = jnp.concatenate([four, self.over_first(four)])
        far = self.over_second(eight)
        return [eight, far, self.over_core(eight), self.over_core(far)]

    def scatter_sum(self, parts):
        if not self.routed:
            return lax.psum_scatter(parts[0][0], AXES, scatter_dimension=0, tiled=True)
        mine, theirs = parts
        got = self.over_core(theirs)
        got = self.over_second(mine[8:] + got[8:]) + (mine[:8] + got[:8])
        got = self.over_first(got[4:]) + got[:4]
        total = got[0]
        for step in (1, 2, 3):
            total = total + self.over_z(got[step], step)
        return total

    def total(self, value):
        if not self.routed:
            return lax.psum(value, AXES)
        value = value + self.over_core(value)
        value = value + self.over_second(value)
        value = value + self.over_first(value)
        return value + self.over_z(value, 1) + self.over_z(value, 2) + self.over_z(value, 3)


def body(
    features, map_size, item_count, conv4_weight, conv4_bias, conv5_weight, conv5_bias, cotangent
):
    slots, side, _, channels = features.shape
    net = Net()
    tiles = side // 3
    rows = -(-slots * tiles // 16) * 16
    shard_rows = conv4_weight.shape[0] // channels
    block_rows = shard_rows if net.routed else 9 * channels
    plan = Plan(channels, rows, tiles, block_rows, net.n_pieces, net.n_outs)

    live = jnp.arange(slots, dtype=jnp.int32) < item_count[0]
    inside = jnp.arange(side, dtype=jnp.int32)[None, :] < map_size[:, None]
    valid = live[:, None, None] & inside[:, :, None] & inside[:, None, :]
    mask = to_planes(plan, jnp.broadcast_to(valid.astype(F32)[..., None], (slots, side, side, LANES)))
    source = to_planes(plan, features * valid.astype(F32)[..., None])
    cot = to_planes(plan, cotangent)
    tab = net.tables()

    pieces4 = net.gather(conv4_weight.reshape(shard_rows, channels))
    pieces5 = net.gather(conv5_weight.reshape(shard_rows, channels))
    hidden, slope4 = run_forward(plan, tab, mask, conv4_bias[None], source, None, pieces4, "conv4")
    out5, back5, bias5 = run_forward(plan, tab, mask, conv5_bias[None], hidden, cot, pieces5, "conv5")
    grad5 = run_grad(plan, tab, hidden, back5, "grad5")
    back4, bias4 = run_back(plan, tab, mask, back5, slope4, pieces5, "back5")
    grad4 = run_grad(plan, tab, source, back4, "grad4")
    input_grad = run_back(plan, tab, mask, back4, None, pieces4, "back4")[0]

    total_cells = slots * net.rep * net.dp * side * side
    scale = float(total_cells) ** (-0.5)
    share5 = net.scatter_sum(grad5)
    share4 = net.scatter_sum(grad4)
    biases = net.total(jnp.concatenate([bias4, bias5])) * scale
    return (
        from_planes(plan, out5, slots),
        from_planes(plan, input_grad, slots),
        (share4 * scale).reshape(-1),
        biases[0],
        (share5 * scale).reshape(-1),
        biases[1],
    )


def solution(mesh):
    placed = (
        P(AXES, None, None, None),
        P(AXES),
        P(AXES),
        P(AXES),
        P(),
        P(AXES),
        P(),
        P(AXES, None, None, None),
    )
    return jax.shard_map(
        body,
        mesh=mesh,
        in_specs=placed,
        out_specs=(
            P(AXES, None, None, None),
            P(AXES, None, None, None),
            P(AXES),
            P(),
            P(AXES),
            P(),
        ),
        check_vma=False,
    )
```

time: 945 us -> 521 us (0.55)
  matrix products: 423 us -> 0 us
  local copies, waits for them, and re-layouts: 270 us -> 42.8 us
  Pallas kernels: 0 us -> 226 us
  starting transfers between devices: 0.11 us -> 52.1 us
  blocking collectives: 40.4 us -> 0 us
  other arithmetic: 29.5 us -> 14 us
  waiting for transfers between devices: 161 us -> 176 us
  between operations: 14.7 us -> 1.87 us
    dot_general x6 -> x0, matrix products: 423 us -> none  [the longest x2 147 us: convolve_back(): jnp.dot(columns, flipped_kernel, precision=lax.Precision.HIGHEST, preferr...]
    pallas_call x0 -> x6, Pallas kernels: none -> 226 us  [call(): pl.pallas_call(kernel, out_shape=outs, in_specs=in_specs, out_specs=out_s...]
    ppermute x0 -> x32, waiting for transfers between devices: none -> 176 us  [send(): return lax.ppermute(value, AXES, self.perm(move))]
    unnamed x4 -> x0, waiting for transfers between devices: 136 us -> none
    unnamed x73 -> x38, local copies, waits for them, and re-layouts: 118 us -> 9.94 us
    reshape x6 -> x5, local copies, waits for them, and re-layouts: 97.9 us -> 6.97 us  [the longest x3 5.15 us: to_planes(): flat = tiled.reshape(3, side, slots * plan.T, channels)]
    ppermute x0 -> x32, starting transfers between devices: none -> 52.1 us  [send(): return lax.ppermute(value, AXES, self.perm(move))]
    psum x1 -> x0, blocking collectives: 40.4 us -> none  [body(): bias4_sum, bias5_sum = lax.psum((bias4_local, bias5_local), ('rep', 'dp'))]
  transfers between devices with their start and end apart: 3 -> 32, of which waited for: 2 -> 14; matrix products, arithmetic and copies ran while one was open for 35% -> 10% of each run, Pallas kernels for 0% -> 22%
where the time goes in v1:
time: 521 us; the launch traced here: 512 us
  Pallas kernels  226 us (43%)
  waiting for transfers between devices  176 us (34%)
  starting transfers between devices  52.1 us (10%)
  local copies, waits for them, and re-layouts  42.8 us (8%)
  other arithmetic  14 us (3%)
    pallas_call x6, Pallas kernels, call(): pl.pallas_call(kernel, out_shape=outs, in_specs=in_specs, out_specs=out_s...  226 us
    ppermute x32, waiting for transfers between devices, send(): return lax.ppermute(value, AXES, self.perm(move))  176 us
    ppermute x32, starting transfers between devices, send(): return lax.ppermute(value, AXES, self.perm(move))  52.1 us
    transpose x2, local copies, waits for them, and re-layouts, from_planes(): kept.transpose(2, 3, 0, 1, 4).reshape(slots, side, side, planes.shape[3])  11.4 us
  transfers between devices with their start and end apart: 32, of which 14 were waited for; matrix products, arithmetic and copies ran while one was open for 10% of the time, Pallas kernels for 22%

profile of v1, /device:TPU:0, one launch (start us, length us, event | category | flops | bytes accessed | tf_op | source)
XLA Modules:
  0.0 511.9 jit_solution(4318262554626219322)
XLA Ops:
  1.7 5.1 collective-permute-start.2
  8.8 5.4 %collective-permute-done.2 = f32[144,512]{1,0:T(8,128)S(1)} collective-permute-done((f32[144,512]{1,0:T(8,128)S(1)}, f32[144,512]{1,0:T(8,128)S(1)}, u32[]{:S(2)}, u32[]{:S(2)}) %collective-permute-start.2) | collective-permute-done | bytes 294944 | tf_op jit(solution)/shard_map/ppermute | solution.py:599
  14.3 17.7 %collective-permute-done.1 = f32[144,512]{1,0:T(8,128)S(1)} collective-permute-done((f32[144,512]{1,0:T(8,128)S(1)}, f32[144,512]{1,0:T(8,128)S(1)}, u32[]{:S(2)}, u32[]{:S(2)}) %collective-permute-start.1) | collective-permute-done | bytes 294944 | tf_op jit(solution)/shard_map/ppermute | solution.py:599
  43.6 19.8 %collective-permute-done.8 = f32[144,512]{1,0:T(8,128)S(1)} collective-permute-done((f32[144,512]{1,0:T(8,128)}, f32[144,512]{1,0:T(8,128)S(1)}, u32[]{:S(2)}, u32[]{:S(2)}) %collective-permute-start.8) | collective-permute-done | bytes 294944 | tf_op jit(solution)/shard_map/ppermute | solution.py:599
  71.1 19.4 %collective-permute-done.10 = f32[4,144,512]{2,1,0:T(8,128)S(1)} collective-permute-done((f32[4,144,512]{2,1,0:T(8,128)S(1)}, f32[4,144,512]{2,1,0:T(8,128)S(1)}, u32[]{:S(2)}, u32[]{:S(2)}) %collective-permute-start.10) | collective-permute-done | bytes 1179680 | tf_op jit(solution)/shard_map/ppermute | solution.py:599
  91.7 10.7 %collective-permute-done.4.refs_2_.refs_1_ = f32[8,144,512]{2,1,0:T(8,128)} collective-permute-done((f32[8,144,512]{2,1,0:T(8,128)}, f32[8,144,512]{2,1,0:T(8,128)}, u32[]{:S(2)}, u32[]{:S(2)}) %collective-permute-start.4) | collective-permute-done | bytes 2359328 | tf_op jit(solution)/shard_map/ppermute | solution.py:599
  102.4 2.8 collective-permute-start.6
  106.0 21.7 %collective-permute-done.11.refs_3_.refs_2_ = f32[8,144,512]{2,1,0:T(8,128)} collective-permute-done((f32[8,144,512]{2,1,0:T(8,128)}, f32[8,144,512]{2,1,0:T(8,128)}, u32[]{:S(2)}, u32[]{:S(2)}) %collective-permute-start.11) | collective-permute-done | bytes 2359328 | tf_op jit(solution)/shard_map/ppermute | solution.py:599
  143.6 2.9 pad.13.refs_1_
  147.2 38.5 %conv4.1 = (f32[3,15,48,512]{3,2,1,0:T(8,128)}, f32[3,15,48,512]{3,2,1,0:T(8,128)}) custom-call(s32[4,32]{1,0:T(4,128)} %pad_add_fusion.tab, f32[3,15,48,128]{3,2,1,0:T(8,128)} %pad.11.mask, f32[1,512]{1,0:T(1,128)} %bitcast.106, f32[3,15,48,512]{3,2,1,0:T(8,128)} %pad.12.refs_0_.x_hbm, f32[8,144,512]{2,1,0:T(8,128)} %constant_dynamic-update-slice_fusion.refs_1_.refs_0_, ...), custom_call_target="tpu_custom_call" | custom-call | flops 9437184000 | bytes 23816704 | tf_op jit(solution)/shard_map/conv4/pallas_call | solution.py:461
  185.7 41.2 %conv5.1 = (f32[3,15,48,512]{3,2,1,0:T(8,128)}, f32[3,15,48,512]{3,2,1,0:T(8,128)}, f32[1,512]{1,0:T(1,128)}) custom-call(s32[4,32]{1,0:T(4,128)} %pad_add_fusion.tab, f32[3,15,48,128]{3,2,1,0:T(8,128)} %pad.11.mask, f32[1,512]{1,0:T(1,128)} %bitcast.107, f32[3,15,48,512]{3,2,1,0:T(8,128)} %get-tuple-element.17.refs_0_.x_hbm, ...), custom_call_target="tpu_custom_call" | custom-call | flops 9437184000 | bytes 28242432 | tf_op jit(solution)/shard_map/conv5/pallas_call | solution.py:461
  226.9 37.3 %back5.1 = (f32[3,15,48,512]{3,2,1,0:T(8,128)}, f32[1,512]{1,0:T(1,128)}) custom-call(s32[4,32]{1,0:T(4,128)} %pad_add_fusion.tab, f32[3,15,48,128]{3,2,1,0:T(8,128)} %pad.11.mask, f32[3,15,48,512]{3,2,1,0:T(8,128)} %get-tuple-element.19.y_hbm, f32[3,15,48,512]{3,2,1,0:T(8,128)} %get-tuple-element.20.refs_0_, ...), custom_call_target="tpu_custom_call" | custom-call | flops 9437184000 | bytes 23816704 | tf_op jit(solution)/shard_map/back5/pallas_call | solution.py:461
  264.1 36.7 %grad4.1 = (f32[16,144,512]{2,1,0:T(8,128)}, f32[16,144,512]{2,1,0:T(8,128)}) custom-call(s32[4,32]{1,0:T(4,128)} %pad_add_fusion.tab, f32[3,15,48,512]{3,2,1,0:T(8,128)} %pad.12.refs_0_.x_hbm, f32[3,15,48,512]{3,2,1,0:T(8,128)} %get-tuple-element.21.y_hbm), custom_call_target="tpu_custom_call" | custom-call | flops 9437184000 | bytes 18285056 | tf_op jit(solution)/shard_map/grad4/pallas_call | solution.py:461
  300.9 37.0 %grad5.1 = (f32[16,144,512]{2,1,0:T(8,128)}, f32[16,144,512]{2,1,0:T(8,128)}) custom-call(s32[4,32]{1,0:T(4,128)} %pad_add_fusion.tab, f32[3,15,48,512]{3,2,1,0:T(8,128)} %get-tuple-element.17.refs_0_.x_hbm, f32[3,15,48,512]{3,2,1,0:T(8,128)} %get-tuple-element.19.y_hbm), custom_call_target="tpu_custom_call" | custom-call | flops 9437184000 | bytes 18285056 | tf_op jit(solution)/shard_map/grad5/pallas_call | solution.py:461
  338.6 3.1 slice_add_fusion.3
  342.2 4.1 collective-permute-done.26
  350.3 45.6 %collective-permute-done.21 = f32[2,512]{1,0:T(2,128)S(1)} collective-permute-done((f32[2,512]{1,0:T(2,128)S(1)}, f32[2,512]{1,0:T(2,128)S(1)}, u32[]{:S(2)}, u32[]{:S(2)}) %collective-permute-start.21) | collective-permute-done | bytes 4128 | tf_op jit(solution)/shard_map/ppermute | solution.py:599
  410.8 34.9 %back4.1 = f32[3,15,48,512]{3,2,1,0:T(8,128)} custom-call(s32[4,32]{1,0:T(4,128)} %pad_add_fusion.tab, f32[3,15,48,128]{3,2,1,0:T(8,128)} %pad.11.mask, f32[3,15,48,512]{3,2,1,0:T(8,128)} %get-tuple-element.21.y_hbm, f32[8,144,512]{2,1,0:T(8,128)} %constant_dynamic-update-slice_fusion.refs_1_.refs_0_, f32[8,144,512]{2,1,0:T(8,128)} %collective-permute-done.4.refs_2_.refs_1_, ...), custom_call_target="tpu_custom_call" | custom-call | flops 9437184000 | bytes 19390976 | tf_op jit(solution)/shard_map/back4/pallas_call | solution.py:461
  445.8 6.9 %copy.38 = f32[3,15,45,512]{3,1,0,2:T(8,128)} copy(f32[3,15,45,512]{3,2,1,0:T(8,128)} %bitcast.94) | data formatting | bytes 8294400 | tf_op jit(solution)/shard_map/transpose | solution.py:577
  452.7 4.5 copy.37
  464.4 3.7 collective-permute-start.31
  470.9 13.7 %collective-permute-start.30 = (f32[144,512]{1,0:T(8,128)S(1)}, f32[144,512]{1,0:T(8,128)S(1)}, u32[]{:S(2)}, u32[]{:S(2)}) collective-permute-start(f32[144,512]{1,0:T(8,128)S(1)} %get-tuple-element.30), channel_id=1, source_target_pairs={{0,4},{1,5},{2,6},{3,7},{4,0},{5,1},{6,2},{7,3},{8,12},{9,13},{10,... | collective-permute-start | bytes 884744 | tf_op jit(solution)/shard_map/ppermute | solution.py:599
  485.2 14.6 %collective-permute-done.18 = f32[144,512]{1,0:T(8,128)S(1)} collective-permute-done((f32[144,512]{1,0:T(8,128)S(1)}, f32[144,512]{1,0:T(8,128)S(1)}, u32[]{:S(2)}, u32[]{:S(2)}) %collective-permute-start.18) | collective-permute-done | bytes 294944 | tf_op jit(solution)/shard_map/ppermute | solution.py:599
  500.7 10.1 %collective-permute-done.30 = f32[144,512]{1,0:T(8,128)S(1)} collective-permute-done((f32[144,512]{1,0:T(8,128)S(1)}, f32[144,512]{1,0:T(8,128)S(1)}, u32[]{:S(2)}, u32[]{:S(2)}) %collective-permute-start.30) | collective-permute-done | bytes 294944 | tf_op jit(solution)/shard_map/ppermute | solution.py:599
  (132 shorter events, 72.6 us)
Async XLA Ops:
  6.8 25.1 %collective-permute-start.1 = (f32[144,512]{1,0:T(8,128)S(1)}, f32[144,512]{1,0:T(8,128)S(1)}, u32[]{:S(2)}, u32[]{:S(2)}) collective-permute-start(f32[144,512]{1,0:T(8,128)S(1)} %reshape.415), channel_id=1, source_target_pairs={{0,4},{1,5},{2,6},{3,7},{4,0},{5,1},{6,2},{7,3},{8,12},{9,13},{10,... | collective-permute-start | bytes 884744 | tf_op jit(solution)/shard_map/ppermute | solution.py:599
  33.0 34.2 %collective-permute-start.3 = (f32[4,144,512]{2,1,0:T(8,128)}, f32[4,144,512]{2,1,0:T(8,128)S(1)}, u32[]{:S(2)}, u32[]{:S(2)}) collective-permute-start(f32[4,144,512]{2,1,0:T(8,128)} %pad_maximum_fusion), channel_id=1, source_target_pairs={{0,1},{1,0},{2,3},{3,2},{4,5},{5,4},{6,7},{7,6},{8,24},{9,25},{10,... | collective-permute-start | bytes 3538952 | tf_op jit(solution)/shard_map/ppermute | solution.py:599
  35.3 28.1 %collective-permute-start.8 = (f32[144,512]{1,0:T(8,128)}, f32[144,512]{1,0:T(8,128)S(1)}, u32[]{:S(2)}, u32[]{:S(2)}) collective-permute-start(f32[144,512]{1,0:T(8,128)} %reshape.418), channel_id=1, source_target_pairs={{0,4},{1,5},{2,6},{3,7},{4,0},{5,1},{6,2},{7,3},{8,12},{9,13},{10,... | collective-permute-start | bytes 884744 | tf_op jit(solution)/shard_map/ppermute | solution.py:599
  38.1 25.3 %collective-permute-start.7 = (f32[144,512]{1,0:T(8,128)}, f32[144,512]{1,0:T(8,128)S(1)}, u32[]{:S(2)}, u32[]{:S(2)}) collective-permute-start(f32[144,512]{1,0:T(8,128)} %reshape.418), channel_id=1, source_target_pairs={{0,2},{1,3},{2,4},{3,5},{4,6},{5,7},{6,0},{7,1},{8,10},{9,11},{10,... | collective-permute-start | bytes 884744 | tf_op jit(solution)/shard_map/ppermute | solution.py:599
  63.5 27.1 %collective-permute-start.10 = (f32[4,144,512]{2,1,0:T(8,128)S(1)}, f32[4,144,512]{2,1,0:T(8,128)S(1)}, u32[]{:S(2)}, u32[]{:S(2)}) collective-permute-start(f32[4,144,512]{2,1,0:T(8,128)S(1)} %pad_maximum_fusion.1), channel_id=1, source_target_pairs={{0,1},{1,0},{2,3},{3,2},{4,5},{5,4},{6,7},{7,6},{8,24},{9,25},{10,... | collective-permute-start | bytes 3538952 | tf_op jit(solution)/shard_map/ppermute | solution.py:599
  68.4 34.1 %collective-permute-start.4 = (f32[8,144,512]{2,1,0:T(8,128)}, f32[8,144,512]{2,1,0:T(8,128)}, u32[]{:S(2)}, u32[]{:S(2)}) collective-permute-start(f32[8,144,512]{2,1,0:T(8,128)} %constant_dynamic-update-slice_fusion.refs_1_.refs_0_), channel_id=1, source_target_pairs={{0,16},{1,17},{2,18},{3,19},{4,20},{5,21},{6,22},{7,23},{8,9},{9,8... | collective-permute-start | bytes 7077896 | tf_op jit(solution)/shard_map/ppermute | solution.py:599
  91.7 36.0 %collective-permute-start.11 = (f32[8,144,512]{2,1,0:T(8,128)}, f32[8,144,512]{2,1,0:T(8,128)}, u32[]{:S(2)}, u32[]{:S(2)}) collective-permute-start(f32[8,144,512]{2,1,0:T(8,128)} %constant_dynamic-update-slice_fusion.5.refs_2_.refs_1_), channel_id=1, source_target_pairs={{0,16},{1,17},{2,18},{3,19},{4,20},{5,21},{6,22},{7,23},{8,9},{9,8... | collective-permute-start | bytes 7077896 | tf_op jit(solution)/shard_map/ppermute | solution.py:599
  91.7 55.5 %collective-permute-start.5 = (f32[8,144,512]{2,1,0:T(8,128)}, f32[8,144,512]{2,1,0:T(8,128)}, u32[]{:S(2)}, u32[]{:S(2)}) collective-permute-start(f32[8,144,512]{2,1,0:T(8,128)} %constant_dynamic-update-slice_fusion.refs_1_.refs_0_), channel_id=1, source_target_pairs={{0,8},{1,9},{2,10},{3,11},{4,12},{5,13},{6,14},{7,15},{8,0},{9,1},... | collective-permute-start | bytes 7077896 | tf_op jit(solution)/shard_map/ppermute | solution.py:599
  102.4 44.8 %collective-permute-start.6 = (f32[8,144,512]{2,1,0:T(8,128)}, f32[8,144,512]{2,1,0:T(8,128)}, u32[]{:S(2)}, u32[]{:S(2)}) collective-permute-start(f32[8,144,512]{2,1,0:T(8,128)} %collective-permute-done.4.refs_2_.refs_1_), channel_id=1, source_target_pairs={{0,8},{1,9},{2,10},{3,11},{4,12},{5,13},{6,14},{7,15},{8,0},{9,1},... | collective-permute-start | bytes 7077896 | tf_op jit(solution)/shard_map/ppermute | solution.py:599
  106.0 79.7 %collective-permute-start.12 = (f32[8,144,512]{2,1,0:T(8,128)}, f32[8,144,512]{2,1,0:T(8,128)}, u32[]{:S(2)}, u32[]{:S(2)}) collective-permute-start(f32[8,144,512]{2,1,0:T(8,128)} %constant_dynamic-update-slice_fusion.5.refs_2_.refs_1_), channel_id=1, source_target_pairs={{0,8},{1,9},{2,10},{3,11},{4,12},{5,13},{6,14},{7,15},{8,0},{9,1},... | collective-permute-start | bytes 7077896 | tf_op jit(solution)/shard_map/ppermute | solution.py:599
  127.7 58.0 %collective-permute-start.13 = (f32[8,144,512]{2,1,0:T(8,128)}, f32[8,144,512]{2,1,0:T(8,128)}, u32[]{:S(2)}, u32[]{:S(2)}) collective-permute-start(f32[8,144,512]{2,1,0:T(8,128)} %collective-permute-done.11.refs_3_.refs_2_), channel_id=1, source_target_pairs={{0,8},{1,9},{2,10},{3,11},{4,12},{5,13},{6,14},{7,15},{8,0},{9,1},... | collective-permute-start | bytes 7077896 | tf_op jit(solution)/shard_map/ppermute | solution.py:599
  300.8 37.7 %collective-permute-start.14 = (f32[16,144,512]{2,1,0:T(8,128)}, f32[16,144,512]{2,1,0:T(8,128)}, u32[]{:S(2)}, u32[]{:S(2)}) collective-permute-start(f32[16,144,512]{2,1,0:T(8,128)} %get-tuple-element.23), channel_id=1, source_target_pairs={{0,8},{1,9},{2,10},{3,11},{4,12},{5,13},{6,14},{7,15},{8,0},{9,1},... | collective-permute-start | bytes 14155784 | tf_op jit(solution)/shard_map/ppermute | solution.py:599
  341.7 60.0 %collective-permute-start.15 = (f32[8,144,512]{2,1,0:T(8,128)S(1)}, f32[8,144,512]{2,1,0:T(8,128)S(1)}, u32[]{:S(2)}, u32[]{:S(2)}) collective-permute-start(f32[8,144,512]{2,1,0:T(8,128)S(1)} %slice_add_fusion.3), channel_id=1, source_target_pairs={{0,16},{1,17},{2,18},{3,19},{4,20},{5,21},{6,22},{7,23},{8,9},{9,8... | collective-permute-start | bytes 7077896 | tf_op jit(solution)/shard_map/ppermute | solution.py:599
  346.9 60.0 %collective-permute-start.27 = (f32[8,144,512]{2,1,0:T(8,128)S(1)}, f32[8,144,512]{2,1,0:T(8,128)S(1)}, u32[]{:S(2)}, u32[]{:S(2)}) collective-permute-start(f32[8,144,512]{2,1,0:T(8,128)S(1)} %slice_add_fusion.1), channel_id=1, source_target_pairs={{0,16},{1,17},{2,18},{3,19},{4,20},{5,21},{6,22},{7,23},{8,9},{9,8... | collective-permute-start | bytes 7077896 | tf_op jit(solution)/shard_map/ppermute | solution.py:599
  349.5 46.4 %collective-permute-start.21 = (f32[2,512]{1,0:T(2,128)S(1)}, f32[2,512]{1,0:T(2,128)S(1)}, u32[]{:S(2)}, u32[]{:S(2)}) collective-permute-start(f32[2,512]{1,0:T(2,128)S(1)} %fusion.23), channel_id=1, source_target_pairs={{0,16},{1,17},{2,18},{3,19},{4,20},{5,21},{6,22},{7,23},{8,9},{9,8... | collective-permute-start | bytes 12296 | tf_op jit(solution)/shard_map/ppermute | solution.py:599
  399.6 57.6 %collective-permute-start.25 = (f32[2,512]{1,0:T(2,128)S(1)}, f32[2,512]{1,0:T(2,128)S(1)}, u32[]{:S(2)}, u32[]{:S(2)}) collective-permute-start(f32[2,512]{1,0:T(2,128)S(1)} %add.274), channel_id=1, source_target_pairs={{0,6},{1,7},{2,0},{3,1},{4,2},{5,3},{6,4},{7,5},{8,14},{9,15},{10,... | collective-permute-start | bytes 12296 | tf_op jit(solution)/shard_map/ppermute | solution.py:599
  399.6 57.6 %collective-permute-start.24 = (f32[2,512]{1,0:T(2,128)S(1)}, f32[2,512]{1,0:T(2,128)S(1)}, u32[]{:S(2)}, u32[]{:S(2)}) collective-permute-start(f32[2,512]{1,0:T(2,128)S(1)} %add.274), channel_id=1, source_target_pairs={{0,4},{1,5},{2,6},{3,7},{4,0},{5,1},{6,2},{7,3},{8,12},{9,13},{10,... | collective-permute-start | bytes 12296 | tf_op jit(solution)/shard_map/ppermute | solution.py:599
  399.7 57.5 %collective-permute-start.23 = (f32[2,512]{1,0:T(2,128)S(1)}, f32[2,512]{1,0:T(2,128)S(1)}, u32[]{:S(2)}, u32[]{:S(2)}) collective-permute-start(f32[2,512]{1,0:T(2,128)S(1)} %add.274), channel_id=1, source_target_pairs={{0,2},{1,3},{2,4},{3,5},{4,6},{5,7},{6,0},{7,1},{8,10},{9,11},{10,... | collective-permute-start | bytes 12296 | tf_op jit(solution)/shard_map/ppermute | solution.py:599
  405.4 51.9 %collective-permute-start.16 = (f32[4,144,512]{2,1,0:T(8,128)}, f32[4,144,512]{2,1,0:T(8,128)}, u32[]{:S(2)}, u32[]{:S(2)}) collective-permute-start(f32[4,144,512]{2,1,0:T(8,128)} %slice.99), channel_id=1, source_target_pairs={{0,1},{1,0},{2,3},{3,2},{4,5},{5,4},{6,7},{7,6},{8,24},{9,25},{10,... | collective-permute-start | bytes 3538952 | tf_op jit(solution)/shard_map/ppermute | solution.py:599
  410.2 53.7 %collective-permute-start.28 = (f32[4,144,512]{2,1,0:T(8,128)}, f32[4,144,512]{2,1,0:T(8,128)S(1)}, u32[]{:S(2)}, u32[]{:S(2)}) collective-permute-start(f32[4,144,512]{2,1,0:T(8,128)} %slice.108), channel_id=1, source_target_pairs={{0,1},{1,0},{2,3},{3,2},{4,5},{5,4},{6,7},{7,6},{8,24},{9,25},{10,... | collective-permute-start | bytes 3538952 | tf_op jit(solution)/shard_map/ppermute | solution.py:599
  462.9 37.0 %collective-permute-start.18 = (f32[144,512]{1,0:T(8,128)S(1)}, f32[144,512]{1,0:T(8,128)S(1)}, u32[]{:S(2)}, u32[]{:S(2)}) collective-permute-start(f32[144,512]{1,0:T(8,128)S(1)} %get-tuple-element.33), channel_id=1, source_target_pairs={{0,4},{1,5},{2,6},{3,7},{4,0},{5,1},{6,2},{7,3},{8,12},{9,13},{10,... | collective-permute-start | bytes 884744 | tf_op jit(solution)/shard_map/ppermute | solution.py:599
  464.3 36.4 %collective-permute-start.29 = (f32[144,512]{1,0:T(8,128)S(1)}, f32[144,512]{1,0:T(8,128)S(1)}, u32[]{:S(2)}, u32[]{:S(2)}) collective-permute-start(f32[144,512]{1,0:T(8,128)S(1)} %get-tuple-element.28), channel_id=1, source_target_pairs={{0,2},{1,3},{2,4},{3,5},{4,6},{5,7},{6,0},{7,1},{8,10},{9,11},{10,... | collective-permute-start | bytes 884744 | tf_op jit(solution)/shard_map/ppermute | solution.py:599
  464.4 36.3 %collective-permute-start.31 = (f32[144,512]{1,0:T(8,128)S(1)}, f32[144,512]{1,0:T(8,128)S(1)}, u32[]{:S(2)}, u32[]{:S(2)}) collective-permute-start(f32[144,512]{1,0:T(8,128)S(1)} %get-tuple-element.29), channel_id=1, source_target_pairs={{0,6},{1,7},{2,0},{3,1},{4,2},{5,3},{6,4},{7,5},{8,14},{9,15},{10,... | collective-permute-start | bytes 884744 | tf_op jit(solution)/shard_map/ppermute | solution.py:599
  470.9 39.9 %collective-permute-start.30 = (f32[144,512]{1,0:T(8,128)S(1)}, f32[144,512]{1,0:T(8,128)S(1)}, u32[]{:S(2)}, u32[]{:S(2)}) collective-permute-start(f32[144,512]{1,0:T(8,128)S(1)} %get-tuple-element.30), channel_id=1, source_target_pairs={{0,4},{1,5},{2,6},{3,7},{4,0},{5,1},{6,2},{7,3},{8,12},{9,13},{10,... | collective-permute-start | bytes 884744 | tf_op jit(solution)/shard_map/ppermute | solution.py:599
  (22 other events, 270.2 us)

commit v2 on v1

v2 whole, which is shorter than its diff:
```python
import functools

import jax
import jax.numpy as jnp
from jax import lax
from jax.experimental import pallas as pl
from jax.experimental.pallas import tpu as pltpu
from jax.sharding import PartitionSpec as P

AXES = ("rep", "dp")
F32 = jnp.float32
BF16 = jnp.bfloat16
LANES = 128
VMEM_LIMIT = 62 * 2**20
NN = (((1,), (0,)), ((), ()))
NT = (((1,), (1,)), ((), ()))
TN = (((0,), (0,)), ((), ()))
GELU_K = 0.7978845608028654
GELU_C = 0.044715


def patch_to_points(p0, p1, p2, p3, p4):
    d31 = p3 - p1
    return (
        2.0 * (p0 - p2) + d31,
        (p3 - p2) - 2.0 * p1,
        2.0 * p1 - 3.0 * p2 + p3,
        d31,
        (p4 - p2) - 2.0 * d31,
    )


def points_to_patch(n0, n1, n2, n3, n4):
    s = n1 + n2
    return (
        2.0 * (n2 - n1 + n4) - (n0 + n3),
        -(2.0 * (n0 + n2) + (s + n4)),
        (n0 + s) + (n3 - 2.0 * n4),
    )


def taps_to_points(k0, k1, k2):
    s = k0 + k2
    return (k0, s + k1, s - k1, k0 + 2.0 * (k1 + 2.0 * k2), k2)


def taps_to_point(index, k0, k1, k2, at):
    if index == 0:
        return k0[at]
    if index == 1:
        return (k0[at] + k2[at]) + k1[at]
    if index == 2:
        return (k0[at] + k2[at]) - k1[at]
    if index == 3:
        return k0[at] + 2.0 * (k1[at] + 2.0 * k2[at])
    return k2[at]


POINT_TAPS = (((0, 1.0),), ((0, 1.0), (1, 1.0), (2, 1.0)), ((0, 1.0), (1, -1.0), (2, 1.0)), ((0, 1.0), (1, 2.0), (2, 4.0)), ((2, 1.0),))


def points_to_taps(d0, d1, d2, d3, d4):
    s = d1 + d2
    return (d0 + s + d3, (d1 - d2) + 2.0 * d3, s + 4.0 * d3 + d4)


def points_to_cells(m0, m1, m2, m3, m4):
    half = 0.5 * m1
    f = (1.0 / 6.0) * m2
    g = (1.0 / 6.0) * m3
    return (0.5 * m0 - half - f + g, f - half + 2.0 * g, (4.0 * g - half) + (m4 - f))


def cells_to_points(y0, y1, y2):
    s = y0 + y2
    return (
        0.5 * y0,
        -0.5 * (s + y1),
        (1.0 / 6.0) * (y1 - s),
        (1.0 / 6.0) * (y0 + 2.0 * (y1 + 2.0 * y2)),
        y2,
    )


def split(value):
    high = value.astype(BF16)
    return high, (value - high.astype(F32)).astype(BF16)


def dot3(left_high, left_low, right_high, right_low, dims):
    def dot(left, right):
        return lax.dot_general(left, right, dims, preferred_element_type=F32)

    return dot(left_high, right_high) + dot(left_low, right_high) + dot(left_high, right_low)


def gelu_parts(v):
    square = v * v
    t = jnp.tanh(GELU_K * (v + GELU_C * (square * v)))
    half = 0.5 * (1.0 + t)
    slope = half + (0.5 * v) * (1.0 - t * t) * (GELU_K + (3.0 * GELU_K * GELU_C) * square)
    return v * half, slope


def segments(tap, start, rows, tap_rows, block_rows):
    cuts = []
    at = tap * tap_rows + start
    end = at + rows
    first = at
    while at < end:
        block = at // block_rows
        stop = min(end, (block + 1) * block_rows)
        cuts.append((block, at - block * block_rows, at - first, stop - at))
        at = stop
    return cuts


class Plan:
    def __init__(self, channels, rows, tiles, block_rows, n_pieces, n_outs):
        self.C = channels
        self.R = rows
        self.T = tiles
        self.block_rows = block_rows
        self.n_pieces = n_pieces
        self.n_outs = n_outs
        self.N = min(256, channels)


def for_each_cut(plan, tab, row, count, cut_block, act):
    if count == 1:
        act(0, 0)
        return
    which = tab[row, cut_block]
    index = tab[row + 1, cut_block]
    for ref in range(count):
        pl.when(which == ref)(functools.partial(act, ref, index))


def start_kernel_fetch(plan, tab, pieces, buf, sem, row_start, rows, col_start, cols):
    for tap in range(9):
        for block, at, to, length in segments(tap, row_start, rows, plan.C, plan.block_rows):

            def act(ref, index, tap=tap, at=at, to=to, length=length):
                pltpu.make_async_copy(
                    pieces[ref].at[index, pl.ds(at, length), pl.ds(col_start, cols)],
                    buf.at[tap, pl.ds(to, length)],
                    sem,
                ).start()

            for_each_cut(plan, tab, 0, plan.n_pieces, block, act)


def start_grad_store(plan, tab, buf, outs, sem, col_start, cols):
    for tap in range(9):
        for block, at, to, length in segments(tap, 0, plan.C, plan.C, plan.block_rows):

            def act(ref, index, tap=tap, at=at, to=to, length=length):
                pltpu.make_async_copy(
                    buf.at[tap, pl.ds(to, length)],
                    outs[ref].at[index, pl.ds(at, length), pl.ds(col_start, cols)],
                    sem,
                ).start()

            for_each_cut(plan, tab, 2, plan.n_outs, block, act)


def wait_for(buf, sem):
    pltpu.make_async_copy(buf, buf, sem).wait()


def edge_masks(plan):
    place = lax.broadcasted_iota(jnp.int32, (plan.R, LANES), 0) % plan.T
    return (place != 0).astype(F32), (place != plan.T - 1).astype(F32)


def interleave(dots, tasks):
    done = 0
    for i, dot in enumerate(dots):
        dot()
        upto = len(tasks) * (i + 1) // len(dots)
        for task in tasks[done:upto]:
            task()
        done = upto


def run_all(tasks):
    for task in tasks:
        task()


def store_split(high_ref, low_ref, at, value):
    high, low = split(value)
    high_ref[at] = high
    low_ref[at] = low


def patch_tasks(plan, xp, vh, vl, u):
    T = plan.T

    def task(lane, rb):
        rows, at = pl.ds(rb, 16), pl.ds(lane, LANES)
        line = []
        for col in range(3 * T + 2):
            if col in (0, 3 * T + 1):
                line.append(jnp.zeros((16, LANES), F32))
            else:
                line.append(patch_to_point(u, [xp.at[k, col - 1] for k in range(5)], (rows, at)))
        for j in range(T):
            for v, value in enumerate(patch_to_points(*line[3 * j : 3 * j + 5])):
                store_split(vh, vl, (u, v, j, rows, at), value)

    return [functools.partial(task, lane, rb) for lane in range(0, plan.C, LANES) for rb in range(0, plan.R, 16)]


def patch_to_point(u, planes, at):
    if u == 0:
        p1, p3 = planes[1][at], planes[3][at]
        return 2.0 * (planes[0][at] - planes[2][at]) + (p3 - p1)
    if u == 1:
        return (planes[3][at] - planes[2][at]) - 2.0 * planes[1][at]
    if u == 2:
        return 2.0 * planes[1][at] - 3.0 * planes[2][at] + planes[3][at]
    if u == 3:
        return planes[3][at] - planes[1][at]
    return (planes[4][at] - planes[2][at]) - 2.0 * (planes[3][at] - planes[1][at])


def cell_to_point(u, planes, at):
    if u == 0:
        return 0.5 * planes[0][at]
    if u == 1:
        return -0.5 * ((planes[0][at] + planes[2][at]) + planes[1][at])
    if u == 2:
        return (1.0 / 6.0) * (planes[1][at] - (planes[0][at] + planes[2][at]))
    if u == 3:
        return (1.0 / 6.0) * (planes[0][at] + 2.0 * (planes[1][at] + 2.0 * planes[2][at]))
    return planes[2][at]


def cell_tasks(plan, yb, wh, wl, u):
    def task(j, lane, rb):
        rows, at = pl.ds(rb, 16), pl.ds(lane, LANES)
        line = [cell_to_point(u, [yb.at[a, 3 * j + b] for a in range(3)], (rows, at)) for b in range(3)]
        for v, value in enumerate(cells_to_points(*line)):
            store_split(wh, wl, (v, j, rows, at), value)

    return [
        functools.partial(task, j, lane, rb)
        for j in range(plan.T)
        for lane in range(0, plan.N, LANES)
        for rb in range(0, plan.R, 16)
    ]


def tap_tasks(kbuf, uh, ul, point):
    def task(row):
        at = pl.ds(row, 16)
        parts = [taps_to_point(point, kbuf.at[q], kbuf.at[3 + q], kbuf.at[6 + q], at) for q in range(3)]
        for v, value in enumerate(taps_to_points(*parts)):
            store_split(uh, ul, (v, at), value)

    return [functools.partial(task, row) for row in range(0, kbuf.shape[1], 16)]


def dot_tasks(lefts, rights, dims, put):
    def dot(v):
        left = tuple(part.reshape(part.shape[0] * part.shape[1], part.shape[2]) for part in lefts(v))
        put(v, dot3(*left, *rights(v), dims))

    return [functools.partial(dot, v) for v in range(5)]


def forward_kernel(plan, last, tab, mask, bias, *refs):
    refs = list(refs)
    C, N, R, T = plan.C, plan.N, plan.R, plan.T
    cols = 3 * T
    x_hbm = refs.pop(0)
    cot_hbm = refs.pop(0) if last else None
    pieces = [refs.pop(0) for _ in range(plan.n_pieces)]
    act_hbm, slope_hbm, v_hbm = refs.pop(0), refs.pop(0), refs.pop(0)
    bias_sum = refs.pop(0) if last else None
    xp, vh, vl, kbuf, uh, ul, mbuf, ebuf, tail, x_sem, k_sem, out_sem, v_sem = refs[:13]
    cbuf, total, c_sem = refs[13:] if last else (None, None, None)
    chunks = C // N
    lanes = [pl.ds(lane, LANES) for lane in range(0, C, LANES)]

    def x_copy(i):
        return pltpu.make_async_copy(x_hbm.at[:, :, :, lanes[i]], xp.at[pl.ds(1, 3), :, :, lanes[i]], x_sem.at[i])

    def cot_copy(n):
        return pltpu.make_async_copy(cot_hbm.at[:, :, :, pl.ds(n * N, N)], cbuf, c_sem)

    def v_copies(u):
        return [
            pltpu.make_async_copy(part.at[u], v_hbm.at[which, u], v_sem.at[which, u])
            for which, part in enumerate((vh, vl))
        ]

    def out_copies(n):
        to = pl.ds(n * N, N)
        return [
            pltpu.make_async_copy(ebuf.at[n, pl.ds(0, 3)], act_hbm.at[:, :, :, to], out_sem.at[n, 0]),
            pltpu.make_async_copy(ebuf.at[n, pl.ds(3, 2)], slope_hbm.at[pl.ds(0, 2), :, :, to], out_sem.at[n, 1]),
            pltpu.make_async_copy(tail.at[n], slope_hbm.at[2, :, :, to], out_sem.at[n, 2]),
        ]

    for i in range(len(lanes)):
        x_copy(i).start()
    for n in range(chunks):
        start_kernel_fetch(plan, tab, pieces, kbuf.at[n], k_sem.at[n], 0, C, n * N, N)
    if last:
        cot_copy(0).start()
        total[...] = jnp.zeros((16, C), F32)
    not_first, not_last = edge_masks(plan)

    def shift(to, source, by, keep, at, col, _):
        xp[to, col, :, at] = pltpu.roll(xp[source, col, :, at], by, 0) * keep
        return 0

    first = patch_tasks(plan, xp, vh, vl, 0)
    per_lane = len(first) // len(lanes)
    for i, at in enumerate(lanes):
        x_copy(i).wait()
        lax.fori_loop(0, cols, functools.partial(shift, 0, 3, 1, not_first, at), 0)
        lax.fori_loop(0, cols, functools.partial(shift, 4, 1, R - 1, not_last, at), 0)
        run_all(first[i * per_lane : (i + 1) * per_lane])
    for copy in v_copies(0):
        copy.start()

    def column_task(n, u, j, rb):
        rows = pl.ds(rb, 16)
        cells = points_to_cells(*[mbuf[(n * 5 + u) % 2, v, j, rows] for v in range(5)])
        for b in range(3):
            ebuf[n, u, 3 * j + b, rows] = cells[b]

    def column_tasks(n, u):
        return [functools.partial(column_task, n, u, j, rb) for j in range(T) for rb in range(0, R, 16)]

    def finish_task(n, col, lane, rb):
        at, rows = pl.ds(lane, LANES), pl.ds(rb, 16)
        wide = pl.ds(n * N + lane, LANES)
        offset = bias[0:1, wide]
        cells = points_to_cells(*[ebuf[n, u, col, rows, at] for u in range(5)])
        sums = None
        for a in range(3):
            value, slope = gelu_parts(cells[a] + offset)
            keep = mask[a, col, rows]
            slope = slope * keep
            if last:
                slope = slope * cbuf[a, col, rows, at]
                sums = slope if sums is None else sums + slope
            ebuf[n, a, col, rows, at] = value * keep
            if a < 2:
                ebuf[n, 3 + a, col, rows, at] = slope
            else:
                tail[n, col, rows, at] = slope
        if last:
            total[:, wide] += sums

    def finish_tasks(n):
        return [
            functools.partial(finish_task, n, col, lane, rb)
            for col in range(cols)
            for lane in range(0, N, LANES)
            for rb in range(0, R, 16)
        ]

    steps = [(n, u) for n in range(chunks) for u in range(5)]
    wait_for(kbuf.at[0], k_sem.at[0])
    run_all(tap_tasks(kbuf.at[0], uh.at[0], ul.at[0], 0))
    for s, (n, u) in enumerate(steps):
        tasks = []
        if n > 0 and u == 0:
            finishing = finish_tasks(n - 1)
            if last:
                cot_copy(n - 1).wait()
        if s + 1 < len(steps):
            next_n, next_u = steps[s + 1]
            if next_u == 0:
                wait_for(kbuf.at[next_n], k_sem.at[next_n])
            if n == 0 and u < 4:
                tasks += patch_tasks(plan, xp, vh, vl, u + 1)
            tasks += tap_tasks(kbuf.at[next_n], uh.at[(s + 1) % 2], ul.at[(s + 1) % 2], next_u)
        if s > 0:
            tasks = column_tasks(*steps[s - 1]) + tasks
        if n > 0 and u > 0:
            count = len(finishing)
            tasks += finishing[count * (u - 1) // 4 : count * u // 4]

        def put(v, value, s=s):
            mbuf[s % 2, v] = value.reshape(T, R, N)

        interleave(
            dot_tasks(
                lambda v: (vh[u, v], vl[u, v]),
                lambda v: (uh[s % 2, v], ul[s % 2, v]),
                NN,
                put,
            ),
            tasks,
        )
        if n == 0 and u < 4:
            for copy in v_copies(u + 1):
                copy.start()
        if n > 0 and u == 4:
            for copy in out_copies(n - 1):
                copy.start()
            if last:
                cot_copy(n).start()
    run_all(column_tasks(*steps[-1]))
    n = chunks - 1
    if last:
        cot_copy(n).wait()
    run_all(finish_tasks(n))
    for copy in out_copies(n):
        copy.start()
    if last:
        bias_sum[...] = jnp.sum(total[...], axis=0, keepdims=True)
    for u in range(5):
        for copy in v_copies(u):
            copy.wait()
    for n in range(chunks):
        for copy in out_copies(n):
            copy.wait()


def back_kernel(plan, last, tab, mask, *refs):
    refs = list(refs)
    C, N, R, T = plan.C, plan.N, plan.R, plan.T
    cols = 3 * T
    chunks = C // N
    w_hbm = refs.pop(0)
    slope_hbm = None if last else refs.pop(0)
    pieces = [refs.pop(0) for _ in range(plan.n_pieces)]
    out_hbm = refs.pop(0)
    bias_sum = None if last else refs.pop(0)
    wh, wl, kbuf, uh, ul, mbuf, ebuf, w_sem, k_sem, out_sem = refs[:10]
    sbuf, total, s_sem = (None, None, None) if last else refs[10:]

    def w_copies(u):
        return [
            pltpu.make_async_copy(w_hbm.at[which, u], part.at[u], w_sem.at[which, u])
            for which, part in enumerate((wh, wl))
        ]

    def slope_copy(n):
        return pltpu.make_async_copy(slope_hbm.at[:, :, :, pl.ds(n * N, N)], sbuf, s_sem)

    def out_copy(n):
        return pltpu.make_async_copy(ebuf.at[n, pl.ds(0, 3)], out_hbm.at[:, :, :, pl.ds(n * N, N)], out_sem.at[n])

    start_kernel_fetch(plan, tab, pieces, kbuf.at[0], k_sem.at[0], 0, N, 0, C)
    for u in range(5):
        for copy in w_copies(u):
            copy.start()
    for n in range(1, chunks):
        start_kernel_fetch(plan, tab, pieces, kbuf.at[n], k_sem.at[n], n * N, N, 0, C)
    if not last:
        slope_copy(0).start()
        total[...] = jnp.zeros((R, C), F32)
    not_first, not_last = edge_masks(plan)
    for parity in range(2):
        for v in (0, 4):
            mbuf[parity, v, 0] = jnp.zeros((R, N), F32)
            mbuf[parity, v, T + 1] = jnp.zeros((R, N), F32)

    def column_task(n, u, j, rb):
        rows = pl.ds(rb, 16)
        parity = (n * 5 + u) % 2
        here = points_to_patch(*[mbuf[parity, v, j + 1, rows] for v in range(5)])
        ebuf[n, u, 3 * j, rows] = here[0] + mbuf[parity, 4, j, rows]
        ebuf[n, u, 3 * j + 1, rows] = here[1]
        ebuf[n, u, 3 * j + 2, rows] = here[2] + 2.0 * mbuf[parity, 0, j + 2, rows]

    def column_tasks(n, u):
        return [functools.partial(column_task, n, u, j, rb) for j in range(T) for rb in range(0, R, 16)]

    def finish_task(n, col, lane):
        at = pl.ds(lane, LANES)
        wide = pl.ds(n * N + lane, LANES)
        points = [ebuf[n, u, col, :, at] for u in range(5)]
        here = points_to_patch(*points)
        cells = (
            here[0] + pltpu.roll(points[4], 1, 0) * not_first,
            here[1],
            here[2] + 2.0 * (pltpu.roll(points[0], R - 1, 0) * not_last),
        )
        sums = None
        for a in range(3):
            back = cells[a] * (mask[a, col] if last else sbuf[a, col, :, at])
            ebuf[n, a, col, :, at] = back
            sums = back if sums is None else sums + back
        if not last:
            total[:, wide] += sums

    def finish_tasks(n):
        return [functools.partial(finish_task, n, col, lane) for col in range(cols) for lane in range(0, N, LANES)]

    steps = [(n, u) for n in range(chunks) for u in range(5)]
    wait_for(kbuf.at[0], k_sem.at[0])
    run_all(tap_tasks(kbuf.at[0], uh.at[0], ul.at[0], 0))
    for s, (n, u) in enumerate(steps):
        tasks = []
        if n == 0:
            for copy in w_copies(u):
                copy.wait()
        if n > 0 and u == 0:
            finishing = finish_tasks(n - 1)
            if not last:
                slope_copy(n - 1).wait()
        if s + 1 < len(steps):
            next_n, next_u = steps[s + 1]
            if next_u == 0:
                wait_for(kbuf.at[next_n], k_sem.at[next_n])
            tasks += tap_tasks(kbuf.at[next_n], uh.at[(s + 1) % 2], ul.at[(s + 1) % 2], next_u)
        if s > 0:
            tasks = column_tasks(*steps[s - 1]) + tasks
        if n > 0 and u > 0:
            count = len(finishing)
            tasks += finishing[count * (u - 1) // 4 : count * u // 4]

        def put(v, value, s=s):
            mbuf[s % 2, v, pl.ds(1, T)] = value.reshape(T, R, N)

        interleave(
            dot_tasks(
                lambda v: (wh[u, v], wl[u, v]),
                lambda v: (uh[s % 2, v], ul[s % 2, v]),
                NT,
                put,
            ),
            tasks,
        )
        if n > 0 and u == 4:
            out_copy(n - 1).start()
            if not last:
                slope_copy(n).start()
    run_all(column_tasks(*steps[-1]))
    n = chunks - 1
    if not last:
        slope_copy(n).wait()
    run_all(finish_tasks(n))
    out_copy(n).start()
    if not last:
        bias_sum[...] = jnp.sum(total[...], axis=0, keepdims=True)
    for n in range(chunks):
        out_copy(n).wait()


def grad_kernel(plan, tab, bias_rows, v_hbm, y_hbm, *refs):
    refs = list(refs)
    C, N, R, T = plan.C, plan.N, plan.R, plan.T
    chunks = C // N
    outs = [refs.pop(0) for _ in range(plan.n_outs)]
    w_hbm = refs.pop(0)
    vh, vl, yb, wh, wl, dbuf, kgrad, v_sem, y_sem, w_sem, out_sem, bias_sem = refs

    def v_copies(u):
        return [
            pltpu.make_async_copy(v_hbm.at[which, u], part.at[u], v_sem.at[which, u])
            for which, part in enumerate((vh, vl))
        ]

    def y_copy(n):
        return pltpu.make_async_copy(y_hbm.at[:, :, :, pl.ds(n * N, N)], yb.at[n], y_sem.at[n])

    def w_copies(s):
        n, u = steps[s]
        return [
            pltpu.make_async_copy(
                part.at[s % 3], w_hbm.at[which, u, :, :, :, pl.ds(n * N, N)], w_sem.at[which, s % 3]
            )
            for which, part in enumerate((wh, wl))
        ]

    def add_task(n, u, row):
        at = pl.ds(row, 16)
        taps = points_to_taps(*[dbuf[(n * 5 + u) % 2, v, at] for v in range(5)])
        for p, weight in POINT_TAPS[u]:
            for q in range(3):
                term = taps[q] if weight == 1.0 else weight * taps[q]
                if u == 0 or (u == 1 and p > 0):
                    kgrad[n, 3 * p + q, at] = term
                else:
                    kgrad[n, 3 * p + q, at] += term

    def add_tasks(n, u):
        return [functools.partial(add_task, n, u, row) for row in range(0, C, 16)]

    def bias_copies():
        if plan.n_outs == 1:
            return []
        blocks = 9 * C // plan.block_rows // plan.n_outs
        return [
            pltpu.make_async_copy(bias_rows, out.at[i, pl.ds(plan.block_rows, 8)], bias_sem)
            for out in outs
            for i in range(blocks)
        ]

    steps = [(n, u) for n in range(chunks) for u in range(5)]
    y_copy(0).start()
    for u in range(5):
        for copy in v_copies(u):
            copy.start()
    for n in range(1, chunks):
        y_copy(n).start()
    for copy in bias_copies():
        copy.start()
    y_copy(0).wait()
    run_all(cell_tasks(plan, yb.at[0], wh.at[0], wl.at[0], 0))
    for s, (n, u) in enumerate(steps):
        for copy in w_copies(s):
            copy.start()
        tasks = []
        if n == 0:
            for copy in v_copies(u):
                copy.wait()
        if s > 0:
            tasks += add_tasks(*steps[s - 1])
        if s + 1 < len(steps):
            if s >= 2:
                for copy in w_copies(s - 2):
                    copy.wait()
            next_n, next_u = steps[s + 1]
            if next_u == 0:
                y_copy(next_n).wait()
            tasks += cell_tasks(plan, yb.at[next_n], wh.at[(s + 1) % 3], wl.at[(s + 1) % 3], next_u)

        def put(v, value, s=s):
            dbuf[s % 2, v] = value

        def rights(v, s=s):
            return tuple(part[s % 3, v].reshape(T * R, N) for part in (wh, wl))

        interleave(dot_tasks(lambda v: (vh[u, v], vl[u, v]), rights, TN, put), tasks)
        if n > 0 and u == 0:
            start_grad_store(plan, tab, kgrad.at[n - 1], outs, out_sem.at[n - 1], (n - 1) * N, N)
    run_all(add_tasks(*steps[-1]))
    n = chunks - 1
    start_grad_store(plan, tab, kgrad.at[n], outs, out_sem.at[n], n * N, N)
    for s in range(max(0, len(steps) - 3), len(steps)):
        for copy in w_copies(s):
            copy.wait()
    for copy in bias_copies():
        copy.wait()
    for n in range(chunks):
        wait_for(kgrad.at[n], out_sem.at[n])


SMEM_SPEC = pl.BlockSpec(memory_space=pltpu.SMEM)
VMEM_SPEC = pl.BlockSpec(memory_space=pltpu.VMEM)
ANY_SPEC = pl.BlockSpec(memory_space=pl.ANY)


def plane_shape(plan):
    return jax.ShapeDtypeStruct((3, 3 * plan.T, plan.R, plan.C), F32)


def point_scratch(plan, width):
    shape = (5, 5, plan.T, plan.R, width)
    return [pltpu.VMEM(shape, BF16), pltpu.VMEM(shape, BF16)]


def call(kernel, outs, in_specs, out_specs, scratch, flops, args, name):
    moved = sum(a.size * a.dtype.itemsize for a in args) + sum(o.size * 4 for o in outs)
    return pl.pallas_call(
        kernel,
        out_shape=outs,
        in_specs=in_specs,
        out_specs=out_specs,
        scratch_shapes=scratch,
        compiler_params=pltpu.CompilerParams(vmem_limit_bytes=VMEM_LIMIT),
        cost_estimate=pl.CostEstimate(flops=flops, bytes_accessed=moved, transcendentals=0),
        name=name,
    )(*args)


def pass_flops(plan):
    return 2 * 3 * 25 * plan.T * plan.R * plan.C * plan.C


def point_shape(plan):
    return jax.ShapeDtypeStruct((2, 5, 5, plan.T, plan.R, plan.C), BF16)


def run_forward(plan, tab, mask, bias, x, cot, pieces, name):
    last = cot is not None
    C, N, R, T = plan.C, plan.N, plan.R, plan.T
    cols = 3 * T
    chunks = C // N
    outs = [plane_shape(plan), plane_shape(plan), point_shape(plan)]
    out_specs = [ANY_SPEC, ANY_SPEC, ANY_SPEC]
    scratch = [
        pltpu.VMEM((5, cols, R, C), F32),
        *point_scratch(plan, C),
        pltpu.VMEM((chunks, 9, C, N), F32),
        pltpu.VMEM((2, 5, C, N), BF16),
        pltpu.VMEM((2, 5, C, N), BF16),
        pltpu.VMEM((2, 5, T, R, N), F32),
        pltpu.VMEM((chunks, 5, cols, R, N), F32),
        pltpu.VMEM((chunks, cols, R, N), F32),
        pltpu.SemaphoreType.DMA((C // LANES,)),
        pltpu.SemaphoreType.DMA((chunks,)),
        pltpu.SemaphoreType.DMA((chunks, 3)),
        pltpu.SemaphoreType.DMA((2, 5)),
    ]
    args = [tab, mask, bias, x]
    if last:
        outs.append(jax.ShapeDtypeStruct((1, C), F32))
        out_specs.append(VMEM_SPEC)
        scratch += [pltpu.VMEM((3, cols, R, N), F32), pltpu.VMEM((16, C), F32), pltpu.SemaphoreType.DMA]
        args.append(cot)
    args += pieces
    in_specs = [SMEM_SPEC, VMEM_SPEC, VMEM_SPEC] + [ANY_SPEC] * (len(args) - 3)
    kernel = functools.partial(forward_kernel, plan, last)
    return call(kernel, outs, in_specs, out_specs, scratch, pass_flops(plan), args, name)


def run_back(plan, tab, mask, points, slope, pieces, name):
    last = slope is None
    C, N, R, T = plan.C, plan.N, plan.R, plan.T
    cols = 3 * T
    chunks = C // N
    outs = [plane_shape(plan)]
    out_specs = [ANY_SPEC]
    scratch = [
        *point_scratch(plan, C),
        pltpu.VMEM((chunks, 9, N, C), F32),
        pltpu.VMEM((2, 5, N, C), BF16),
        pltpu.VMEM((2, 5, N, C), BF16),
        pltpu.VMEM((2, 5, T + 2, R, N), F32),
        pltpu.VMEM((chunks, 5, cols, R, N), F32),
        pltpu.SemaphoreType.DMA((2, 5)),
        pltpu.SemaphoreType.DMA((chunks,)),
        pltpu.SemaphoreType.DMA((chunks,)),
    ]
    args = [tab, mask, points]
    if not last:
        outs.append(jax.ShapeDtypeStruct((1, C), F32))
        out_specs.append(VMEM_SPEC)
        scratch += [pltpu.VMEM((3, cols, R, N), F32), pltpu.VMEM((R, C), F32), pltpu.SemaphoreType.DMA]
        args.append(slope)
    args += pieces
    in_specs = [SMEM_SPEC, VMEM_SPEC] + [ANY_SPEC] * (len(args) - 2)
    kernel = functools.partial(back_kernel, plan, last)
    return call(kernel, outs, in_specs, out_specs, scratch, pass_flops(plan), args, name)


def run_grad(plan, tab, bias_rows, points, y, name):
    C, N, R, T = plan.C, plan.N, plan.R, plan.T
    cols = 3 * T
    chunks = C // N
    blocks = 9 * C // plan.block_rows // plan.n_outs
    block = plan.block_rows + (8 if plan.n_outs == 2 else 0)
    outs = [jax.ShapeDtypeStruct((blocks, block, C), F32) for _ in range(plan.n_outs)]
    outs.append(point_shape(plan))
    scratch = [
        *point_scratch(plan, C),
        pltpu.VMEM((chunks, 3, cols, R, N), F32),
        pltpu.VMEM((3, 5, T, R, N), BF16),
        pltpu.VMEM((3, 5, T, R, N), BF16),
        pltpu.VMEM((2, 5, C, N), F32),
        pltpu.VMEM((chunks, 9, C, N), F32),
        pltpu.SemaphoreType.DMA((2, 5)),
        pltpu.SemaphoreType.DMA((chunks,)),
        pltpu.SemaphoreType.DMA((2, 3)),
        pltpu.SemaphoreType.DMA((chunks,)),
        pltpu.SemaphoreType.DMA,
    ]
    in_specs = [SMEM_SPEC, VMEM_SPEC, ANY_SPEC, ANY_SPEC]
    kernel = functools.partial(grad_kernel, plan)
    return call(kernel, outs, in_specs, [ANY_SPEC] * len(outs), scratch, pass_flops(plan), [tab, bias_rows, points, y], name)


def to_planes(plan, cells):
    slots, side, _, channels = cells.shape
    tiled = cells.reshape(slots, plan.T, 3, side, channels).transpose(2, 3, 0, 1, 4)
    flat = tiled.reshape(3, side, slots * plan.T, channels)
    return jnp.pad(flat, ((0, 0), (0, 0), (0, plan.R - slots * plan.T), (0, 0)))


def from_planes(plan, planes, slots):
    side = 3 * plan.T
    kept = planes[:, :, : slots * plan.T].reshape(3, side, slots, plan.T, planes.shape[3])
    return kept.transpose(2, 3, 0, 1, 4).reshape(slots, side, side, planes.shape[3])


def tie(*values):
    return lax.optimization_barrier(values)


class Net:
    def __init__(self):
        self.rep = lax.axis_size("rep")
        self.dp = lax.axis_size("dp")
        self.routed = self.rep == 4 and self.dp == 8
        self.n_pieces = 4 if self.routed else 1
        self.n_outs = 2 if self.routed else 1

    def perm(self, move):
        pairs = []
        for x in range(2):
            for c in range(2):
                for z in range(4):
                    for y in range(2):
                        to = move(x, c, z, y)
                        pairs.append((((x * 2 + c) * 4 + z) * 2 + y, ((to[0] * 2 + to[1]) * 4 + to[2]) * 2 + to[3]))
        return pairs

    def send(self, value, move):
        return lax.ppermute(value, AXES, self.perm(move))

    def over_core(self, value):
        return self.send(value, lambda x, c, z, y: (x, 1 - c, z, y))

    def over_first(self, value):
        return self.send(value, lambda x, c, z, y: (x, c, z, 1 - y) if c == 0 else (1 - x, c, z, y))

    def over_second(self, value):
        return self.send(value, lambda x, c, z, y: (1 - x, c, z, y) if c == 0 else (x, c, z, 1 - y))

    def over_z(self, value, step):
        return self.send(value, lambda x, c, z, y: (x, c, (z + step) % 4, y))

    def tables(self):
        if not self.routed:
            return jnp.zeros((4, 8), jnp.int32)
        rep = lax.axis_index("rep")
        dp = lax.axis_index("dp")
        x, c, z, y = rep // 2, rep % 2, dp // 2, dp % 2
        block = jnp.arange(32, dtype=jnp.int32)
        bx, bc, bz, by = block // 16, block // 8 % 2, block // 2 % 4, block % 2
        dx, dy = bx ^ x, by ^ y
        second = jnp.where(bc == 0, dx, dy)
        first = jnp.where(bc == 0, dy, dx)
        other = (bc != c).astype(jnp.int32)
        return jnp.stack(
            [2 * other + second, 4 * first + (z - bz) % 4, other, 8 * second + 4 * first + (bz - z) % 4]
        ).astype(jnp.int32)

    def gather_z(self, shard):
        return jnp.stack([shard] + [self.over_z(shard, step) for step in (1, 2, 3)])

    def gather_whole(self, shard):
        return [lax.all_gather(shard, AXES, axis=0, tiled=True)[None]]

    def sum_whole(self, parts):
        return lax.psum_scatter(parts[0][0], AXES, scatter_dimension=0, tiled=True)

    def send_z(self, four):
        return [four[0]] + [self.over_z(four[step], step) for step in (1, 2, 3)]


def body(
    features, map_size, item_count, conv4_weight, conv4_bias, conv5_weight, conv5_bias, cotangent
):
    slots, side, _, channels = features.shape
    net = Net()
    tiles = side // 3
    rows = -(-slots * tiles // 16) * 16
    shard_rows = conv4_weight.shape[0] // channels
    block_rows = shard_rows if net.routed else 9 * channels
    plan = Plan(channels, rows, tiles, block_rows, net.n_pieces, net.n_outs)

    live = jnp.arange(slots, dtype=jnp.int32) < item_count[0]
    inside = jnp.arange(side, dtype=jnp.int32)[None, :] < map_size[:, None]
    valid = live[:, None, None] & inside[:, :, None] & inside[:, None, :]
    mask = to_planes(plan, jnp.broadcast_to(valid.astype(F32)[..., None], (slots, side, side, LANES)))
    source = to_planes(plan, features * valid.astype(F32)[..., None])
    cot = to_planes(plan, cotangent)
    tab = net.tables()

    shard4 = conv4_weight.reshape(shard_rows, channels)
    shard5 = conv5_weight.reshape(shard_rows, channels)
    if net.routed:
        four4 = net.gather_z(shard4)
        shard5, four4 = tie(shard5, four4)
        four5 = net.gather_z(shard5)
        eight4 = jnp.concatenate([four4, net.over_first(four4)])
        far4 = net.over_second(eight4)
        four5, far4, eight4 = tie(four5, far4, eight4)
        pieces4 = [eight4, far4, net.over_core(eight4), net.over_core(far4)]
        eight5 = jnp.concatenate([four5, net.over_first(four5)])
        eight5, source = tie(eight5, source)
        far5 = net.over_second(eight5)
        near5 = net.over_core(eight5)
    else:
        pieces4 = net.gather_whole(shard4)
        pieces5 = net.gather_whole(shard5)
    hidden, slope4, points4 = run_forward(plan, tab, mask, conv4_bias[None], source, None, pieces4, "conv4")
    if net.routed:
        far5, near5, hidden = tie(far5, near5, hidden)
        pieces5 = [eight5, far5, near5, net.over_core(far5)]
    out5, back5, points5, bias5 = run_forward(plan, tab, mask, conv5_bias[None], hidden, cot, pieces5, "conv5")
    *grad5, cells5 = run_grad(plan, tab, jnp.pad(bias5, ((0, 7), (0, 0))), points5, back5, "grad5")
    if net.routed:
        got = net.over_core(grad5[1])
        keep5, send5 = grad5[0][:8] + got[:8], grad5[0][8:] + got[8:]
        keep5, send5, cells5 = tie(keep5, send5, cells5)
        got5 = net.over_second(send5)
    back4, bias4 = run_back(plan, tab, mask, cells5, slope4, pieces5, "back5")
    if net.routed:
        got5, back4 = tie(got5, back4)
        keep5, send5 = keep5[:4] + got5[:4], keep5[4:] + got5[4:]
        keep5, send5, back4 = tie(keep5, send5, back4)
        got5 = net.over_first(send5)
    *grad4, cells4 = run_grad(plan, tab, jnp.pad(bias4, ((0, 7), (0, 0))), points4, back4, "grad4")
    if net.routed:
        got5, *grad4 = tie(got5, *grad4)
        got = net.over_core(grad4[1])
        keep4, send4 = grad4[0][:8] + got[:8], grad4[0][8:] + got[8:]
        four5 = keep5 + got5
        keep4, send4, four5, cells4 = tie(keep4, send4, four5, cells4)
        got5 = net.send_z(four5)
        got4 = net.over_second(send4)
    input_grad = run_back(plan, tab, mask, cells4, None, pieces4, "back4")[0]
    if net.routed:
        got4, input_grad, *got5 = tie(got4, input_grad, *got5)
        keep4, send4 = keep4[:4] + got4[:4], keep4[4:] + got4[4:]
        sum4 = sum(net.send_z(keep4 + net.over_first(send4)))
        sum5 = sum(got5)
        share4, total4 = sum4[:shard_rows], sum4[shard_rows]
        share5, total5 = sum5[:shard_rows], sum5[shard_rows]
    else:
        share5 = net.sum_whole(grad5)
        share4 = net.sum_whole(grad4)
        total4, total5 = lax.psum((bias4[0], bias5[0]), AXES)

    total_cells = slots * net.rep * net.dp * side * side
    scale = float(total_cells) ** (-0.5)
    return (
        from_planes(plan, out5, slots),
        from_planes(plan, input_grad, slots),
        (share4 * scale).reshape(-1),
        total4 * scale,
        (share5 * scale).reshape(-1),
        total5 * scale,
    )


def solution(mesh):
    placed = (
        P(AXES, None, None, None),
        P(AXES),
        P(AXES),
        P(AXES),
        P(),
        P(AXES),
        P(),
        P(AXES, None, None, None),
    )
    return jax.shard_map(
        body,
        mesh=mesh,
        in_specs=placed,
        out_specs=(
            P(AXES, None, None, None),
            P(AXES, None, None, None),
            P(AXES),
            P(),
            P(AXES),
            P(),
        ),
        check_vma=False,
    )
```

time: 521 us -> 380 us (0.73)
  waiting for transfers between devices: 176 us -> 114 us
  Pallas kernels: 226 us -> 166 us
  starting transfers between devices: 52.1 us -> 31.9 us
  other arithmetic: 14 us -> 25.9 us
  local copies, waits for them, and re-layouts: 42.8 us -> 34 us
    ppermute x32 -> x26, waiting for transfers between devices: 176 us -> 114 us  [send(): return lax.ppermute(value, AXES, self.perm(move))]
    pallas_call x6, Pallas kernels: 226 us -> 166 us  [call(): pl.pallas_call(kernel, out_shape=outs, in_specs=in_specs, out_specs=out_s...]
    ppermute x32 -> x26, starting transfers between devices: 52.1 us -> 31.9 us  [send(): return lax.ppermute(value, AXES, self.perm(move))]
    add x9 -> x8, other arithmetic: 8.95 us -> 21.5 us  [the longest x1 6.11 us: body(): keep4, send4 = (grad4[0][:8] + got[:8], grad4[0][8:] + got[8:])]
    unnamed x38 -> x17, local copies, waits for them, and re-layouts: 9.94 us -> 1.69 us
  transfers between devices with their start and end apart: 32 -> 26, of which waited for: 14 -> 15; matrix products, arithmetic and copies ran while one was open for 10% -> 10% of each run, Pallas kernels for 22% -> 28%
where the time goes in v2:
time: 380 us; the launch traced here: 374 us
  Pallas kernels  166 us (44%)
  waiting for transfers between devices  114 us (30%)
  local copies, waits for them, and re-layouts  34 us (9%)
  starting transfers between devices  31.9 us (8%)
  other arithmetic  25.9 us (7%)
    pallas_call x6, Pallas kernels, call(): pl.pallas_call(kernel, out_shape=outs, in_specs=in_specs, out_specs=out_s...  166 us
    ppermute x26, waiting for transfers between devices, send(): return lax.ppermute(value, AXES, self.perm(move))  114 us
    ppermute x26, starting transfers between devices, send(): return lax.ppermute(value, AXES, self.perm(move))  31.9 us
    transpose x2, local copies, waits for them, and re-layouts, from_planes(): kept.transpose(2, 3, 0, 1, 4).reshape(slots, side, side, planes.shape[3])  11.4 us
  transfers between devices with their start and end apart: 26, of which 15 were waited for; matrix products, arithmetic and copies ran while one was open for 10% of the time, Pallas kernels for 28%

profile of v2, /device:TPU:0, one launch (start us, length us, event | category | flops | bytes accessed | tf_op | source)
XLA Modules:
  0.0 373.8 jit_solution(17541991090890706287)
XLA Ops:
  1.6 5.1 %collective-permute-start.2 = (f32[144,512]{1,0:T(8,128)S(1)}, f32[144,512]{1,0:T(8,128)S(1)}, u32[]{:S(2)}, u32[]{:S(2)}) collective-permute-start(f32[144,512]{1,0:T(8,128)S(1)} %reshape.418), channel_id=1, source_target_pairs={{0,6},{1,7},{2,0},{3,1},{4,2},{5,3},{6,4},{7,5},{8,14},{9,15},{10,... | collective-permute-start | bytes 884744 | tf_op jit(solution)/shard_map/ppermute | solution.py:811
  9.8 4.4 %collective-permute-done.2 = f32[144,512]{1,0:T(8,128)S(1)} collective-permute-done((f32[144,512]{1,0:T(8,128)S(1)}, f32[144,512]{1,0:T(8,128)S(1)}, u32[]{:S(2)}, u32[]{:S(2)}) %collective-permute-start.2) | collective-permute-done | bytes 294944 | tf_op jit(solution)/shard_map/ppermute | solution.py:811
  14.2 17.7 %collective-permute-done.1 = f32[144,512]{1,0:T(8,128)S(1)} collective-permute-done((f32[144,512]{1,0:T(8,128)S(1)}, f32[144,512]{1,0:T(8,128)S(1)}, u32[]{:S(2)}, u32[]{:S(2)}) %collective-permute-start.1) | collective-permute-done | bytes 294944 | tf_op jit(solution)/shard_map/ppermute | solution.py:811
  33.7 14.6 %collective-permute-done.6 = f32[4,144,512]{2,1,0:T(8,128)S(1)} collective-permute-done((f32[4,144,512]{2,1,0:T(8,128)S(1)}, f32[4,144,512]{2,1,0:T(8,128)S(1)}, u32[]{:S(2)}, u32[]{:S(2)}) %collective-permute-start.6) | collective-permute-done | bytes 1179680 | tf_op jit(solution)/shard_map/ppermute | solution.py:811
  57.4 19.5 %collective-permute-done.4 = f32[144,512]{1,0:T(8,128)S(1)} collective-permute-done((f32[144,512]{1,0:T(8,128)S(1)}, f32[144,512]{1,0:T(8,128)S(1)}, u32[]{:S(2)}, u32[]{:S(2)}) %collective-permute-start.4) | collective-permute-done | bytes 294944 | tf_op jit(solution)/shard_map/ppermute | solution.py:811
  83.1 3.0 pad.19.refs_0_
  86.1 7.4 %collective-permute-done.8 = f32[4,144,512]{2,1,0:T(8,128)S(1)} collective-permute-done((f32[4,144,512]{2,1,0:T(8,128)S(1)}, f32[4,144,512]{2,1,0:T(8,128)S(1)}, u32[]{:S(2)}, u32[]{:S(2)}) %collective-permute-start.8) | collective-permute-done | bytes 1179680 | tf_op jit(solution)/shard_map/ppermute | solution.py:811
  99.4 28.2 %conv4.1 = (f32[3,15,48,512]{3,2,1,0:T(8,128)}, f32[3,15,48,512]{3,2,1,0:T(8,128)}, bf16[2,5,5,5,48,512]{5,4,3,2,1,0:T(8,128)(2,1)}) custom-call(s32[4,32]{1,0:T(4,128)} %pad_add_fusion.tab, f32[3,15,48,128]{3,2,1,0:T(8,128)} %pad.18.mask, f32[1,512]{1,0:T(1,128)} %bitcast.86, f32[3,15,48,512]{3,2,1,0:T(8,128)} %pad.19.refs_0_, f32[8,144,512]{2,1,0:T(8,128)} %copy-done.2, ...), custom_call_target="tpu_custom_call" | custom-call | flops 9437184000 | bytes 48392704 | tf_op jit(solution)/shard_map/conv4/pallas_call | solution.py:666
  127.9 4.7 %copy.28 = f32[3,15,45,512]{3,2,1,0:T(8,128)S(1)} copy(f32[3,15,45,512]{3,1,0,2:T(8,128)} %bitcast.67) | data formatting | bytes 8294400 | tf_op jit(solution)/shard_map/reshape | solution.py:778
  135.6 32.9 %conv5.1 = (f32[3,15,48,512]{3,2,1,0:T(8,128)}, f32[3,15,48,512]{3,2,1,0:T(8,128)}, bf16[2,5,5,5,48,512]{5,4,3,2,1,0:T(8,128)(2,1)}, f32[1,512]{1,0:T(1,128)}) custom-call(s32[4,32]{1,0:T(4,128)} %pad_add_fusion.tab, f32[3,15,48,128]{3,2,1,0:T(8,128)} %pad.18.mask, f32[1,512]{1,0:T(1,128)} %bitcast.87, f32[3,15,48,512]{3,2,1,0:T(8,128)} %get-tuple-element.60.refs_0_, ...), custom_call_target="tpu_custom_call" | custom-call | flops 9437184000 | bytes 52818432 | tf_op jit(solution)/shard_map/conv5/pallas_call | solution.py:666
  169.8 27.6 %grad5.1 = (f32[16,152,512]{2,1,0:T(8,128)}, f32[16,152,512]{2,1,0:T(8,128)}, bf16[2,5,5,5,48,512]{5,4,3,2,1,0:T(8,128)(2,1)}) custom-call(s32[4,32]{1,0:T(4,128)} %pad_add_fusion.tab, f32[8,512]{1,0:T(8,128)} %pad.21.bias_rows, bf16[2,5,5,5,48,512]{5,4,3,2,1,0:T(8,128)(2,1)} %get-tuple-element.65.v_hbm, f32[3,15,48,512]{3,2,1,0:T(8,128)} %get-tuple-element.66.y_hbm), custom_call_target="tpu_custom_call" | custom-call | flops 9437184000 | bytes 51266048 | tf_op jit(solution)/shard_map/grad5/pallas_call | solution.py:666
  197.7 8.2 %collective-permute-done.14 = f32[16,152,512]{2,1,0:T(8,128)S(1)} collective-permute-done((f32[16,152,512]{2,1,0:T(8,128)}, f32[16,152,512]{2,1,0:T(8,128)S(1)}, u32[]{:S(2)}, u32[]{:S(2)}) %collective-permute-start.14) | collective-permute-done | bytes 4980768 | tf_op jit(solution)/shard_map/ppermute | solution.py:811
  205.9 5.9 %slice_add_fusion.2 = (f32[8,152,512]{2,1,0:T(8,128)}, f32[8,152,512]{2,1,0:T(8,128)}) fusion(f32[16,152,512]{2,1,0:T(8,128)S(1)} %collective-permute-done.14, f32[16,152,512]{2,1,0:T(8,128)} %get-tuple-element.67), kind=kLoop, calls=%fused_computation.2 | loop fusion | flops 1245184 | bytes 14942208 | tf_op jit(solution)/shard_map/add | solution.py:898
  213.4 27.1 %back5.1 = (f32[3,15,48,512]{3,2,1,0:T(8,128)}, f32[1,512]{1,0:T(1,128)}) custom-call(s32[4,32]{1,0:T(4,128)} %pad_add_fusion.tab, f32[3,15,48,128]{3,2,1,0:T(8,128)} %pad.18.mask, bf16[2,5,5,5,48,512]{5,4,3,2,1,0:T(8,128)(2,1)} %get-tuple-element.72.refs_0_, f32[3,15,48,512]{3,2,1,0:T(8,128)} %get-tuple-element.73.refs_1_, ...), custom_call_target="tpu_custom_call" | custom-call | flops 9437184000 | bytes 31681024 | tf_op jit(solution)/shard_map/back5/pallas_call | solution.py:666
  242.5 4.0 %slice_add_fusion.5 = (f32[4,152,512]{2,1,0:T(8,128)}, f32[4,152,512]{2,1,0:T(8,128)S(1)}) fusion(f32[8,152,512]{2,1,0:T(8,128)} %collective-permute-done.15, f32[8,152,512]{2,1,0:T(8,128)} %get-tuple-element.70), kind=kLoop, calls=%fused_computation.8 | loop fusion | flops 622592 | bytes 7471104 | tf_op jit(solution)/shard_map/add | solution.py:904
  248.5 27.4 %grad4.1 = (f32[16,152,512]{2,1,0:T(8,128)}, f32[16,152,512]{2,1,0:T(8,128)}, bf16[2,5,5,5,48,512]{5,4,3,2,1,0:T(8,128)(2,1)}) custom-call(s32[4,32]{1,0:T(4,128)} %pad_add_fusion.tab, f32[8,512]{1,0:T(8,128)} %pad.22.bias_rows, bf16[2,5,5,5,48,512]{5,4,3,2,1,0:T(8,128)(2,1)} %get-tuple-element.79.v_hbm, f32[3,15,48,512]{3,2,1,0:T(8,128)} %get-tuple-element.80.y_hbm), custom_call_target="tpu_custom_call" | custom-call | flops 9437184000 | bytes 51266048 | tf_op jit(solution)/shard_map/grad4/pallas_call | solution.py:666
  277.6 6.9 %collective-permute-done.17 = f32[16,152,512]{2,1,0:T(8,128)S(1)} collective-permute-done((f32[16,152,512]{2,1,0:T(8,128)}, f32[16,152,512]{2,1,0:T(8,128)S(1)}, u32[]{:S(2)}, u32[]{:S(2)}) %collective-permute-start.17) | collective-permute-done | bytes 4980768 | tf_op jit(solution)/shard_map/ppermute | solution.py:811
  284.5 6.1 %slice_add_fusion = (f32[8,152,512]{2,1,0:T(8,128)}, f32[8,152,512]{2,1,0:T(8,128)}) fusion(f32[16,152,512]{2,1,0:T(8,128)S(1)} %collective-permute-done.17, f32[16,152,512]{2,1,0:T(8,128)} %get-tuple-element.83), kind=kLoop, calls=%fused_computation | loop fusion | flops 1245184 | bytes 14942208 | tf_op jit(solution)/shard_map/add | solution.py:911
  296.8 23.3 %back4.1 = f32[3,15,48,512]{3,2,1,0:T(8,128)} custom-call(s32[4,32]{1,0:T(4,128)} %pad_add_fusion.tab, f32[3,15,48,128]{3,2,1,0:T(8,128)} %pad.18.mask, bf16[2,5,5,5,48,512]{5,4,3,2,1,0:T(8,128)(2,1)} %get-tuple-element.89.refs_0_, f32[8,144,512]{2,1,0:T(8,128)} %copy-done.2, f32[8,144,512]{2,1,0:T(8,128)} %collective-permute-done.7.refs_2_, ...), custom_call_target="tpu_custom_call" | custom-call | flops 9437184000 | bytes 27255296 | tf_op jit(solution)/shard_map/back4/pallas_call | solution.py:666
  325.8 6.9 %copy.37 = f32[3,15,45,512]{3,1,0,2:T(8,128)} copy(f32[3,15,45,512]{3,2,1,0:T(8,128)} %bitcast.68) | data formatting | bytes 8294400 | tf_op jit(solution)/shard_map/transpose | solution.py:785
  332.9 8.5 %collective-permute-done.22 = f32[4,152,512]{2,1,0:T(8,128)S(1)} collective-permute-done((f32[4,152,512]{2,1,0:T(8,128)S(1)}, f32[4,152,512]{2,1,0:T(8,128)S(1)}, u32[]{:S(2)}, u32[]{:S(2)}) %collective-permute-start.22) | collective-permute-done | bytes 1245216 | tf_op jit(solution)/shard_map/ppermute | solution.py:811
  343.2 3.8 %collective-permute-start.25 = (f32[152,512]{1,0:T(8,128)S(1)}, f32[152,512]{1,0:T(8,128)S(1)}, u32[]{:S(2)}, u32[]{:S(2)}) collective-permute-start(f32[152,512]{1,0:T(8,128)S(1)} %get-tuple-element.105), channel_id=1, source_target_pairs={{0,6},{1,7},{2,0},{3,1},{4,2},{5,3},{6,4},{7,5},{8,14},{9,15},{10,... | collective-permute-start | bytes 933896 | tf_op jit(solution)/shard_map/ppermute | solution.py:811
  347.1 4.5 %copy.38 = f32[3,15,45,512]{3,1,0,2:T(8,128)} copy(f32[3,15,45,512]{3,2,1,0:T(8,128)S(1)} %bitcast.72) | data formatting | bytes 8294400 | tf_op jit(solution)/shard_map/transpose | solution.py:785
  357.8 14.3 %collective-permute-done.24 = f32[152,512]{1,0:T(8,128)S(1)} collective-permute-done((f32[152,512]{1,0:T(8,128)S(1)}, f32[152,512]{1,0:T(8,128)S(1)}, u32[]{:S(2)}, u32[]{:S(2)}) %collective-permute-start.24) | collective-permute-done | bytes 311328 | tf_op jit(solution)/shard_map/ppermute | solution.py:811
  (95 shorter events, 59.9 us)
Async XLA Ops:
  1.6 12.6 %collective-permute-start.2 = (f32[144,512]{1,0:T(8,128)S(1)}, f32[144,512]{1,0:T(8,128)S(1)}, u32[]{:S(2)}, u32[]{:S(2)}) collective-permute-start(f32[144,512]{1,0:T(8,128)S(1)} %reshape.418), channel_id=1, source_target_pairs={{0,6},{1,7},{2,0},{3,1},{4,2},{5,3},{6,4},{7,5},{8,14},{9,15},{10,... | collective-permute-start | bytes 884744 | tf_op jit(solution)/shard_map/ppermute | solution.py:811
  6.8 25.1 %collective-permute-start.1 = (f32[144,512]{1,0:T(8,128)S(1)}, f32[144,512]{1,0:T(8,128)S(1)}, u32[]{:S(2)}, u32[]{:S(2)}) collective-permute-start(f32[144,512]{1,0:T(8,128)S(1)} %reshape.418), channel_id=1, source_target_pairs={{0,4},{1,5},{2,6},{3,7},{4,0},{5,1},{6,2},{7,3},{8,12},{9,13},{10,... | collective-permute-start | bytes 884744 | tf_op jit(solution)/shard_map/ppermute | solution.py:811
  6.8 25.1 %collective-permute-start = (f32[144,512]{1,0:T(8,128)S(1)}, f32[144,512]{1,0:T(8,128)S(1)}, u32[]{:S(2)}, u32[]{:S(2)}) collective-permute-start(f32[144,512]{1,0:T(8,128)S(1)} %reshape.418), channel_id=1, source_target_pairs={{0,2},{1,3},{2,4},{3,5},{4,6},{5,7},{6,0},{7,1},{8,10},{9,11},{10,... | collective-permute-start | bytes 884744 | tf_op jit(solution)/shard_map/ppermute | solution.py:811
  32.0 16.3 %collective-permute-start.6 = (f32[4,144,512]{2,1,0:T(8,128)S(1)}, f32[4,144,512]{2,1,0:T(8,128)S(1)}, u32[]{:S(2)}, u32[]{:S(2)}) collective-permute-start(f32[4,144,512]{2,1,0:T(8,128)S(1)} %pad_maximum_fusion.1), channel_id=1, source_target_pairs={{0,1},{1,0},{2,3},{3,2},{4,5},{5,4},{6,7},{7,6},{8,24},{9,25},{10,... | collective-permute-start | bytes 3538952 | tf_op jit(solution)/shard_map/ppermute | solution.py:811
  48.3 29.0 %collective-permute-start.7 = (f32[8,144,512]{2,1,0:T(8,128)S(1)}, f32[8,144,512]{2,1,0:T(8,128)}, u32[]{:S(2)}, u32[]{:S(2)}) collective-permute-start(f32[8,144,512]{2,1,0:T(8,128)S(1)} %constant_dynamic-update-slice_fusion.refs_1_), channel_id=1, source_target_pairs={{0,16},{1,17},{2,18},{3,19},{4,20},{5,21},{6,22},{7,23},{8,9},{9,8... | collective-permute-start | bytes 7077896 | tf_op jit(solution)/shard_map/ppermute | solution.py:811
  49.9 27.1 %collective-permute-start.4 = (f32[144,512]{1,0:T(8,128)S(1)}, f32[144,512]{1,0:T(8,128)S(1)}, u32[]{:S(2)}, u32[]{:S(2)}) collective-permute-start(f32[144,512]{1,0:T(8,128)S(1)} %reshape.417), channel_id=1, source_target_pairs={{0,4},{1,5},{2,6},{3,7},{4,0},{5,1},{6,2},{7,3},{8,12},{9,13},{10,... | collective-permute-start | bytes 884744 | tf_op jit(solution)/shard_map/ppermute | solution.py:811
  52.7 24.3 %collective-permute-start.3 = (f32[144,512]{1,0:T(8,128)S(1)}, f32[144,512]{1,0:T(8,128)S(1)}, u32[]{:S(2)}, u32[]{:S(2)}) collective-permute-start(f32[144,512]{1,0:T(8,128)S(1)} %reshape.417), channel_id=1, source_target_pairs={{0,2},{1,3},{2,4},{3,5},{4,6},{5,7},{6,0},{7,1},{8,10},{9,11},{10,... | collective-permute-start | bytes 884744 | tf_op jit(solution)/shard_map/ppermute | solution.py:811
  77.3 16.2 %collective-permute-start.8 = (f32[4,144,512]{2,1,0:T(8,128)S(1)}, f32[4,144,512]{2,1,0:T(8,128)S(1)}, u32[]{:S(2)}, u32[]{:S(2)}) collective-permute-start(f32[4,144,512]{2,1,0:T(8,128)S(1)} %pad_maximum_fusion.2), channel_id=1, source_target_pairs={{0,1},{1,0},{2,3},{3,2},{4,5},{5,4},{6,7},{7,6},{8,24},{9,25},{10,... | collective-permute-start | bytes 3538952 | tf_op jit(solution)/shard_map/ppermute | solution.py:811
  79.5 19.8 %collective-permute-start.11 = (f32[8,144,512]{2,1,0:T(8,128)S(1)}, f32[8,144,512]{2,1,0:T(8,128)}, u32[]{:S(2)}, u32[]{:S(2)}) collective-permute-start(f32[8,144,512]{2,1,0:T(8,128)S(1)} %constant_dynamic-update-slice_fusion.refs_1_), channel_id=1, source_target_pairs={{0,8},{1,9},{2,10},{3,11},{4,12},{5,13},{6,14},{7,15},{8,0},{9,1},... | collective-permute-start | bytes 7077896 | tf_op jit(solution)/shard_map/ppermute | solution.py:811
  79.6 19.8 %collective-permute-start.12 = (f32[8,144,512]{2,1,0:T(8,128)}, f32[8,144,512]{2,1,0:T(8,128)}, u32[]{:S(2)}, u32[]{:S(2)}) collective-permute-start(f32[8,144,512]{2,1,0:T(8,128)} %collective-permute-done.7.refs_2_), channel_id=1, source_target_pairs={{0,8},{1,9},{2,10},{3,11},{4,12},{5,13},{6,14},{7,15},{8,0},{9,1},... | collective-permute-start | bytes 7077896 | tf_op jit(solution)/shard_map/ppermute | solution.py:811
  95.2 32.4 %collective-permute-start.10 = (f32[8,144,512]{2,1,0:T(8,128)}, f32[8,144,512]{2,1,0:T(8,128)}, u32[]{:S(2)}, u32[]{:S(2)}) collective-permute-start(f32[8,144,512]{2,1,0:T(8,128)} %pad_maximum_fusion.refs_2_), channel_id=1, source_target_pairs={{0,8},{1,9},{2,10},{3,11},{4,12},{5,13},{6,14},{7,15},{8,0},{9,1},... | collective-permute-start | bytes 7077896 | tf_op jit(solution)/shard_map/ppermute | solution.py:811
  95.2 32.4 %collective-permute-start.9 = (f32[8,144,512]{2,1,0:T(8,128)}, f32[8,144,512]{2,1,0:T(8,128)}, u32[]{:S(2)}, u32[]{:S(2)}) collective-permute-start(f32[8,144,512]{2,1,0:T(8,128)} %pad_maximum_fusion.refs_2_), channel_id=1, source_target_pairs={{0,16},{1,17},{2,18},{3,19},{4,20},{5,21},{6,22},{7,23},{8,9},{9,8... | collective-permute-start | bytes 7077896 | tf_op jit(solution)/shard_map/ppermute | solution.py:811
  197.4 8.6 %collective-permute-start.14 = (f32[16,152,512]{2,1,0:T(8,128)}, f32[16,152,512]{2,1,0:T(8,128)S(1)}, u32[]{:S(2)}, u32[]{:S(2)}) collective-permute-start(f32[16,152,512]{2,1,0:T(8,128)} %get-tuple-element.68), channel_id=1, source_target_pairs={{0,8},{1,9},{2,10},{3,11},{4,12},{5,13},{6,14},{7,15},{8,0},{9,1},... | collective-permute-start | bytes 14942216 | tf_op jit(solution)/shard_map/ppermute | solution.py:811
  211.9 30.6 %collective-permute-start.15 = (f32[8,152,512]{2,1,0:T(8,128)}, f32[8,152,512]{2,1,0:T(8,128)}, u32[]{:S(2)}, u32[]{:S(2)}) collective-permute-start(f32[8,152,512]{2,1,0:T(8,128)} %get-tuple-element.71), channel_id=1, source_target_pairs={{0,16},{1,17},{2,18},{3,19},{4,20},{5,21},{6,22},{7,23},{8,9},{9,8... | collective-permute-start | bytes 7471112 | tf_op jit(solution)/shard_map/ppermute | solution.py:811
  246.5 29.4 %collective-permute-start.16 = (f32[4,152,512]{2,1,0:T(8,128)}, f32[4,152,512]{2,1,0:T(8,128)}, u32[]{:S(2)}, u32[]{:S(2)}) collective-permute-start(f32[4,152,512]{2,1,0:T(8,128)} %get-tuple-element.77), channel_id=1, source_target_pairs={{0,1},{1,0},{2,3},{3,2},{4,5},{5,4},{6,7},{7,6},{8,24},{9,25},{10,... | collective-permute-start | bytes 3735560 | tf_op jit(solution)/shard_map/ppermute | solution.py:811
  275.9 8.6 %collective-permute-start.17 = (f32[16,152,512]{2,1,0:T(8,128)}, f32[16,152,512]{2,1,0:T(8,128)S(1)}, u32[]{:S(2)}, u32[]{:S(2)}) collective-permute-start(f32[16,152,512]{2,1,0:T(8,128)} %get-tuple-element.84), channel_id=1, source_target_pairs={{0,8},{1,9},{2,10},{3,11},{4,12},{5,13},{6,14},{7,15},{8,0},{9,1},... | collective-permute-start | bytes 14942216 | tf_op jit(solution)/shard_map/ppermute | solution.py:811
  290.6 31.9 %collective-permute-start.18 = (f32[8,152,512]{2,1,0:T(8,128)}, f32[8,152,512]{2,1,0:T(8,128)}, u32[]{:S(2)}, u32[]{:S(2)}) collective-permute-start(f32[8,152,512]{2,1,0:T(8,128)} %get-tuple-element.88), channel_id=1, source_target_pairs={{0,16},{1,17},{2,18},{3,19},{4,20},{5,21},{6,22},{7,23},{8,9},{9,8... | collective-permute-start | bytes 7471112 | tf_op jit(solution)/shard_map/ppermute | solution.py:811
  292.0 28.1 %collective-permute-start.21 = (f32[152,512]{1,0:T(8,128)}, f32[152,512]{1,0:T(8,128)S(1)}, u32[]{:S(2)}, u32[]{:S(2)}) collective-permute-start(f32[152,512]{1,0:T(8,128)} %get-tuple-element.107), channel_id=1, source_target_pairs={{0,6},{1,7},{2,0},{3,1},{4,2},{5,3},{6,4},{7,5},{8,14},{9,15},{10,... | collective-permute-start | bytes 933896 | tf_op jit(solution)/shard_map/ppermute | solution.py:811
  292.0 30.5 %collective-permute-start.20 = (f32[152,512]{1,0:T(8,128)S(1)}, f32[152,512]{1,0:T(8,128)S(1)}, u32[]{:S(2)}, u32[]{:S(2)}) collective-permute-start(f32[152,512]{1,0:T(8,128)S(1)} %get-tuple-element.108), channel_id=1, source_target_pairs={{0,4},{1,5},{2,6},{3,7},{4,0},{5,1},{6,2},{7,3},{8,12},{9,13},{10,... | collective-permute-start | bytes 933896 | tf_op jit(solution)/shard_map/ppermute | solution.py:811
  294.7 27.7 %collective-permute-start.19 = (f32[152,512]{1,0:T(8,128)S(1)}, f32[152,512]{1,0:T(8,128)S(1)}, u32[]{:S(2)}, u32[]{:S(2)}) collective-permute-start(f32[152,512]{1,0:T(8,128)S(1)} %get-tuple-element.109), channel_id=1, source_target_pairs={{0,2},{1,3},{2,4},{3,5},{4,6},{5,7},{6,0},{7,1},{8,10},{9,11},{10,... | collective-permute-start | bytes 933896 | tf_op jit(solution)/shard_map/ppermute | solution.py:811
  324.4 17.0 %collective-permute-start.22 = (f32[4,152,512]{2,1,0:T(8,128)S(1)}, f32[4,152,512]{2,1,0:T(8,128)S(1)}, u32[]{:S(2)}, u32[]{:S(2)}) collective-permute-start(f32[4,152,512]{2,1,0:T(8,128)S(1)} %slice_add_fusion.4), channel_id=1, source_target_pairs={{0,1},{1,0},{2,3},{3,2},{4,5},{5,4},{6,7},{7,6},{8,24},{9,25},{10,... | collective-permute-start | bytes 3735560 | tf_op jit(solution)/shard_map/ppermute | solution.py:811
  343.2 12.2 %collective-permute-start.23 = (f32[152,512]{1,0:T(8,128)S(1)}, f32[152,512]{1,0:T(8,128)S(1)}, u32[]{:S(2)}, u32[]{:S(2)}) collective-permute-start(f32[152,512]{1,0:T(8,128)S(1)} %get-tuple-element.104), channel_id=1, source_target_pairs={{0,2},{1,3},{2,4},{3,5},{4,6},{5,7},{6,0},{7,1},{8,10},{9,11},{10,... | collective-permute-start | bytes 933896 | tf_op jit(solution)/shard_map/ppermute | solution.py:811
  343.2 14.6 %collective-permute-start.25 = (f32[152,512]{1,0:T(8,128)S(1)}, f32[152,512]{1,0:T(8,128)S(1)}, u32[]{:S(2)}, u32[]{:S(2)}) collective-permute-start(f32[152,512]{1,0:T(8,128)S(1)} %get-tuple-element.105), channel_id=1, source_target_pairs={{0,6},{1,7},{2,0},{3,1},{4,2},{5,3},{6,4},{7,5},{8,14},{9,15},{10,... | collective-permute-start | bytes 933896 | tf_op jit(solution)/shard_map/ppermute | solution.py:811
  347.0 25.1 %collective-permute-start.24 = (f32[152,512]{1,0:T(8,128)S(1)}, f32[152,512]{1,0:T(8,128)S(1)}, u32[]{:S(2)}, u32[]{:S(2)}) collective-permute-start(f32[152,512]{1,0:T(8,128)S(1)} %get-tuple-element.106), channel_id=1, source_target_pairs={{0,4},{1,5},{2,6},{3,7},{4,0},{5,1},{6,2},{7,3},{8,12},{9,13},{10,... | collective-permute-start | bytes 933896 | tf_op jit(solution)/shard_map/ppermute | solution.py:811
  (9 other events, 197.5 us)

commit v3 on v2

v3 whole, which is shorter than its diff:
```python
import functools

import jax
import jax.numpy as jnp
from jax import lax
from jax.experimental import pallas as pl
from jax.experimental.pallas import tpu as pltpu
from jax.sharding import PartitionSpec as P

AXES = ("rep", "dp")
F32 = jnp.float32
BF16 = jnp.bfloat16
LANES = 128
VMEM_LIMIT = 62 * 2**20
NN = (((1,), (0,)), ((), ()))
NT = (((1,), (1,)), ((), ()))
TN = (((0,), (0,)), ((), ()))
GELU_K = 0.7978845608028654
GELU_C = 0.044715


def patch_to_points(p0, p1, p2, p3, p4):
    d = p3 - p1
    return (
        (p0 - p2) + 0.5 * d,
        p1 + 0.5 * (p2 - p3),
        0.5 * p2 - (1.0 / 6.0) * (p1 + p1 + p3),
        (1.0 / 6.0) * d,
        (p4 - p2) - 2.0 * d,
    )


def points_to_patch(n0, n1, n2, n3, n4):
    e = 0.5 * n0 - 2.0 * n4
    f = (1.0 / 6.0) * n3
    g = (1.0 / 6.0) * n2
    return (
        (n1 - e) - (g + g + f),
        0.5 * (n1 + n2) - (n0 + n4),
        (e - 0.5 * n1) + (f - g),
    )


def taps_to_points(k0, k1, k2):
    s = k0 + k2
    return (k0, s + k1, s - k1, k0 + 2.0 * (k1 + 2.0 * k2), k2)


def taps_to_point(index, k0, k1, k2, at):
    if index == 0:
        return k0[at]
    if index == 1:
        return (k0[at] + k2[at]) + k1[at]
    if index == 2:
        return (k0[at] + k2[at]) - k1[at]
    if index == 3:
        return k0[at] + 2.0 * (k1[at] + 2.0 * k2[at])
    return k2[at]


POINT_TAPS = (((0, 1.0),), ((0, 1.0), (1, 1.0), (2, 1.0)), ((0, 1.0), (1, -1.0), (2, 1.0)), ((0, 1.0), (1, 2.0), (2, 4.0)), ((2, 1.0),))


def points_to_taps(d0, d1, d2, d3, d4):
    s = d1 + d2
    return (d0 + s + d3, (d1 - d2) + 2.0 * d3, s + 4.0 * d3 + d4)


def split(value):
    high = value.astype(BF16)
    return high, (value - high.astype(F32)).astype(BF16)


def dot3(left_high, left_low, right_high, right_low, dims):
    def dot(left, right):
        return lax.dot_general(left, right, dims, preferred_element_type=F32)

    return dot(left_high, right_high) + dot(left_low, right_high) + dot(left_high, right_low)


def gelu_parts(v):
    square = v * v
    half = 0.5 + 0.5 * jnp.tanh(v * (GELU_K + (GELU_K * GELU_C) * square))
    value = v * half
    return value, half + value * ((1.0 - half) * (2.0 * GELU_K + (6.0 * GELU_K * GELU_C) * square))


def segments(tap, start, rows, tap_rows, block_rows):
    cuts = []
    at = tap * tap_rows + start
    end = at + rows
    first = at
    while at < end:
        block = at // block_rows
        stop = min(end, (block + 1) * block_rows)
        cuts.append((block, at - block * block_rows, at - first, stop - at))
        at = stop
    return cuts


class Plan:
    def __init__(self, channels, rows, tiles, block_rows, n_pieces, n_outs):
        self.C = channels
        self.R = rows
        self.T = tiles
        self.block_rows = block_rows
        self.n_pieces = n_pieces
        self.n_outs = n_outs
        self.N = min(256, channels)


def for_each_cut(plan, tab, row, count, cut_block, act):
    if count == 1:
        act(0, 0)
        return
    which = tab[row, cut_block]
    index = tab[row + 1, cut_block]
    for ref in range(count):
        pl.when(which == ref)(functools.partial(act, ref, index))


def start_kernel_fetch(plan, tab, pieces, buf, sem, row_start, rows, col_start, cols):
    for first in range(0, len(pieces), plan.n_pieces):
        group = pieces[first : first + plan.n_pieces]
        width = group[0].shape[2]
        group_start = first // plan.n_pieces * width
        low = max(col_start, group_start)
        high = min(col_start + cols, group_start + width)
        if low >= high:
            continue
        for tap in range(9):
            for block, at, to, length in segments(tap, row_start, rows, plan.C, plan.block_rows):

                def act(ref, index, tap=tap, at=at, to=to, length=length):
                    pltpu.make_async_copy(
                        group[ref].at[index, pl.ds(at, length), pl.ds(low - group_start, high - low)],
                        buf.at[tap, pl.ds(to, length), pl.ds(low - col_start, high - low)],
                        sem,
                    ).start()

                for_each_cut(plan, tab, 0, plan.n_pieces, block, act)


def start_grad_store(plan, tab, buf, folded, outs, sem, col_start):
    N = plan.N
    for tap in range(9):
        for start in range(0, plan.C, N):
            for block, at, to, length in segments(tap, start, N, plan.C, plan.block_rows):
                if folded:
                    part = buf.at[tap, pl.ds(to, length), pl.ds(start, N)]
                else:
                    part = buf.at[tap, pl.ds(start + to, length)]

                def act(ref, index, part=part, at=at, length=length):
                    pltpu.make_async_copy(
                        part, outs[ref].at[index, pl.ds(at, length), pl.ds(col_start, N)], sem
                    ).start()

                for_each_cut(plan, tab, 2, plan.n_outs, block, act)


def wait_for(buf, sem):
    pltpu.make_async_copy(buf, buf, sem).wait()


def edge_masks(plan):
    place = lax.broadcasted_iota(jnp.int32, (plan.R, LANES), 0) % plan.T
    return (place != 0).astype(F32), (place != plan.T - 1).astype(F32)


def interleave(dots, tasks):
    done = 0
    for i, dot in enumerate(dots):
        dot()
        upto = len(tasks) * (i + 1) // len(dots)
        for task in tasks[done:upto]:
            task()
        done = upto


def run_all(tasks):
    for task in tasks:
        task()


def store_split(high_ref, low_ref, at, value):
    high, low = split(value)
    high_ref[at] = high
    low_ref[at] = low


def patch_tasks(plan, xp, vh, vl, u):
    T = plan.T

    def task(lane, rb):
        rows, at = pl.ds(rb, 16), pl.ds(lane, LANES)
        line = []
        for col in range(3 * T + 2):
            if col in (0, 3 * T + 1):
                line.append(jnp.zeros((16, LANES), F32))
            else:
                line.append(patch_to_point(u, [xp.at[k, col - 1] for k in range(5)], (rows, at)))
        for j in range(T):
            for v, value in enumerate(patch_to_points(*line[3 * j : 3 * j + 5])):
                store_split(vh, vl, (u, v, j, rows, at), value)

    return [functools.partial(task, lane, rb) for lane in range(0, plan.C, LANES) for rb in range(0, plan.R, 16)]


def patch_to_point(u, planes, at):
    if u == 0:
        return (planes[0][at] - planes[2][at]) + 0.5 * (planes[3][at] - planes[1][at])
    if u == 1:
        return planes[1][at] + 0.5 * (planes[2][at] - planes[3][at])
    if u == 2:
        p1 = planes[1][at]
        return 0.5 * planes[2][at] - (1.0 / 6.0) * (p1 + p1 + planes[3][at])
    if u == 3:
        return (1.0 / 6.0) * (planes[3][at] - planes[1][at])
    return (planes[4][at] - planes[2][at]) - 2.0 * (planes[3][at] - planes[1][at])


def cell_tasks(plan, planes, wh, wl, u):
    def task(lane, j, rb):
        rows, at = pl.ds(rb, 16), pl.ds(lane, LANES)
        line = [taps_to_point(u, *[plane.at[3 * j + b] for plane in planes], (rows, at)) for b in range(3)]
        for v, value in enumerate(taps_to_points(*line)):
            store_split(wh, wl, (v, j, rows, at), value)

    return [
        functools.partial(task, lane, j, rb)
        for lane in range(0, planes[0].shape[2], LANES)
        for j in range(plan.T)
        for rb in range(0, plan.R, 16)
    ]


def tap_tasks(kbuf, uh, ul, point):
    def task(row):
        at = pl.ds(row, 16)
        parts = [taps_to_point(point, kbuf.at[q], kbuf.at[3 + q], kbuf.at[6 + q], at) for q in range(3)]
        for v, value in enumerate(taps_to_points(*parts)):
            store_split(uh, ul, (v, at), value)

    return [functools.partial(task, row) for row in range(0, kbuf.shape[1], 16)]


def dot_tasks(lefts, rights, dims, put):
    def dot(v):
        left = tuple(part.reshape(part.shape[0] * part.shape[1], part.shape[2]) for part in lefts(v))
        put(v, dot3(*left, *rights(v), dims))

    return [functools.partial(dot, v) for v in range(5)]


class GradSteps:
    def __init__(self, plan, tab, vh, vl, planes_of, wh, wl, dbuf, grads, folded, outs, out_sem):
        self.plan, self.tab, self.vh, self.vl, self.planes_of = plan, tab, vh, vl, planes_of
        self.wh, self.wl, self.dbuf, self.grads, self.folded = wh, wl, dbuf, grads, folded
        self.outs, self.out_sem = outs, out_sem
        self.steps = [(n, u) for n in range(plan.C // plan.N) for u in range(5)]

    def cells(self, s):
        n, u = self.steps[s]
        return cell_tasks(self.plan, self.planes_of(n), self.wh.at[s % 2], self.wl.at[s % 2], u)

    def add(self, s, row):
        n, u = self.steps[s]
        plan, grad = self.plan, self.grads.at[n]
        taps = points_to_taps(*[self.dbuf[s % 2, v, pl.ds(row, 16)] for v in range(5)])
        if self.folded:
            place = (pl.ds(row % plan.N, 16), pl.ds(row // plan.N * plan.N, plan.N))
        else:
            place = (pl.ds(row, 16), slice(None))
        for k, weight in POINT_TAPS[u]:
            for q in range(3):
                term = taps[q] if weight == 1.0 else weight * taps[q]
                if u == 0 or (u == 1 and k > 0):
                    grad[(3 * k + q, *place)] = term
                else:
                    grad[(3 * k + q, *place)] += term

    def adds(self, s):
        return [functools.partial(self.add, s, row) for row in range(0, self.plan.C, 16)]

    def dots(self, s):
        n, u = self.steps[s]
        rows = self.plan.T * self.plan.R

        def put(v, value):
            self.dbuf[s % 2, v] = value

        def rights(v):
            return tuple(part[s % 2, v].reshape(rows, self.plan.N) for part in (self.wh, self.wl))

        return dot_tasks(lambda v: (self.vh[u, v], self.vl[u, v]), rights, TN, put)

    def store(self, n):
        start_grad_store(
            self.plan, self.tab, self.grads.at[n], self.folded, self.outs, self.out_sem.at[n], n * self.plan.N
        )

    def wait(self):
        for n in range(self.plan.C // self.plan.N):
            wait_for(self.grads.at[n], self.out_sem.at[n])


def bias_copies(plan, rows, outs, sem):
    if plan.n_outs == 1:
        return []
    return [
        pltpu.make_async_copy(rows, out.at[i, pl.ds(plan.block_rows, 8)], sem)
        for out in outs
        for i in range(out.shape[0])
    ]


def part_of(tasks, index, count):
    return tasks[len(tasks) * index // count : len(tasks) * (index + 1) // count]


def load_patches(plan, x_hbm, xp, x_sem, tasks):
    R = plan.R
    cols = 3 * plan.T
    not_first, not_last = edge_masks(plan)
    lanes = [pl.ds(lane, LANES) for lane in range(0, plan.C, LANES)]

    def shift(to, source, by, keep, at, col, _):
        xp[to, col, :, at] = pltpu.roll(xp[source, col, :, at], by, 0) * keep
        return 0

    for i, at in enumerate(lanes):
        patch_copy(x_hbm, xp, x_sem, i).wait()
        lax.fori_loop(0, cols, functools.partial(shift, 0, 3, 1, not_first, at), 0)
        lax.fori_loop(0, cols, functools.partial(shift, 4, 1, R - 1, not_last, at), 0)
        run_all(part_of(tasks, i, len(lanes)))


def patch_copy(x_hbm, xp, x_sem, i):
    at = pl.ds(i * LANES, LANES)
    return pltpu.make_async_copy(x_hbm.at[:, :, :, at], xp.at[pl.ds(1, 3), :, :, at], x_sem.at[i])


def points_kernel(plan, x_hbm, v_hbm, xp, vh, vl, x_sem, v_sem):
    def copies(u):
        return [
            pltpu.make_async_copy(part.at[u], v_hbm.at[which, u], v_sem.at[which, u])
            for which, part in enumerate((vh, vl))
        ]

    for i in range(plan.C // LANES):
        patch_copy(x_hbm, xp, x_sem, i).start()
    load_patches(plan, x_hbm, xp, x_sem, patch_tasks(plan, xp, vh, vl, 0))
    for u in range(5):
        if u > 0:
            run_all(patch_tasks(plan, xp, vh, vl, u))
        for copy in copies(u):
            copy.start()
    for u in range(5):
        for copy in copies(u):
            copy.wait()


def forward_kernel(plan, last, n_refs, tab, mask, bias, *refs):
    refs = list(refs)
    C, N, R, T = plan.C, plan.N, plan.R, plan.T
    cols = 3 * T
    chunks = C // N
    x_hbm = refs.pop(0)
    cot_hbm = refs.pop(0) if last else None
    pieces = [refs.pop(0) for _ in range(n_refs)]
    act_hbm, slope_hbm = refs.pop(0), refs.pop(0)
    if last:
        bias_sum = refs.pop(0)
        outs = [refs.pop(0) for _ in range(plan.n_outs)]
    vh, vl, kbuf, uh, ul, mbuf, ebuf, tail, k_sem, out_sem = refs[:10]
    if last:
        xp, x_sem, cbuf, total, bias_rows, wh, wl, dbuf, c_sem, g_sem, bias_sem = refs[10:]
    else:
        (v_sem,) = refs[10:]

    def cot_copy(n):
        return pltpu.make_async_copy(cot_hbm.at[:, :, :, pl.ds(n * N, N)], cbuf.at[n], c_sem.at[n])

    def v_copies(u):
        return [
            pltpu.make_async_copy(x_hbm.at[which, u], part.at[u], v_sem.at[which, u])
            for which, part in enumerate((vh, vl))
        ]

    def out_copies(n):
        to = pl.ds(n * N, N)
        return [
            pltpu.make_async_copy(ebuf.at[n, pl.ds(0, 3)], act_hbm.at[:, :, :, to], out_sem.at[n, 0]),
            pltpu.make_async_copy(ebuf.at[n, pl.ds(3, 2)], slope_hbm.at[pl.ds(0, 2), :, :, to], out_sem.at[n, 1]),
            pltpu.make_async_copy(tail.at[n], slope_hbm.at[2, :, :, to], out_sem.at[n, 2]),
        ]

    if last:
        patch_copy(x_hbm, xp, x_sem, 0).start()
    else:
        for copy in v_copies(0):
            copy.start()
    start_kernel_fetch(plan, tab, pieces, kbuf.at[0], k_sem.at[0], 0, C, 0, N)
    if last:
        for i in range(1, C // LANES):
            patch_copy(x_hbm, xp, x_sem, i).start()
    else:
        for u in range(1, 5):
            for copy in v_copies(u):
                copy.start()
    for n in range(1, chunks):
        start_kernel_fetch(plan, tab, pieces, kbuf.at[n], k_sem.at[n], 0, C, n * N, N)
    if last:
        for n in range(chunks):
            cot_copy(n).start()
        total[...] = jnp.zeros((16, C), F32)
        load_patches(plan, x_hbm, xp, x_sem, patch_tasks(plan, xp, vh, vl, 0))

    def column_task(s, j, rb):
        n, u = steps[s]
        rows = pl.ds(rb, 16)
        cells = points_to_taps(*[mbuf[s % 2, v, j, rows] for v in range(5)])
        for b in range(3):
            ebuf[n, u, 3 * j + b, rows] = cells[b]

    def column_tasks(s):
        return [functools.partial(column_task, s, j, rb) for j in range(T) for rb in range(0, R, 16)]

    def finish_task(n, col, lane, rb):
        at, rows = pl.ds(lane, LANES), pl.ds(rb, 16)
        wide = pl.ds(n * N + lane, LANES)
        offset = bias[0:1, wide]
        cells = points_to_taps(*[ebuf[n, u, col, rows, at] for u in range(5)])
        sums = None
        for a in range(3):
            value, slope = gelu_parts(cells[a] + offset)
            keep = mask[a, col, rows]
            slope = slope * keep
            if last:
                slope = slope * cbuf[n, a, col, rows, at]
                sums = slope if sums is None else sums + slope
            ebuf[n, a, col, rows, at] = value * keep
            if a < 2:
                ebuf[n, 3 + a, col, rows, at] = slope
            else:
                tail[n, col, rows, at] = slope
        if last:
            total[:, wide] += sums

    def finish_tasks(n):
        return [
            functools.partial(finish_task, n, col, lane, rb)
            for col in range(cols)
            for lane in range(0, N, LANES)
            for rb in range(0, R, 16)
        ]

    steps = [(n, u) for n in range(chunks) for u in range(5)]
    wait_for(kbuf.at[0], k_sem.at[0])
    run_all(tap_tasks(kbuf.at[0], uh.at[0], ul.at[0], 0))
    if last:
        grad = GradSteps(
            plan,
            tab,
            vh,
            vl,
            lambda n: [ebuf.at[n, 3], ebuf.at[n, 4], tail.at[n]],
            wh,
            wl,
            dbuf,
            kbuf,
            False,
            outs,
            g_sem,
        )
    for s, (n, u) in enumerate(steps):
        if u == 4 and n + 1 < chunks:
            wait_for(kbuf.at[n + 1], k_sem.at[n + 1])
            if n == 0 and last:
                for other in range(chunks):
                    cot_copy(other).wait()
        if n == 0 and not last:
            for ready in {0: (0, 1), 2: (2, 3), 4: (4,)}.get(u, ()):
                for copy in v_copies(ready):
                    copy.wait()
        tasks = []
        if s > 0:
            tasks += column_tasks(s - 1)
        if s + 1 < len(steps):
            next_n, next_u = steps[s + 1]
            if n == 0 and u < 4 and last:
                tasks += patch_tasks(plan, xp, vh, vl, u + 1)
            tasks += tap_tasks(kbuf.at[next_n], uh.at[(s + 1) % 2], ul.at[(s + 1) % 2], next_u)
        if n > 0 and u > 0:
            tasks += part_of(finish_tasks(n - 1), u - 1, 4)
        if s + 1 == len(steps) and last:
            if chunks == 1:
                tasks = []
            else:
                tasks += grad.cells(0)

        def put(v, value, s=s):
            mbuf[s % 2, v] = value.reshape(T, R, N)

        interleave(
            dot_tasks(lambda v: (vh[u, v], vl[u, v]), lambda v: (uh[s % 2, v], ul[s % 2, v]), NN, put),
            tasks,
        )
    end = chunks - 1
    if not last:
        for n in range(end):
            for copy in out_copies(n):
                copy.start()
        run_all(column_tasks(len(steps) - 1) + finish_tasks(end))
        for copy in out_copies(end):
            copy.start()
        for n in range(chunks):
            for copy in out_copies(n):
                copy.wait()
        return

    for n in range(end):
        for copy in out_copies(n):
            copy.start()
    closing = column_tasks(len(steps) - 1) + finish_tasks(end)
    if chunks == 1:
        run_all(closing)
        run_all(grad.cells(0))
    for s, (n, u) in enumerate(steps):
        if s + 1 == len(steps) - 3:
            for copy in out_copies(end):
                copy.start()
            for done in range(end):
                grad.store(done)
            bias_rows[...] = jnp.broadcast_to(jnp.sum(total[...], axis=0, keepdims=True), (8, C))
            bias_sum[...] = bias_rows[0:1]
            for copy in bias_copies(plan, bias_rows, outs, bias_sem):
                copy.start()
        tasks = []
        if chunks > 1 and s < 4:
            tasks += part_of(closing, s, 4)
        if s > 0:
            tasks += grad.adds(s - 1)
        if s + 1 < len(steps):
            tasks += grad.cells(s + 1)
        interleave(grad.dots(s), tasks)
    run_all(grad.adds(len(steps) - 1))
    grad.store(end)
    for n in range(chunks):
        for copy in out_copies(n):
            copy.wait()
    for copy in bias_copies(plan, bias_rows, outs, bias_sem):
        copy.wait()
    grad.wait()


def back_kernel(plan, last, n_refs, tab, mask, y_hbm, *refs):
    refs = list(refs)
    C, N, R, T = plan.C, plan.N, plan.R, plan.T
    cols = 3 * T
    chunks = C // N
    if not last:
        slope_hbm, v_hbm = refs.pop(0), refs.pop(0)
    pieces = [refs.pop(0) for _ in range(n_refs)]
    out_hbm = refs.pop(0)
    if not last:
        bias_sum = refs.pop(0)
        outs = [refs.pop(0) for _ in range(plan.n_outs)]
    yb, wh, wl, kbuf, uh, ul, mbuf, ebuf, y_sem, k_sem, out_sem = refs[:11]
    if not last:
        sbuf, total, bias_rows, gh, gl, dbuf, s_sem, v_sem, g_sem, bias_sem = refs[11:]
    lanes = [pl.ds(lane, LANES) for lane in range(0, C, LANES)]

    def y_copy(i):
        return pltpu.make_async_copy(y_hbm.at[:, :, :, lanes[i]], yb.at[:, :, :, lanes[i]], y_sem.at[i])

    def v_copies(u):
        return [
            pltpu.make_async_copy(v_hbm.at[which, u], part.at[u], v_sem.at[which, u])
            for which, part in enumerate((wh, wl))
        ]

    def slope_copy(n):
        return pltpu.make_async_copy(slope_hbm.at[:, :, :, pl.ds(n * N, N)], sbuf.at[n], s_sem.at[n])

    def out_copy(n):
        return pltpu.make_async_copy(ebuf.at[n, pl.ds(0, 3)], out_hbm.at[:, :, :, pl.ds(n * N, N)], out_sem.at[n])

    y_copy(0).start()
    start_kernel_fetch(plan, tab, pieces, kbuf.at[0], k_sem.at[0], 0, N, 0, C)
    for i in range(1, len(lanes)):
        y_copy(i).start()
    for n in range(1, chunks):
        start_kernel_fetch(plan, tab, pieces, kbuf.at[n], k_sem.at[n], n * N, N, 0, C)
    if not last:
        for n in range(chunks):
            slope_copy(n).start()
        total[...] = jnp.zeros((R, C), F32)
    not_first, not_last = edge_masks(plan)
    for parity in range(2):
        for v in (0, 4):
            mbuf[parity, v, 0] = jnp.zeros((R, N), F32)
            mbuf[parity, v, T + 1] = jnp.zeros((R, N), F32)

    def cells(u):
        return cell_tasks(plan, [yb.at[a] for a in range(3)], wh.at[u], wl.at[u], u)

    def column_task(s, j, rb):
        n, u = steps[s]
        rows = pl.ds(rb, 16)
        here = points_to_patch(*[mbuf[s % 2, v, j + 1, rows] for v in range(5)])
        ebuf[n, u, 3 * j, rows] = here[0] + mbuf[s % 2, 4, j, rows]
        ebuf[n, u, 3 * j + 1, rows] = here[1]
        ebuf[n, u, 3 * j + 2, rows] = here[2] + mbuf[s % 2, 0, j + 2, rows]

    def column_tasks(s):
        return [functools.partial(column_task, s, j, rb) for j in range(T) for rb in range(0, R, 16)]

    def finish_task(n, col, lane):
        at = pl.ds(lane, LANES)
        points = [ebuf[n, u, col, :, at] for u in range(5)]
        here = points_to_patch(*points)
        values = (
            here[0] + pltpu.roll(points[4], 1, 0) * not_first,
            here[1],
            here[2] + pltpu.roll(points[0], R - 1, 0) * not_last,
        )
        sums = None
        for a in range(3):
            back = values[a] * (mask[a, col] if last else sbuf[n, a, col, :, at])
            ebuf[n, a, col, :, at] = back
            sums = back if sums is None else sums + back
        if not last:
            total[:, pl.ds(n * N + lane, LANES)] += sums

    def finish_tasks(n):
        return [functools.partial(finish_task, n, col, lane) for col in range(cols) for lane in range(0, N, LANES)]

    first = cells(0)
    for i in range(len(lanes)):
        y_copy(i).wait()
        run_all(part_of(first, i, len(lanes)))
    steps = [(n, u) for n in range(chunks) for u in range(5)]
    wait_for(kbuf.at[0], k_sem.at[0])
    run_all(tap_tasks(kbuf.at[0], uh.at[0], ul.at[0], 0))
    if not last:
        grad = GradSteps(
            plan,
            tab,
            wh,
            wl,
            lambda n: [ebuf.at[n, a] for a in range(3)],
            gh,
            gl,
            dbuf,
            kbuf,
            True,
            outs,
            g_sem,
        )
    for s, (n, u) in enumerate(steps):
        if u == 4 and n + 1 < chunks:
            wait_for(kbuf.at[n + 1], k_sem.at[n + 1])
            if n == 0 and not last:
                for other in range(chunks):
                    slope_copy(other).wait()
        if s == len(steps) - 2 and not last:
            for early in range(3):
                for copy in v_copies(early):
                    copy.start()
        tasks = []
        if s > 0:
            tasks += column_tasks(s - 1)
        if s + 1 < len(steps):
            next_n, next_u = steps[s + 1]
            if n == 0 and u < 4:
                tasks += cells(u + 1)
            tasks += tap_tasks(kbuf.at[next_n], uh.at[(s + 1) % 2], ul.at[(s + 1) % 2], next_u)
        if n > 0 and u > 0:
            tasks += part_of(finish_tasks(n - 1), u - 1, 4)
        if s + 1 == len(steps) and not last and chunks > 1:
            tasks += grad.cells(0)

        def put(v, value, s=s):
            mbuf[s % 2, v, pl.ds(1, T)] = value.reshape(T, R, N)

        interleave(
            dot_tasks(lambda v: (wh[u, v], wl[u, v]), lambda v: (uh[s % 2, v], ul[s % 2, v]), NT, put),
            tasks,
        )
    end = chunks - 1
    for n in range(end):
        out_copy(n).start()
    closing = column_tasks(len(steps) - 1) + finish_tasks(end)
    if last:
        run_all(closing)
        out_copy(end).start()
        for n in range(chunks):
            out_copy(n).wait()
        return

    for late in range(3, 5):
        for copy in v_copies(late):
            copy.start()
    if chunks == 1:
        run_all(closing)
        run_all(grad.cells(0))
    for early in range(3):
        for copy in v_copies(early):
            copy.wait()
    for s, (n, u) in enumerate(steps):
        if s == 2:
            for late in range(3, 5):
                for copy in v_copies(late):
                    copy.wait()
        if s + 1 == len(steps) - 3:
            out_copy(end).start()
            for done in range(end):
                grad.store(done)
            bias_rows[...] = jnp.broadcast_to(jnp.sum(total[...], axis=0, keepdims=True), (8, C))
            bias_sum[...] = bias_rows[0:1]
            for copy in bias_copies(plan, bias_rows, outs, bias_sem):
                copy.start()
        tasks = []
        if chunks > 1 and s < 4:
            tasks += part_of(closing, s, 4)
        if s > 0:
            tasks += grad.adds(s - 1)
        if s + 1 < len(steps):
            tasks += grad.cells(s + 1)
        interleave(grad.dots(s), tasks)
    run_all(grad.adds(len(steps) - 1))
    grad.store(end)
    for n in range(chunks):
        out_copy(n).wait()
    for copy in bias_copies(plan, bias_rows, outs, bias_sem):
        copy.wait()
    grad.wait()


SMEM_SPEC = pl.BlockSpec(memory_space=pltpu.SMEM)
VMEM_SPEC = pl.BlockSpec(memory_space=pltpu.VMEM)
ANY_SPEC = pl.BlockSpec(memory_space=pl.ANY)


def plane_shape(plan):
    return jax.ShapeDtypeStruct((3, 3 * plan.T, plan.R, plan.C), F32)


def point_scratch(plan, width):
    shape = (5, 5, plan.T, plan.R, width)
    return [pltpu.VMEM(shape, BF16), pltpu.VMEM(shape, BF16)]


def call(kernel, outs, in_specs, out_specs, scratch, flops, args, name):
    moved = sum(a.size * a.dtype.itemsize for a in args) + sum(o.size * 4 for o in outs)
    return pl.pallas_call(
        kernel,
        out_shape=outs,
        in_specs=in_specs,
        out_specs=out_specs,
        scratch_shapes=scratch,
        compiler_params=pltpu.CompilerParams(vmem_limit_bytes=VMEM_LIMIT),
        cost_estimate=pl.CostEstimate(flops=flops, bytes_accessed=moved, transcendentals=0),
        name=name,
    )(*args)


def pass_flops(plan):
    return 2 * 3 * 25 * plan.T * plan.R * plan.C * plan.C


def point_shape(plan):
    return jax.ShapeDtypeStruct((2, 5, 5, plan.T, plan.R, plan.C), BF16)


def grad_shapes(plan):
    blocks = 9 * plan.C // plan.block_rows // plan.n_outs
    block = plan.block_rows + (8 if plan.n_outs == 2 else 0)
    return [jax.ShapeDtypeStruct((blocks, block, plan.C), F32) for _ in range(plan.n_outs)]


def grad_scratch(plan):
    shape = (2, 5, plan.T, plan.R, plan.N)
    return [
        pltpu.VMEM((8, plan.C), F32),
        pltpu.VMEM(shape, BF16),
        pltpu.VMEM(shape, BF16),
        pltpu.VMEM((2, 5, plan.C, plan.N), F32),
    ]


def run_points(plan, x, name):
    scratch = [
        pltpu.VMEM((5, 3 * plan.T, plan.R, plan.C), F32),
        *point_scratch(plan, plan.C),
        pltpu.SemaphoreType.DMA((plan.C // LANES,)),
        pltpu.SemaphoreType.DMA((2, 5)),
    ]
    kernel = functools.partial(points_kernel, plan)
    return call(kernel, [point_shape(plan)], [ANY_SPEC], [ANY_SPEC], scratch, x.size * 40, [x], name)[0]


def run_forward(plan, tab, mask, bias, x, cot, pieces, name):
    last = cot is not None
    C, N, R, T = plan.C, plan.N, plan.R, plan.T
    cols = 3 * T
    chunks = C // N
    outs = [plane_shape(plan), plane_shape(plan)]
    scratch = [
        *point_scratch(plan, C),
        pltpu.VMEM((chunks, 9, C, N), F32),
        pltpu.VMEM((2, 5, C, N), BF16),
        pltpu.VMEM((2, 5, C, N), BF16),
        pltpu.VMEM((2, 5, T, R, N), F32),
        pltpu.VMEM((chunks, 5, cols, R, N), F32),
        pltpu.VMEM((chunks, cols, R, N), F32),
        pltpu.SemaphoreType.DMA((chunks,)),
        pltpu.SemaphoreType.DMA((chunks, 3)),
    ]
    args = [tab, mask, bias, x]
    if last:
        outs += [jax.ShapeDtypeStruct((1, C), F32)] + grad_shapes(plan)
        out_specs = [ANY_SPEC, ANY_SPEC, VMEM_SPEC] + [ANY_SPEC] * plan.n_outs
        scratch += [
            pltpu.VMEM((5, cols, R, C), F32),
            pltpu.SemaphoreType.DMA((C // LANES,)),
            pltpu.VMEM((chunks, 3, cols, R, N), F32),
            pltpu.VMEM((16, C), F32),
            *grad_scratch(plan),
            pltpu.SemaphoreType.DMA((chunks,)),
            pltpu.SemaphoreType.DMA((chunks,)),
            pltpu.SemaphoreType.DMA,
        ]
        args.append(cot)
    else:
        out_specs = [ANY_SPEC] * 2
        scratch.append(pltpu.SemaphoreType.DMA((2, 5)))
    args += pieces
    in_specs = [SMEM_SPEC, VMEM_SPEC, VMEM_SPEC] + [ANY_SPEC] * (len(args) - 3)
    kernel = functools.partial(forward_kernel, plan, last, len(pieces))
    return call(kernel, outs, in_specs, out_specs, scratch, pass_flops(plan) * (1 + last), args, name)


def run_back(plan, tab, mask, y, slope, points, pieces, name):
    last = slope is None
    C, N, R, T = plan.C, plan.N, plan.R, plan.T
    cols = 3 * T
    chunks = C // N
    outs = [plane_shape(plan)]
    out_specs = [ANY_SPEC]
    scratch = [
        pltpu.VMEM((3, cols, R, C), F32),
        *point_scratch(plan, C),
        pltpu.VMEM((chunks, 9, N, C), F32),
        pltpu.VMEM((2, 5, N, C), BF16),
        pltpu.VMEM((2, 5, N, C), BF16),
        pltpu.VMEM((2, 5, T + 2, R, N), F32),
        pltpu.VMEM((chunks, 5, cols, R, N), F32),
        pltpu.SemaphoreType.DMA((C // LANES,)),
        pltpu.SemaphoreType.DMA((chunks,)),
        pltpu.SemaphoreType.DMA((chunks,)),
    ]
    args = [tab, mask, y]
    if not last:
        outs += [jax.ShapeDtypeStruct((1, C), F32)] + grad_shapes(plan)
        out_specs += [VMEM_SPEC] + [ANY_SPEC] * plan.n_outs
        scratch += [
            pltpu.VMEM((chunks, 3, cols, R, N), F32),
            pltpu.VMEM((R, C), F32),
            *grad_scratch(plan),
            pltpu.SemaphoreType.DMA((chunks,)),
            pltpu.SemaphoreType.DMA((2, 5)),
            pltpu.SemaphoreType.DMA((chunks,)),
            pltpu.SemaphoreType.DMA,
        ]
        args += [slope, points]
    args += pieces
    mask_spec = VMEM_SPEC if last else ANY_SPEC
    in_specs = [SMEM_SPEC, mask_spec] + [ANY_SPEC] * (len(args) - 2)
    kernel = functools.partial(back_kernel, plan, last, len(pieces))
    return call(kernel, outs, in_specs, out_specs, scratch, pass_flops(plan) * (2 - last), args, name)


def to_planes(plan, cells):
    slots, side, _, channels = cells.shape
    tiled = cells.reshape(slots, plan.T, 3, side, channels).transpose(2, 3, 0, 1, 4)
    flat = tiled.reshape(3, side, slots * plan.T, channels)
    return jnp.pad(flat, ((0, 0), (0, 0), (0, plan.R - slots * plan.T), (0, 0)))


def from_planes(plan, planes, slots):
    side = 3 * plan.T
    kept = planes[:, :, : slots * plan.T].reshape(3, side, slots, plan.T, planes.shape[3])
    return kept.transpose(2, 3, 0, 1, 4).reshape(slots, side, side, planes.shape[3])


def tie(*values):
    return lax.optimization_barrier(values)


class Net:
    def __init__(self):
        self.rep = lax.axis_size("rep")
        self.dp = lax.axis_size("dp")
        self.routed = self.rep == 4 and self.dp == 8
        self.n_pieces = 4 if self.routed else 1
        self.n_outs = 2 if self.routed else 1

    def perm(self, move):
        pairs = []
        for x in range(2):
            for c in range(2):
                for z in range(4):
                    for y in range(2):
                        to = move(x, c, z, y)
                        pairs.append((((x * 2 + c) * 4 + z) * 2 + y, ((to[0] * 2 + to[1]) * 4 + to[2]) * 2 + to[3]))
        return pairs

    def send(self, value, move):
        return lax.ppermute(value, AXES, self.perm(move))

    def over_core(self, value):
        return self.send(value, lambda x, c, z, y: (x, 1 - c, z, y))

    def over_first(self, value):
        return self.send(value, lambda x, c, z, y: (x, c, z, 1 - y) if c == 0 else (1 - x, c, z, y))

    def over_second(self, value):
        return self.send(value, lambda x, c, z, y: (1 - x, c, z, y) if c == 0 else (x, c, z, 1 - y))

    def over_both(self, value):
        return self.send(value, lambda x, c, z, y: (1 - x, c, z, 1 - y))

    def over_z(self, value, step):
        return self.send(value, lambda x, c, z, y: (x, c, (z + step) % 4, y))

    def tables(self):
        if not self.routed:
            return jnp.zeros((4, 8), jnp.int32)
        rep = lax.axis_index("rep")
        dp = lax.axis_index("dp")
        x, c, z, y = rep // 2, rep % 2, dp // 2, dp % 2
        block = jnp.arange(32, dtype=jnp.int32)
        bx, bc, bz, by = block // 16, block // 8 % 2, block // 2 % 4, block % 2
        dx, dy = bx ^ x, by ^ y
        second = jnp.where(bc == 0, dx, dy)
        first = jnp.where(bc == 0, dy, dx)
        other = (bc != c).astype(jnp.int32)
        return jnp.stack(
            [2 * other + second, 4 * first + (z - bz) % 4, other, 8 * second + 4 * first + (bz - z) % 4]
        ).astype(jnp.int32)

    def gather_z(self, shard):
        return jnp.stack([shard] + [self.over_z(shard, step) for step in (1, 2, 3)])

    def double(self, part):
        return jnp.concatenate([part, self.over_first(part)])

    def gather_whole(self, shard):
        return [lax.all_gather(shard, AXES, axis=0, tiled=True)[None]]

    def sum_whole(self, parts):
        return lax.psum_scatter(parts[0][0], AXES, scatter_dimension=0, tiled=True)

    def send_z(self, four):
        return [four[0]] + [self.over_z(four[step], step) for step in (1, 2, 3)]


def body(
    features, map_size, item_count, conv4_weight, conv4_bias, conv5_weight, conv5_bias, cotangent
):
    slots, side, _, channels = features.shape
    net = Net()
    tiles = side // 3
    rows = -(-slots * tiles // 16) * 16
    shard_rows = conv4_weight.shape[0] // channels
    block_rows = shard_rows if net.routed else 9 * channels
    plan = Plan(channels, rows, tiles, block_rows, net.n_pieces, net.n_outs)

    live = jnp.arange(slots, dtype=jnp.int32) < item_count[0]
    inside = jnp.arange(side, dtype=jnp.int32)[None, :] < map_size[:, None]
    valid = live[:, None, None] & inside[:, :, None] & inside[:, None, :]
    mask = to_planes(plan, jnp.broadcast_to(valid.astype(F32)[..., None], (slots, side, side, LANES)))
    source = to_planes(plan, features * valid.astype(F32)[..., None])
    cot = to_planes(plan, cotangent)
    tab = net.tables()

    shard4 = conv4_weight.reshape(shard_rows, channels)
    shard5 = conv5_weight.reshape(shard_rows, channels)
    if net.routed:
        four4 = net.gather_z(shard4)
        shard5, four4, source, mask, cot = tie(shard5, four4, source, mask, cot)
        four5 = net.gather_z(shard5)
        eight4 = net.double(four4)
        far4 = net.over_second(eight4)
        four5, far4, eight4 = tie(four5, far4, eight4)
        points4 = run_points(plan, source, "points4")
        pieces4 = [eight4, far4, net.over_core(eight4), net.over_core(far4)]
        eight5 = net.double(four5)
        eight5, points4 = tie(eight5, points4)
        far5 = net.over_second(eight5)
        near5 = net.over_core(eight5)
    else:
        pieces4 = net.gather_whole(shard4)
        pieces5 = net.gather_whole(shard5)
        points4 = run_points(plan, source, "points4")
    hidden, slope4 = run_forward(plan, tab, mask, conv4_bias[None], points4, None, pieces4, "conv4")
    if net.routed:
        far5, near5, hidden = tie(far5, near5, hidden)
        pieces5 = [eight5, far5, near5, net.over_core(far5)]
    out5, back5, bias5, *grad5 = run_forward(
        plan, tab, mask, conv5_bias[None], hidden, cot, pieces5, "conv5_grad5"
    )
    if net.routed:
        mine5, other5 = grad5
        core5 = net.over_core(other5)
        sends5 = [mine5[i : i + 4] + core5[i : i + 4] for i in (4, 8, 12)]
        *sends5, back5 = tie(*sends5, back5)
        got5 = [net.over_first(sends5[0]), net.over_second(sends5[1]), net.over_both(sends5[2])]
    back4, bias4, *grad4 = run_back(plan, tab, mask, back5, slope4, points4, pieces5, "back5_grad4")
    if net.routed:
        mine4, theirs4 = grad4
        core4, *got5 = tie(net.over_core(theirs4), *got5)
        four5 = mine5[:4] + core5[:4] + got5[0] + got5[1] + got5[2]
        send4, four5, back4 = tie(mine4[8:] + core4[8:], four5, back4)
        second4 = net.over_second(send4)
        got5 = net.send_z(four5)
    input_grad = run_back(plan, tab, mask, back4, None, None, pieces4, "back4")[0]
    if net.routed:
        second4, input_grad, *got5 = tie(second4, input_grad, *got5)
        first4 = net.over_first(mine4[4:8] + core4[4:8] + second4[4:])
        sum4 = sum(net.send_z(mine4[:4] + core4[:4] + second4[:4] + first4))
        sum5 = sum(got5)
        share4, total4 = sum4[:shard_rows], sum4[shard_rows]
        share5, total5 = sum5[:shard_rows], sum5[shard_rows]
    else:
        share5 = net.sum_whole(grad5)
        share4 = net.sum_whole(grad4)
        total4, total5 = lax.psum((bias4[0], bias5[0]), AXES)

    total_cells = slots * net.rep * net.dp * side * side
    scale = float(total_cells) ** (-0.5)
    return (
        from_planes(plan, out5, slots),
        from_planes(plan, input_grad, slots),
        (share4 * scale).reshape(-1),
        total4 * scale,
        (share5 * scale).reshape(-1),
        total5 * scale,
    )


def solution(mesh):
    placed = (
        P(AXES, None, None, None),
        P(AXES),
        P(AXES),
        P(AXES),
        P(),
        P(AXES),
        P(),
        P(AXES, None, None, None),
    )
    return jax.shard_map(
        body,
        mesh=mesh,
        in_specs=placed,
        out_specs=(
            P(AXES, None, None, None),
            P(AXES, None, None, None),
            P(AXES),
            P(),
            P(AXES),
            P(),
        ),
        check_vma=False,
    )
```

time: 380 us -> 392 us (1.032)
  waiting for transfers between devices: 114 us -> 147 us
  Pallas kernels: 166 us -> 142 us
    ppermute x26 -> x27, waiting for transfers between devices: 114 us -> 147 us  [send(): return lax.ppermute(value, AXES, self.perm(move))]
    pallas_call x6 -> x5, Pallas kernels: 166 us -> 142 us  [call(): pl.pallas_call(kernel, out_shape=outs, in_specs=in_specs, out_specs=out_s...]
    unnamed x17, local copies, waits for them, and re-layouts: 1.69 us -> 6.01 us
    add x7 -> x6, other arithmetic: 21.4 us -> 17.5 us  [the longest x1 6.16 us: body(): sends5 = [mine5[i:i + 4] + core5[i:i + 4] for i in (4, 8, 12)]]
    ppermute x26 -> x27, starting transfers between devices: 31.9 us -> 32.3 us  [send(): return lax.ppermute(value, AXES, self.perm(move))]
  transfers between devices with their start and end apart: 26 -> 27, of which waited for: 15 -> 17; matrix products, arithmetic and copies ran while one was open for 10% -> 9% of each run, Pallas kernels for 28% -> 15%
where the time goes in v3:
time: 392 us; the launch traced here: 384 us
  waiting for transfers between devices  147 us (38%)
  Pallas kernels  142 us (36%)
  local copies, waits for them, and re-layouts  33.8 us (9%)
  starting transfers between devices  32.3 us (8%)
  other arithmetic  26.9 us (7%)
    ppermute x27, waiting for transfers between devices, send(): return lax.ppermute(value, AXES, self.perm(move))  147 us
    pallas_call x5, Pallas kernels, call(): pl.pallas_call(kernel, out_shape=outs, in_specs=in_specs, out_specs=out_s...  142 us
    ppermute x27, starting transfers between devices, send(): return lax.ppermute(value, AXES, self.perm(move))  32.3 us
    transpose x2, local copies, waits for them, and re-layouts, from_planes(): kept.transpose(2, 3, 0, 1, 4).reshape(slots, side, side, planes.shape[3])  11.3 us
  transfers between devices with their start and end apart: 27, of which 17 were waited for; matrix products, arithmetic and copies ran while one was open for 9% of the time, Pallas kernels for 15%

profile of v3, /device:TPU:0, one launch (start us, length us, event | category | flops | bytes accessed | tf_op | source)
XLA Modules:
  0.0 384.0 jit_solution(12357958811377629350)
XLA Ops:
  1.7 5.1 %collective-permute-start.2 = (f32[144,512]{1,0:T(8,128)S(1)}, f32[144,512]{1,0:T(8,128)S(1)}, u32[]{:S(2)}, u32[]{:S(2)}) collective-permute-start(f32[144,512]{1,0:T(8,128)S(1)} %reshape.417), channel_id=1, source_target_pairs={{0,6},{1,7},{2,0},{3,1},{4,2},{5,3},{6,4},{7,5},{8,14},{9,15},{10,... | collective-permute-start | bytes 884744 | tf_op jit(solution)/shard_map/ppermute | solution.py:922
  24.3 3.0 pad.13.refs_1_
  27.3 4.6 %collective-permute-done.1 = f32[144,512]{1,0:T(8,128)S(1)} collective-permute-done((f32[144,512]{1,0:T(8,128)S(1)}, f32[144,512]{1,0:T(8,128)S(1)}, u32[]{:S(2)}, u32[]{:S(2)}) %collective-permute-start.1) | collective-permute-done | bytes 294944 | tf_op jit(solution)/shard_map/ppermute | solution.py:922
  34.8 13.5 %collective-permute-done.6 = f32[4,144,512]{2,1,0:T(8,128)S(1)} collective-permute-done((f32[4,144,512]{2,1,0:T(8,128)S(1)}, f32[4,144,512]{2,1,0:T(8,128)S(1)}, u32[]{:S(2)}, u32[]{:S(2)}) %collective-permute-start.6) | collective-permute-done | bytes 1179680 | tf_op jit(solution)/shard_map/ppermute | solution.py:922
  58.4 19.5 %collective-permute-done.4 = f32[144,512]{1,0:T(8,128)S(1)} collective-permute-done((f32[144,512]{1,0:T(8,128)S(1)}, f32[144,512]{1,0:T(8,128)S(1)}, u32[]{:S(2)}, u32[]{:S(2)}) %collective-permute-start.4) | collective-permute-done | bytes 294944 | tf_op jit(solution)/shard_map/ppermute | solution.py:922
  80.6 8.5 %points4.1.refs_0_.refs_1_ = bf16[2,5,5,5,48,512]{5,4,3,2,1,0:T(8,128)(2,1)} custom-call(f32[3,15,48,512]{3,2,1,0:T(8,128)} %pad.11.x_hbm), custom_call_target="tpu_custom_call" | custom-call | flops 44236800 | bytes 28999680 | tf_op jit(solution)/shard_map/points4/pallas_call | solution.py:758
  89.1 5.7 %collective-permute-done.8 = f32[4,144,512]{2,1,0:T(8,128)} collective-permute-done((f32[4,144,512]{2,1,0:T(8,128)S(1)}, f32[4,144,512]{2,1,0:T(8,128)}, u32[]{:S(2)}, u32[]{:S(2)}) %collective-permute-start.8) | collective-permute-done | bytes 1179680 | tf_op jit(solution)/shard_map/ppermute | solution.py:922
  94.9 2.9 pad_maximum_fusion.refs_2_
  99.9 22.9 %conv4.1 = (f32[3,15,48,512]{3,2,1,0:T(8,128)}, f32[3,15,48,512]{3,2,1,0:T(8,128)}) custom-call(s32[4,32]{1,0:T(4,128)} %pad_add_fusion.tab, f32[3,15,48,128]{3,2,1,0:T(8,128)} %pad.12.mask, f32[1,512]{1,0:T(1,128)} %bitcast.88, bf16[2,5,5,5,48,512]{5,4,3,2,1,0:T(8,128)(2,1)} %points4.1.refs_0_.refs_1_, ...), custom_call_target="tpu_custom_call" | custom-call | flops 9437184000 | bytes 31681024 | tf_op jit(solution)/shard_map/conv4/pallas_call | solution.py:758
  122.8 4.1 %collective-permute-done.9.refs_3_ = f32[8,144,512]{2,1,0:T(8,128)} collective-permute-done((f32[8,144,512]{2,1,0:T(8,128)}, f32[8,144,512]{2,1,0:T(8,128)}, u32[]{:S(2)}, u32[]{:S(2)}) %collective-permute-start.9) | collective-permute-done | bytes 2359328 | tf_op jit(solution)/shard_map/ppermute | solution.py:922
  126.9 4.9 %collective-permute-done.13.refs_5_ = f32[8,144,512]{2,1,0:T(8,128)} collective-permute-done((f32[8,144,512]{2,1,0:T(8,128)}, f32[8,144,512]{2,1,0:T(8,128)}, u32[]{:S(2)}, u32[]{:S(2)}) %collective-permute-start.13) | collective-permute-done | bytes 2359328 | tf_op jit(solution)/shard_map/ppermute | solution.py:922
  131.8 45.0 %conv5_grad5.1 = (f32[3,15,48,512]{3,2,1,0:T(8,128)}, f32[3,15,48,512]{3,2,1,0:T(8,128)}, f32[1,512]{1,0:T(1,128)}, f32[16,152,512]{2,1,0:T(8,128)}, f32[16,152,512]{2,1,0:T(8,128)}) custom-call(s32[4,32]{1,0:T(4,128)} %pad_add_fusion.tab, f32[3,15,48,128]{3,2,1,0:T(8,128)} %pad.12.mask, f32[1,512]{1,0:T(1,128)} %bitcast.89, ...), custom_call_target="tpu_custom_call" | custom-call | flops 18874368000 | bytes 38203904 | tf_op jit(solution)/shard_map/conv5_grad5/pallas_call | solution.py:758
  177.1 8.3 %collective-permute-done.14 = f32[16,152,512]{2,1,0:T(8,128)S(1)} collective-permute-done((f32[16,152,512]{2,1,0:T(8,128)}, f32[16,152,512]{2,1,0:T(8,128)S(1)}, u32[]{:S(2)}, u32[]{:S(2)}) %collective-permute-start.14) | collective-permute-done | bytes 4980768 | tf_op jit(solution)/shard_map/ppermute | solution.py:922
  185.4 6.2 %slice_add_fusion.2 = (f32[4,152,512]{2,1,0:T(8,128)S(1)}, f32[4,152,512]{2,1,0:T(8,128)}, f32[4,152,512]{2,1,0:T(8,128)}) fusion(f32[16,152,512]{2,1,0:T(8,128)S(1)} %collective-permute-done.14, f32[16,152,512]{2,1,0:T(8,128)} %get-tuple-element.60), kind=kLoop, calls=%fused_computation.7 | loop fusion | flops 933888 | bytes 11206656 | tf_op jit(solution)/shard_map/add | solution.py:1019
  191.6 41.5 %back5_grad4.1 = (f32[3,15,48,512]{3,2,1,0:T(8,128)}, f32[1,512]{1,0:T(1,128)}, f32[16,152,512]{2,1,0:T(8,128)}, f32[16,152,512]{2,1,0:T(8,128)}) custom-call(s32[4,32]{1,0:T(4,128)} %pad_add_fusion.tab, f32[3,15,48,128]{3,2,1,0:T(8,128)} %pad.12.mask, f32[3,15,48,512]{3,2,1,0:T(8,128)} %get-tuple-element.63.y_hbm, ...), custom_call_target="tpu_custom_call" | custom-call | flops 18874368000 | bytes 46066176 | tf_op jit(solution)/shard_map/back5_grad4/pallas_call | solution.py:758
  236.9 27.6 %collective-permute-done.16 = f32[4,152,512]{2,1,0:T(8,128)S(1)} collective-permute-done((f32[4,152,512]{2,1,0:T(8,128)}, f32[4,152,512]{2,1,0:T(8,128)S(1)}, u32[]{:S(2)}, u32[]{:S(2)}) %collective-permute-start.16) | collective-permute-done | bytes 1245216 | tf_op jit(solution)/shard_map/ppermute | solution.py:922
  265.4 25.5 %collective-permute-done.18 = f32[4,152,512]{2,1,0:T(8,128)S(1)} collective-permute-done((f32[4,152,512]{2,1,0:T(8,128)S(1)}, f32[4,152,512]{2,1,0:T(8,128)S(1)}, u32[]{:S(2)}, u32[]{:S(2)}) %collective-permute-start.18) | collective-permute-done | bytes 1245216 | tf_op jit(solution)/shard_map/ppermute | solution.py:922
  293.2 3.7 slice_add_fusion
  306.5 24.5 %back4.1 = f32[3,15,48,512]{3,2,1,0:T(8,128)} custom-call(s32[4,32]{1,0:T(4,128)} %pad_add_fusion.tab, f32[3,15,48,128]{3,2,1,0:T(8,128)} %pad.12.mask, f32[3,15,48,512]{3,2,1,0:T(8,128)} %get-tuple-element.76.y_hbm, f32[8,144,512]{2,1,0:T(8,128)} %constant_dynamic-update-slice_fusion.refs_1_.refs_0_, f32[8,144,512]{2,1,0:T(8,128)} %collective-permute-done.7.refs_2_.refs_1_, ...), custom_call_target="tpu_custom_call" | custom-call | flops 9437184000 | bytes 19390976 | tf_op jit(solution)/shard_map/back4/pallas_call | solution.py:758
  334.5 6.8 %copy.37 = f32[3,15,45,512]{3,1,0,2:T(8,128)} copy(f32[3,15,45,512]{3,2,1,0:T(8,128)} %bitcast.70) | data formatting | bytes 8294400 | tf_op jit(solution)/shard_map/transpose | solution.py:896
  341.3 9.6 %collective-permute-done.23 = f32[4,152,512]{2,1,0:T(8,128)S(1)} collective-permute-done((f32[4,152,512]{2,1,0:T(8,128)S(1)}, f32[4,152,512]{2,1,0:T(8,128)S(1)}, u32[]{:S(2)}, u32[]{:S(2)}) %collective-permute-start.23) | collective-permute-done | bytes 1245216 | tf_op jit(solution)/shard_map/ppermute | solution.py:922
  353.7 3.8 collective-permute-start.26
  357.6 4.5 %copy.38 = f32[3,15,45,512]{3,1,0,2:T(8,128)} copy(f32[3,15,45,512]{3,2,1,0:T(8,128)S(1)} %bitcast.74) | data formatting | bytes 8294400 | tf_op jit(solution)/shard_map/transpose | solution.py:896
  368.2 13.9 %collective-permute-done.25 = f32[152,512]{1,0:T(8,128)S(1)} collective-permute-done((f32[152,512]{1,0:T(8,128)S(1)}, f32[152,512]{1,0:T(8,128)S(1)}, u32[]{:S(2)}, u32[]{:S(2)}) %collective-permute-start.25) | collective-permute-done | bytes 311328 | tf_op jit(solution)/shard_map/ppermute | solution.py:922
  (94 shorter events, 66.4 us)
Async XLA Ops:
  1.7 25.6 %collective-permute-start.2 = (f32[144,512]{1,0:T(8,128)S(1)}, f32[144,512]{1,0:T(8,128)S(1)}, u32[]{:S(2)}, u32[]{:S(2)}) collective-permute-start(f32[144,512]{1,0:T(8,128)S(1)} %reshape.417), channel_id=1, source_target_pairs={{0,6},{1,7},{2,0},{3,1},{4,2},{5,3},{6,4},{7,5},{8,14},{9,15},{10,... | collective-permute-start | bytes 884744 | tf_op jit(solution)/shard_map/ppermute | solution.py:922
  6.8 25.1 %collective-permute-start.1 = (f32[144,512]{1,0:T(8,128)S(1)}, f32[144,512]{1,0:T(8,128)S(1)}, u32[]{:S(2)}, u32[]{:S(2)}) collective-permute-start(f32[144,512]{1,0:T(8,128)S(1)} %reshape.417), channel_id=1, source_target_pairs={{0,4},{1,5},{2,6},{3,7},{4,0},{5,1},{6,2},{7,3},{8,12},{9,13},{10,... | collective-permute-start | bytes 884744 | tf_op jit(solution)/shard_map/ppermute | solution.py:922
  6.8 25.1 %collective-permute-start = (f32[144,512]{1,0:T(8,128)S(1)}, f32[144,512]{1,0:T(8,128)S(1)}, u32[]{:S(2)}, u32[]{:S(2)}) collective-permute-start(f32[144,512]{1,0:T(8,128)S(1)} %reshape.417), channel_id=1, source_target_pairs={{0,2},{1,3},{2,4},{3,5},{4,6},{5,7},{6,0},{7,1},{8,10},{9,11},{10,... | collective-permute-start | bytes 884744 | tf_op jit(solution)/shard_map/ppermute | solution.py:922
  32.0 16.3 %collective-permute-start.6 = (f32[4,144,512]{2,1,0:T(8,128)S(1)}, f32[4,144,512]{2,1,0:T(8,128)S(1)}, u32[]{:S(2)}, u32[]{:S(2)}) collective-permute-start(f32[4,144,512]{2,1,0:T(8,128)S(1)} %pad_maximum_fusion.1), channel_id=1, source_target_pairs={{0,1},{1,0},{2,3},{3,2},{4,5},{5,4},{6,7},{7,6},{8,24},{9,25},{10,... | collective-permute-start | bytes 3538952 | tf_op jit(solution)/shard_map/ppermute | solution.py:922
  49.4 29.2 %collective-permute-start.7 = (f32[8,144,512]{2,1,0:T(8,128)}, f32[8,144,512]{2,1,0:T(8,128)}, u32[]{:S(2)}, u32[]{:S(2)}) collective-permute-start(f32[8,144,512]{2,1,0:T(8,128)} %constant_dynamic-update-slice_fusion.refs_1_.refs_0_), channel_id=1, source_target_pairs={{0,16},{1,17},{2,18},{3,19},{4,20},{5,21},{6,22},{7,23},{8,9},{9,8... | collective-permute-start | bytes 7077896 | tf_op jit(solution)/shard_map/ppermute | solution.py:922
  50.9 27.1 %collective-permute-start.4 = (f32[144,512]{1,0:T(8,128)S(1)}, f32[144,512]{1,0:T(8,128)S(1)}, u32[]{:S(2)}, u32[]{:S(2)}) collective-permute-start(f32[144,512]{1,0:T(8,128)S(1)} %reshape.416), channel_id=1, source_target_pairs={{0,4},{1,5},{2,6},{3,7},{4,0},{5,1},{6,2},{7,3},{8,12},{9,13},{10,... | collective-permute-start | bytes 884744 | tf_op jit(solution)/shard_map/ppermute | solution.py:922
  53.7 24.3 %collective-permute-start.3 = (f32[144,512]{1,0:T(8,128)S(1)}, f32[144,512]{1,0:T(8,128)S(1)}, u32[]{:S(2)}, u32[]{:S(2)}) collective-permute-start(f32[144,512]{1,0:T(8,128)S(1)} %reshape.416), channel_id=1, source_target_pairs={{0,2},{1,3},{2,4},{3,5},{4,6},{5,7},{6,0},{7,1},{8,10},{9,11},{10,... | collective-permute-start | bytes 884744 | tf_op jit(solution)/shard_map/ppermute | solution.py:922
  78.6 16.3 %collective-permute-start.8 = (f32[4,144,512]{2,1,0:T(8,128)S(1)}, f32[4,144,512]{2,1,0:T(8,128)}, u32[]{:S(2)}, u32[]{:S(2)}) collective-permute-start(f32[4,144,512]{2,1,0:T(8,128)S(1)} %pad_maximum_fusion.2), channel_id=1, source_target_pairs={{0,1},{1,0},{2,3},{3,2},{4,5},{5,4},{6,7},{7,6},{8,24},{9,25},{10,... | collective-permute-start | bytes 3538952 | tf_op jit(solution)/shard_map/ppermute | solution.py:922
  80.1 19.8 %collective-permute-start.11 = (f32[8,144,512]{2,1,0:T(8,128)}, f32[8,144,512]{2,1,0:T(8,128)}, u32[]{:S(2)}, u32[]{:S(2)}) collective-permute-start(f32[8,144,512]{2,1,0:T(8,128)} %constant_dynamic-update-slice_fusion.refs_1_.refs_0_), channel_id=1, source_target_pairs={{0,8},{1,9},{2,10},{3,11},{4,12},{5,13},{6,14},{7,15},{8,0},{9,1},... | collective-permute-start | bytes 7077896 | tf_op jit(solution)/shard_map/ppermute | solution.py:922
  80.1 19.8 %collective-permute-start.12 = (f32[8,144,512]{2,1,0:T(8,128)}, f32[8,144,512]{2,1,0:T(8,128)}, u32[]{:S(2)}, u32[]{:S(2)}) collective-permute-start(f32[8,144,512]{2,1,0:T(8,128)} %collective-permute-done.7.refs_2_.refs_1_), channel_id=1, source_target_pairs={{0,8},{1,9},{2,10},{3,11},{4,12},{5,13},{6,14},{7,15},{8,0},{9,1},... | collective-permute-start | bytes 7077896 | tf_op jit(solution)/shard_map/ppermute | solution.py:922
  97.8 25.0 %collective-permute-start.10 = (f32[8,144,512]{2,1,0:T(8,128)}, f32[8,144,512]{2,1,0:T(8,128)}, u32[]{:S(2)}, u32[]{:S(2)}) collective-permute-start(f32[8,144,512]{2,1,0:T(8,128)} %pad_maximum_fusion.refs_2_), channel_id=1, source_target_pairs={{0,8},{1,9},{2,10},{3,11},{4,12},{5,13},{6,14},{7,15},{8,0},{9,1},... | collective-permute-start | bytes 7077896 | tf_op jit(solution)/shard_map/ppermute | solution.py:922
  97.8 29.2 %collective-permute-start.9 = (f32[8,144,512]{2,1,0:T(8,128)}, f32[8,144,512]{2,1,0:T(8,128)}, u32[]{:S(2)}, u32[]{:S(2)}) collective-permute-start(f32[8,144,512]{2,1,0:T(8,128)} %pad_maximum_fusion.refs_2_), channel_id=1, source_target_pairs={{0,16},{1,17},{2,18},{3,19},{4,20},{5,21},{6,22},{7,23},{8,9},{9,8... | collective-permute-start | bytes 7077896 | tf_op jit(solution)/shard_map/ppermute | solution.py:922
  233.1 57.8 %collective-permute-start.15 = (f32[16,152,512]{2,1,0:T(8,128)}, f32[16,152,512]{2,1,0:T(8,128)S(1)}, u32[]{:S(2)}, u32[]{:S(2)}) collective-permute-start(f32[16,152,512]{2,1,0:T(8,128)} %get-tuple-element.66), channel_id=1, source_target_pairs={{0,8},{1,9},{2,10},{3,11},{4,12},{5,13},{6,14},{7,15},{8,0},{9,1},... | collective-permute-start | bytes 14942216 | tf_op jit(solution)/shard_map/ppermute | solution.py:922
  233.4 31.1 %collective-permute-start.16 = (f32[4,152,512]{2,1,0:T(8,128)}, f32[4,152,512]{2,1,0:T(8,128)S(1)}, u32[]{:S(2)}, u32[]{:S(2)}) collective-permute-start(f32[4,152,512]{2,1,0:T(8,128)} %get-tuple-element.67), channel_id=1, source_target_pairs={{0,1},{1,0},{2,3},{3,2},{4,5},{5,4},{6,7},{7,6},{8,24},{9,25},{10,... | collective-permute-start | bytes 3735560 | tf_op jit(solution)/shard_map/ppermute | solution.py:922
  234.9 30.5 %collective-permute-start.17 = (f32[4,152,512]{2,1,0:T(8,128)}, f32[4,152,512]{2,1,0:T(8,128)S(1)}, u32[]{:S(2)}, u32[]{:S(2)}) collective-permute-start(f32[4,152,512]{2,1,0:T(8,128)} %get-tuple-element.68), channel_id=1, source_target_pairs={{0,16},{1,17},{2,18},{3,19},{4,20},{5,21},{6,22},{7,23},{8,9},{9,8... | collective-permute-start | bytes 3735560 | tf_op jit(solution)/shard_map/ppermute | solution.py:922
  236.4 54.5 %collective-permute-start.18 = (f32[4,152,512]{2,1,0:T(8,128)S(1)}, f32[4,152,512]{2,1,0:T(8,128)S(1)}, u32[]{:S(2)}, u32[]{:S(2)}) collective-permute-start(f32[4,152,512]{2,1,0:T(8,128)S(1)} %get-tuple-element.69), channel_id=1, source_target_pairs={{0,17},{1,16},{2,19},{3,18},{4,21},{5,20},{6,23},{7,22},{8,25},{9,... | collective-permute-start | bytes 3735560 | tf_op jit(solution)/shard_map/ppermute | solution.py:922
  299.3 32.2 %collective-permute-start.19 = (f32[8,152,512]{2,1,0:T(8,128)}, f32[8,152,512]{2,1,0:T(8,128)}, u32[]{:S(2)}, u32[]{:S(2)}) collective-permute-start(f32[8,152,512]{2,1,0:T(8,128)} %slice_add_fusion), channel_id=1, source_target_pairs={{0,16},{1,17},{2,18},{3,19},{4,20},{5,21},{6,22},{7,23},{8,9},{9,8... | collective-permute-start | bytes 7471112 | tf_op jit(solution)/shard_map/ppermute | solution.py:922
  301.6 29.3 %collective-permute-start.22 = (f32[152,512]{1,0:T(8,128)}, f32[152,512]{1,0:T(8,128)S(1)}, u32[]{:S(2)}, u32[]{:S(2)}) collective-permute-start(f32[152,512]{1,0:T(8,128)} %get-tuple-element.90), channel_id=1, source_target_pairs={{0,6},{1,7},{2,0},{3,1},{4,2},{5,3},{6,4},{7,5},{8,14},{9,15},{10,... | collective-permute-start | bytes 933896 | tf_op jit(solution)/shard_map/ppermute | solution.py:922
  301.6 29.8 %collective-permute-start.21 = (f32[152,512]{1,0:T(8,128)S(1)}, f32[152,512]{1,0:T(8,128)S(1)}, u32[]{:S(2)}, u32[]{:S(2)}) collective-permute-start(f32[152,512]{1,0:T(8,128)S(1)} %get-tuple-element.91), channel_id=1, source_target_pairs={{0,4},{1,5},{2,6},{3,7},{4,0},{5,1},{6,2},{7,3},{8,12},{9,13},{10,... | collective-permute-start | bytes 933896 | tf_op jit(solution)/shard_map/ppermute | solution.py:922
  304.5 27.0 %collective-permute-start.20 = (f32[152,512]{1,0:T(8,128)S(1)}, f32[152,512]{1,0:T(8,128)S(1)}, u32[]{:S(2)}, u32[]{:S(2)}) collective-permute-start(f32[152,512]{1,0:T(8,128)S(1)} %get-tuple-element.92), channel_id=1, source_target_pairs={{0,2},{1,3},{2,4},{3,5},{4,6},{5,7},{6,0},{7,1},{8,10},{9,11},{10,... | collective-permute-start | bytes 933896 | tf_op jit(solution)/shard_map/ppermute | solution.py:922
  333.9 17.0 %collective-permute-start.23 = (f32[4,152,512]{2,1,0:T(8,128)S(1)}, f32[4,152,512]{2,1,0:T(8,128)S(1)}, u32[]{:S(2)}, u32[]{:S(2)}) collective-permute-start(f32[4,152,512]{2,1,0:T(8,128)S(1)} %slice_add_fusion.5), channel_id=1, source_target_pairs={{0,1},{1,0},{2,3},{3,2},{4,5},{5,4},{6,7},{7,6},{8,24},{9,25},{10,... | collective-permute-start | bytes 3735560 | tf_op jit(solution)/shard_map/ppermute | solution.py:922
  353.6 12.1 %collective-permute-start.24 = (f32[152,512]{1,0:T(8,128)S(1)}, f32[152,512]{1,0:T(8,128)S(1)}, u32[]{:S(2)}, u32[]{:S(2)}) collective-permute-start(f32[152,512]{1,0:T(8,128)S(1)} %get-tuple-element.87), channel_id=1, source_target_pairs={{0,2},{1,3},{2,4},{3,5},{4,6},{5,7},{6,0},{7,1},{8,10},{9,11},{10,... | collective-permute-start | bytes 933896 | tf_op jit(solution)/shard_map/ppermute | solution.py:922
  353.7 14.5 %collective-permute-start.26 = (f32[152,512]{1,0:T(8,128)S(1)}, f32[152,512]{1,0:T(8,128)S(1)}, u32[]{:S(2)}, u32[]{:S(2)}) collective-permute-start(f32[152,512]{1,0:T(8,128)S(1)} %get-tuple-element.88), channel_id=1, source_target_pairs={{0,6},{1,7},{2,0},{3,1},{4,2},{5,3},{6,4},{7,5},{8,14},{9,15},{10,... | collective-permute-start | bytes 933896 | tf_op jit(solution)/shard_map/ppermute | solution.py:922
  357.5 24.6 %collective-permute-start.25 = (f32[152,512]{1,0:T(8,128)S(1)}, f32[152,512]{1,0:T(8,128)S(1)}, u32[]{:S(2)}, u32[]{:S(2)}) collective-permute-start(f32[152,512]{1,0:T(8,128)S(1)} %get-tuple-element.89), channel_id=1, source_target_pairs={{0,4},{1,5},{2,6},{3,7},{4,0},{5,1},{6,2},{7,3},{8,12},{9,13},{10,... | collective-permute-start | bytes 933896 | tf_op jit(solution)/shard_map/ppermute | solution.py:922
  (10 other events, 80.1 us)
